TPU v7x, 256 devices: a whole 4x4x8 slice. The times are simulated.
256 devices in a mesh: vox: 32 (over x, y, core), row: 8 (over z).
Axes of the slice: x: 4, y: 4, z: 8, core: 2. Of those that a mesh axis runs over, the one named last changes fastest.
Arguments:
- tile_values: float32 [32768, 128, 128], P(('vox', 'row')), may hold values from -0.375 to 0.375
- tile_vox: int32 [32768], P(('vox', 'row')), may hold values from 0 to 255
- tile_slot: int32 [32768], P(('vox', 'row')), may hold values from 0 to 127, as said below
- slot_block: int32 [256, 128], P(('vox', 'row')), may hold values from 0 to 64, as said below
- ray_data: float32 [16384, 128], P(('vox', 'row')), may hold values from -23 to 23
Outputs:
- solution: float32 [8192, 128], P('vox')
- ray_residual: float32 [16384, 128], P(('vox', 'row'))
- normal_residual: float32 [8192, 128], P('vox')
Inputs may be any that keep to these rules, and one draw needn't show every extreme that they name: `slot_block`: row g lists device g's send slots, 4 for each index d of vox in order. For each d the live slots come first and hold the index, 0 to 63, of one of the 64 ray blocks owned by the device at vox index d in g's row group; the other slots hold 64. Each device has at least one live slot for each d, and in every draw one index of vox receives 4 live slots from every device of its row group. `tile_slot`: every tile names a live slot of its own device, and every live slot of a device is named by at least one of its tiles.
All inputs are finite; a program needn't handle non-finite values.
Results may differ from a plain program's by a relative error of at most 0.0003.
Values sent between devices are 32-bit elements; how exact they have to be, the bound alone decides.
No kernel may reach another device: no remote copies, remote signals or barrier semaphores. Data moves between devices by JAX's collectives and lax.ppermute only.
A program may use at most 64 MiB of HBM per device.

v0:
```python
import jax
import jax.numpy as jnp
from jax import lax
from jax.sharding import PartitionSpec as P

TILE = 128
VT_DEV = 256
CAP = 4
ITERS = 2


def local(tile_values, tile_vox, tile_slot, slot_block, ray_data):
    vox_count = lax.axis_size("vox")
    owned = ray_data.shape[0]
    send_map = slot_block[0]
    dense_index = tile_slot // CAP * owned + jnp.take(send_map, tile_slot, axis=0)

    def backward(values):
        whole = lax.all_gather(values, "vox", axis=0, tiled=True)
        picked = jnp.take(whole, dense_index, axis=0)
        partial_voxels = jnp.einsum(
            "tab,ta->tb", tile_values, picked, precision=lax.Precision.HIGHEST
        )
        local_sum = jax.ops.segment_sum(partial_voxels, tile_vox, num_segments=VT_DEV)
        return lax.psum(local_sum, "row")

    def voxel_norm(field):
        return lax.psum(jnp.sum(field * field), "vox")

    solution = jnp.zeros((VT_DEV, TILE), jnp.float32)
    ray_residual = ray_data
    normal_residual = backward(ray_residual)
    direction = normal_residual
    norm_now = voxel_norm(normal_residual)
    for count in range(ITERS):
        gathered = jnp.take(direction, tile_vox, axis=0)
        partial_rays = jnp.einsum(
            "tab,tb->ta", tile_values, gathered, precision=lax.Precision.HIGHEST
        )
        term = jax.ops.segment_sum(partial_rays, dense_index, num_segments=vox_count * owned)
        result = lax.psum_scatter(term, "vox", scatter_dimension=0, tiled=True)
        step_size = norm_now / lax.psum(jnp.sum(result * result), ("vox", "row"))
        solution = solution + step_size * direction
        ray_residual = ray_residual - step_size * result
        normal_residual = backward(ray_residual)
        if count + 1 < ITERS:
            norm_next = voxel_norm(normal_residual)
            direction = normal_residual + norm_next / norm_now * direction
            norm_now = norm_next
    return (solution, ray_residual, normal_residual)


def solution(mesh):
    return jax.shard_map(
        local,
        mesh=mesh,
        in_specs=(
            P(("vox", "row"), None, None),
            P(("vox", "row")),
            P(("vox", "row")),
            P(("vox", "row"), None),
            P(("vox", "row"), None),
        ),
        out_specs=(P("vox", None), P(("vox", "row"), None), P("vox", None)),
        check_vma=False,
    )
```

profile of v0, /device:TPU:32, one launch (start us, length us, event | category | flops | bytes accessed | tf_op | source)
XLA Modules:
  0.0 900.4 jit_solution(1961269323500596541)
XLA Ops:
  7.2 0.7 all-gather.4.cloned.1.call-update
  8.0 0.7 compare_select_fusion.2
  8.6 1.2 gather_fusion
  9.9 0.7 compare_and_fusion.1
  10.6 0.7 compare_and_fusion
  11.2 49.8 %all-gather.4.cloned.1.call-done = f32[2048,128]{1,0:T(8,128)} async-done(((f32[64,128]{1,0:T(8,128)}), f32[2048,128]{1,0:T(8,128)}) %all-gather.4.cloned.1.call-update) | async-done | bytes 1048592 | tf_op jit(solution)/shard_map/all_gather | solution.py:19
  61.0 1.9 gather_fusion.1
  62.9 0.1 broadcast_select_fusion.4
  63.0 9.4 %fusion.12 = f32[128,1,128]{2,1,0:T(1,128)S(1)} fusion(f32[128,128,1]{1,2,0:T(1,128)S(1)} %bitcast.39, f32[128,128,128]{2,1,0:T(8,128)} %param.9), kind=kOutput, calls=%fused_computation.48 | convolution fusion | flops 25165824 | bytes 8519680 | tf_op jit(solution)/shard_map/tab,ta->tb/dot_general | solution.py:21
  72.4 1.6 scatter_custom_fusion
  74.1 71.2 %all-reduce.4.cloned.1.call-done = f32[256,128]{1,0:T(8,128)} async-done(((f32[256,128]{1,0:T(8,128)}), f32[256,128]{1,0:T(8,128)}) %all-reduce.4.cloned.1.call-update) | async-done | bytes 131088 | tf_op jit(solution)/shard_map/psum | solution.py:25
  145.3 1.6 gather_fusion.2
  146.9 0.1 broadcast_select_fusion.3
  147.0 15.4 %fusion.13 = f32[128,1,128]{2,1,0:T(1,128)S(1)} fusion(f32[128,128,1]{1,2,0:T(1,128)S(1)} %bitcast.40, f32[128,128,128]{2,1,0:T(8,128)} %param.9), kind=kOutput, calls=%fused_computation.49 | convolution fusion | flops 25165824 | bytes 8519680 | tf_op jit(solution)/shard_map/tab,tb->ta/dot_general | solution.py:37
  162.4 2.0 scatter_custom_fusion.1
  164.5 0.6 multiply_reduce_fusion.1
  165.2 83.2 %reduce-scatter.3.cloned.1.call-done = f32[64,128]{1,0:T(8,128)} async-done(((f32[2048,128]{1,0:T(8,128)}), f32[64,128]{1,0:T(8,128)}) %reduce-scatter.3.cloned.1.call-update) | async-done | bytes 32784 | tf_op jit(solution)/shard_map/reduce_scatter | solution.py:41
  248.4 1.4 multiply_reduce_fusion.3
  249.7 63.7 %psum.50 = f32[]{:T(128)} all-reduce(f32[]{:T(128)} %multiply_reduce_fusion.1), channel_id=1, replica_groups=mesh['vox'=32,'row'=8] {'vox'}, use_global_device_ids=true, to_apply=%region_3.5 | all-reduce | flops 1 | bytes 8 | tf_op jit(solution)/shard_map/psum | solution.py:28
  313.5 73.9 %psum.51 = f32[]{:T(128)} all-reduce(f32[]{:T(128)} %multiply_reduce_fusion.3), channel_id=1, replica_groups=mesh['vox'=32,'row'=8] {'vox','row'}, use_global_device_ids=true, to_apply=%region_7.10 | all-reduce | flops 1 | bytes 8 | tf_op jit(solution)/shard_map/psum | solution.py:42
  388.7 1.4 multiply_subtract_fusion.1
  390.1 0.2 all-reduce.6.cloned.1.call-start
  390.3 44.6 %all-gather.6.cloned.1.call-done = f32[2048,128]{1,0:T(8,128)} async-done(((f32[64,128]{1,0:T(8,128)}), f32[2048,128]{1,0:T(8,128)}) %all-gather.6.cloned.1.call-update) | async-done | bytes 1048592 | tf_op jit(solution)/shard_map/all_gather | solution.py:19
  434.9 1.9 gather_fusion.3
  436.8 0.1 broadcast_select_fusion.2
  436.9 9.4 %fusion.14 = f32[128,1,128]{2,1,0:T(1,128)S(1)} fusion(f32[128,128,1]{1,2,0:T(1,128)S(1)} %bitcast.41, f32[128,128,128]{2,1,0:T(8,128)} %param.9), kind=kOutput, calls=%fused_computation.50 | convolution fusion | flops 25165824 | bytes 8519680 | tf_op jit(solution)/shard_map/tab,ta->tb/dot_general | solution.py:21
  446.3 1.6 scatter_custom_fusion.2
  448.0 71.2 %all-reduce.6.cloned.1.call-done = f32[256,128]{1,0:T(8,128)} async-done(((f32[256,128]{1,0:T(8,128)}), f32[256,128]{1,0:T(8,128)}) %all-reduce.6.cloned.1.call-update) | async-done | bytes 131088 | tf_op jit(solution)/shard_map/psum | solution.py:25
  519.2 1.5 multiply_reduce_fusion
  520.7 63.3 %psum.53 = f32[]{:T(128)} all-reduce(f32[]{:T(128)} %multiply_reduce_fusion), channel_id=1, replica_groups=mesh['vox'=32,'row'=8] {'vox'}, use_global_device_ids=true, to_apply=%region_11.14 | all-reduce | flops 1 | bytes 8 | tf_op jit(solution)/shard_map/psum | solution.py:28
  585.4 0.9 multiply_add_fusion.1
  586.3 0.6 gather_fusion.4
  586.9 0.1 broadcast_select_fusion.1
  587.0 15.4 %fusion.15 = f32[128,1,128]{2,1,0:T(1,128)S(1)} fusion(f32[128,128,1]{1,2,0:T(1,128)S(1)} %bitcast.37, f32[128,128,128]{2,1,0:T(8,128)} %param.9), kind=kOutput, calls=%fused_computation.51 | convolution fusion | flops 25165824 | bytes 8519680 | tf_op jit(solution)/shard_map/tab,tb->ta/dot_general | solution.py:37
  602.4 2.0 scatter_custom_fusion.3
  604.5 78.9 %reduce-scatter.5.cloned.1.call-done = f32[64,128]{1,0:T(8,128)} async-done(((f32[2048,128]{1,0:T(8,128)}), f32[64,128]{1,0:T(8,128)}) %reduce-scatter.5.cloned.1.call-update) | async-done | bytes 32784 | tf_op jit(solution)/shard_map/reduce_scatter | solution.py:41
  683.5 1.4 multiply_reduce_fusion.2
  684.8 75.8 %psum.54 = f32[]{:T(128)} all-reduce(f32[]{:T(128)} %multiply_reduce_fusion.2), channel_id=1, replica_groups=mesh['vox'=32,'row'=8] {'vox','row'}, use_global_device_ids=true, to_apply=%region_15.18 | all-reduce | flops 1 | bytes 8 | tf_op jit(solution)/shard_map/psum | solution.py:42
  761.9 1.4 multiply_subtract_fusion
  763.4 0.3 all-reduce.8.cloned.1.call-start
  763.6 44.1 %all-gather.8.cloned.1.call-done = f32[2048,128]{1,0:T(8,128)} async-done(((f32[64,128]{1,0:T(8,128)}), f32[2048,128]{1,0:T(8,128)}) %all-gather.8.cloned.1.call-update) | async-done | bytes 1048592 | tf_op jit(solution)/shard_map/all_gather | solution.py:19
  807.8 1.9 gather_fusion.5
  809.6 0.1 broadcast_select_fusion
  809.7 9.4 %fusion.16 = f32[128,1,128]{2,1,0:T(1,128)S(1)} fusion(f32[128,128,1]{1,2,0:T(1,128)S(1)} %bitcast.38, f32[128,128,128]{2,1,0:T(8,128)} %param.9), kind=kOutput, calls=%fused_computation.52 | convolution fusion | flops 25165824 | bytes 8519680 | tf_op jit(solution)/shard_map/tab,ta->tb/dot_general | solution.py:21
  819.1 1.6 scatter_custom_fusion.4
  820.8 0.7 multiply_add_fusion
  821.4 70.6 %all-reduce.8.cloned.1.call-done = f32[256,128]{1,0:T(8,128)} async-done(((f32[256,128]{1,0:T(8,128)}), f32[256,128]{1,0:T(8,128)}) %all-reduce.8.cloned.1.call-update) | async-done | bytes 131088 | tf_op jit(solution)/shard_map/psum | solution.py:25
  892.0 1.6 copy.21
  (28 shorter events, 0.4 us)
Async XLA Ops:
  7.2 1.5 copy-start
  7.2 65.2 %copy-start.4 = (s32[128]{0:T(128)S(1)}, s32[128]{0:T(128)}, u32[]{:S(2)}) copy-start(s32[128]{0:T(128)} %param.10) | copy-start | bytes 1540
  7.2 53.8 %all-gather.4.cloned.1.call-start = ((), (), s32[]{:S(2)}) async-start(), calls=%async_computation.2 | async-start | bytes 1081344 | tf_op jit(solution)/shard_map/all_gather | solution.py:19
  7.9 137.4 %all-reduce.4.cloned.1.call-start = ((), (), s32[]{:S(2)}) async-start(), calls=%async_computation.3 | async-start | bytes 262144 | tf_op jit(solution)/shard_map/psum | solution.py:25
  63.0 325.7 %copy-start.3 = (f32[64,128]{1,0:T(8,128)S(1)}, f32[64,128]{1,0:T(8,128)}, u32[]{:S(2)}) copy-start(f32[64,128]{1,0:T(8,128)} %param.13) | copy-start | bytes 98308
  74.0 174.3 %reduce-scatter.3.cloned.1.call-start = ((), (), s32[]{:S(2)}) async-start(), calls=%async_computation.4 | async-start | bytes 1081344 | tf_op jit(solution)/shard_map/reduce_scatter | solution.py:41
  145.3 19.2 %copy-start.1 = (f32[256,128]{1,0:T(8,128)S(1)}, f32[256,128]{1,0:T(8,128)}, u32[]{:S(2)}) copy-start(f32[256,128]{1,0:T(8,128)} %all-reduce.4.cloned.1.call-done) | copy-start | bytes 393220
  164.5 270.5 %all-gather.6.cloned.1.call-start = ((), (), s32[]{:S(2)}) async-start(), calls=%async_computation.5 | async-start | bytes 1081344 | tf_op jit(solution)/shard_map/all_gather | solution.py:19
  390.1 129.1 %all-reduce.6.cloned.1.call-start = ((), (), s32[]{:S(2)}) async-start(), calls=%async_computation.6 | async-start | bytes 262144 | tf_op jit(solution)/shard_map/psum | solution.py:25
  436.9 325.1 %copy-start.2 = (f32[64,128]{1,0:T(8,128)S(1)}, f32[64,128]{1,0:T(8,128)}, u32[]{:S(2)}) copy-start(f32[64,128]{1,0:T(8,128)} %multiply_subtract_fusion.1) | copy-start | bytes 98308
  447.9 235.5 %reduce-scatter.5.cloned.1.call-start = ((), (), s32[]{:S(2)}) async-start(), calls=%async_computation.7 | async-start | bytes 1081344 | tf_op jit(solution)/shard_map/reduce_scatter | solution.py:41
  604.5 203.3 %all-gather.8.cloned.1.call-start = ((), (), s32[]{:S(2)}) async-start(), calls=%async_computation.8 | async-start | bytes 1081344 | tf_op jit(solution)/shard_map/all_gather | solution.py:19
  763.4 128.7 %all-reduce.8.cloned.1.call-start = ((), (), s32[]{:S(2)}) async-start(), calls=%async_computation.9 | async-start | bytes 262144 | tf_op jit(solution)/shard_map/psum | solution.py:25
Sparse Core Ops, SparseCore 0:
  10.6 50.3 all-gather.3
  74.2 71.1 all-reduce.3
  164.6 83.7 reduce-scatter.2
  390.2 44.6 all-gather.5
  448.0 71.1 all-reduce.5
  604.6 78.8 reduce-scatter.4
  763.5 44.2 all-gather.7
  820.9 71.1 all-reduce.7
where the time goes:
time: 902 us; the launch traced here: 900 us
  waiting for transfers between devices  514 us (57%)
  blocking collectives  277 us (31%)
  matrix products  58.9 us (7%)
  other arithmetic  20.7 us (2%)
  between operations  18.3 us (2%)
  local copies, waits for them, and re-layouts  10.7 us (1%)
    psum x3, waiting for transfers between devices, backward(): return lax.psum(local_sum, 'row')  213 us
    reduce_scatter x2, waiting for transfers between devices, local(): result = lax.psum_scatter(term, 'vox', scatter_dimension=0, tiled=True)  162 us
    psum x2, blocking collectives, local(): step_size = norm_now / lax.psum(jnp.sum(result * result), ('vox', 'row'))  150 us
    all_gather x3, waiting for transfers between devices, backward(): whole = lax.all_gather(values, 'vox', axis=0, tiled=True)  138 us
    psum x2, blocking collectives, voxel_norm(): return lax.psum(jnp.sum(field * field), 'vox')  127 us
    dot_general x2, matrix products, local(): jnp.einsum('tab,tb->ta', tile_values, gathered, precision=lax.Precision.H...  30.8 us
    dot_general x3, matrix products, backward(): jnp.einsum('tab,ta->tb', tile_values, picked, precision=lax.Precision.HIG...  28.2 us
  transfers between devices with their start and end apart: 8, of which 8 were waited for; matrix products, arithmetic and copies ran while one was open for 1% of the time, Pallas kernels for 0%

commit v1 on v0

v1 whole, which is shorter than its diff:
```python
import jax
import jax.numpy as jnp
from jax import lax
from jax.experimental import pallas as pl
from jax.experimental.pallas import tpu as pltpu
from jax.sharding import PartitionSpec as P

TILE = 128
VT_DEV = 256
CAP = 4
N_VOX = 32
N_ROW = 8
PAD = 8
HEAD = CAP
EXCH = TILE + 8

F32 = jnp.float32
BF16 = jnp.bfloat16


def iota(shape, dim):
    return lax.broadcasted_iota(jnp.int32, shape, dim)


def select_rows(choice, values, transposed=False):
    high = values.astype(BF16)
    rest = values - high.astype(F32)
    middle = rest.astype(BF16)
    low = (rest - middle.astype(F32)).astype(BF16)
    total = None
    for term in (low, middle, high):
        if transposed:
            part = lax.dot_general(term, choice, (((1,), (0,)), ((), ())), preferred_element_type=F32)
        else:
            part = lax.dot_general(choice, term, (((1,), (0,)), ((), ())), preferred_element_type=F32)
        total = part if total is None else total + part
    return total


def back_tiles(tiles_ref, weight_ref):
    def step(index, total):
        for inner in range(8):
            ray = index * 8 + inner
            total = total + tiles_ref[ray] * weight_ref[pl.ds(ray, 1), :]
        return total

    return lax.fori_loop(0, TILE // 8, step, jnp.zeros((TILE, TILE), F32))


def write_exchange(exchange_ref, partial, tile_vox_row, scalar):
    rows = jnp.transpose(partial)
    sub, lane = iota((8, TILE), 0), iota((8, TILE), 1)
    tail = jnp.where(sub == 0, jnp.broadcast_to(tile_vox_row.astype(F32), (8, TILE)), 0.0)
    tail = tail + jnp.where((sub == 1) & (lane == 0), scalar, 0.0)
    for target in range(N_ROW):
        exchange_ref[target, 0:TILE, :] = rows
        exchange_ref[target, TILE:EXCH, :] = tail


def back_first_kernel(dense_ref, whole_ref, tiles_ref, tile_vox_ref, exchange_ref, picked_ref, weight_ref):
    for tile in range(TILE):
        picked_ref[tile : tile + 1, :] = whole_ref[pl.ds(dense_ref[tile], 1), :]
    weight_ref[...] = jnp.transpose(picked_ref[...])
    partial = back_tiles(tiles_ref, weight_ref)
    write_exchange(exchange_ref, partial, tile_vox_ref[...], 0.0)


def back_kernel(received_ref, tiles_ref, slot_ref, tile_vox_ref, exchange_ref, weight_ref):
    received = received_ref[...]
    rows = N_VOX * PAD
    sub, lane = iota((rows, TILE), 0), iota((rows, TILE), 1)
    choice = jnp.where(sub == slot_ref[...], 1.0, 0.0).astype(BF16)
    weight_ref[...] = select_rows(choice, jnp.transpose(received), transposed=True)
    square = jnp.sum(jnp.where((sub % PAD == HEAD) & (lane == 0), received, 0.0))
    partial = back_tiles(tiles_ref, weight_ref)
    write_exchange(exchange_ref, partial, tile_vox_ref[...], square)


def gather_field(received_ref):
    field = jnp.zeros((VT_DEV, TILE), F32)
    scalar = 0.0
    sub, lane = iota((8, TILE), 0), iota((8, TILE), 1)
    for source in range(N_ROW):
        where = received_ref[source, TILE : TILE + 1, :].astype(jnp.int32)
        choice = jnp.where(iota((VT_DEV, TILE), 0) == where, 1.0, 0.0).astype(BF16)
        field = field + select_rows(choice, received_ref[source, 0:TILE, :])
        tail = received_ref[source, TILE:EXCH, :]
        scalar = scalar + jnp.sum(jnp.where((sub == 1) & (lane == 0), tail, 0.0))
    return field, scalar


def forward_tiles(field, tiles_ref, slot_ref, tile_vox_ref, extra_ref, payload_ref, sums_ref):
    choice = jnp.where(iota((VT_DEV, TILE), 0) == tile_vox_ref[...], 1.0, 0.0).astype(BF16)
    values = select_rows(choice, jnp.transpose(field), transposed=True)

    def step(index, unused):
        for inner in range(8):
            ray = index * 8 + inner
            product = tiles_ref[ray] * values
            sums_ref[pl.ds(pl.multiple_of(ray * 8, 8), 8), :] = jnp.sum(product.reshape(TILE // 8, 8, TILE), axis=0)
        return unused

    lax.fori_loop(0, TILE // 8, step, 0)
    rays = sums_ref[pl.ds(0, TILE, stride=8), :]
    for inner in range(1, 8):
        rays = rays + sums_ref[pl.ds(inner, TILE, stride=8), :]
    rows = N_VOX * PAD
    sub, lane = iota((rows, TILE), 0), iota((rows, TILE), 1)
    choice = jnp.where(sub == slot_ref[...], 1.0, 0.0).astype(BF16)
    square = jnp.sum(field * field)
    head = extra_ref[...] + jnp.where((sub % PAD == HEAD) & (lane == CAP), square, 0.0)
    payload_ref[...] = select_rows(choice, jnp.transpose(rays)) + head


def forward_first_kernel(received_ref, tiles_ref, slot_ref, tile_vox_ref, extra_ref, payload_ref, normal_ref, sums_ref):
    field, unused = gather_field(received_ref)
    normal_ref[...] = field
    forward_tiles(field, tiles_ref, slot_ref, tile_vox_ref, extra_ref, payload_ref, sums_ref)


def forward_kernel(
    received_ref, tiles_ref, slot_ref, tile_vox_ref, extra_ref, normal0_ref, gamma_ref,
    payload_ref, normal_ref, step_ref, sums_ref,
):
    field, square = gather_field(received_ref)
    step_size = gamma_ref[...] / square
    normal = normal0_ref[...] - step_size[0:1, :] * field
    normal_ref[...] = normal
    step_ref[...] = step_size
    forward_tiles(normal, tiles_ref, slot_ref, tile_vox_ref, extra_ref, payload_ref, sums_ref)


def owner_parts(received_ref):
    received = received_ref[...]
    rows = N_VOX * PAD
    blocks = received.reshape(N_VOX, PAD, TILE)
    head = jnp.broadcast_to(blocks[:, HEAD : HEAD + 1, :], (N_VOX, PAD, TILE)).reshape(rows, TILE)
    sub, lane = iota((rows, TILE), 0), iota((rows, TILE), 1)
    place = sub % PAD
    column = jnp.sum(jnp.where((lane == place) & (place < CAP), head, 0.0), axis=1, keepdims=True)
    hit = (column.astype(jnp.int32) == lane) & (place < CAP)
    choice = jnp.where(hit, 1.0, 0.0)
    total = select_rows(jnp.transpose(choice).astype(BF16), received)
    gamma = jnp.sum(jnp.where((place == HEAD) & (lane == CAP), received, 0.0))
    return choice.astype(BF16), total, gamma


def write_owner(choice, image, owned, payload_ref):
    rows = N_VOX * PAD
    sub, lane = iota((rows, TILE), 0), iota((rows, TILE), 1)
    own_rows = iota((TILE, TILE), 0) < owned
    square = jnp.sum(jnp.where(own_rows, image * image, 0.0))
    head = jnp.where((sub % PAD == HEAD) & (lane == 0), square, 0.0)
    payload_ref[...] = select_rows(choice, image) + head


def owner_first_kernel(received_ref, payload_ref, image_ref, gamma_ref):
    choice, image, gamma = owner_parts(received_ref)
    owned = image_ref.shape[0]
    image_ref[...] = image[0:owned, :]
    gamma_ref[...] = jnp.full((8, TILE), gamma, F32)
    write_owner(choice, image, owned, payload_ref)


def owner_kernel(received_ref, image0_ref, gamma0_ref, payload_ref, image_ref, gamma_ref):
    choice, image, gamma = owner_parts(received_ref)
    owned = image_ref.shape[0]
    now = jnp.full((8, TILE), gamma, F32)
    ratio = now / gamma0_ref[...]
    gamma_ref[...] = now
    lower = image[0:owned, :] + ratio[0:1, :] * image0_ref[...]
    image_ref[...] = lower
    image = jnp.concatenate([lower, jnp.zeros((TILE - owned, TILE), F32)], axis=0)
    write_owner(choice, image, owned, payload_ref)


def last_kernel(
    received_ref, normal0_ref, normal1_ref, gamma0_ref, gamma1_ref, step0_ref, image0_ref, image1_ref, ray_ref,
    solution_ref, residual_ref, normal_ref,
):
    field, square = gather_field(received_ref)
    ratio = (gamma1_ref[...] / gamma0_ref[...])[0:1, :]
    step0 = step0_ref[0:1, :]
    step1 = (gamma1_ref[...] / square)[0:1, :]
    normal0, normal1 = normal0_ref[...], normal1_ref[...]
    direction = normal1 + ratio * normal0
    solution_ref[...] = step0 * normal0 + step1 * direction
    normal_ref[...] = normal1 - step1 * field
    residual_ref[...] = ray_ref[...] - step0 * image0_ref[...] - step1 * image1_ref[...]


def call(kernel, outs, scratch, args, smem=0):
    spec = pl.BlockSpec(memory_space=pltpu.VMEM)
    specs = [pl.BlockSpec(memory_space=pltpu.SMEM)] * smem + [spec] * (len(args) - smem)
    return pl.pallas_call(
        kernel,
        out_shape=[jax.ShapeDtypeStruct(shape, F32) for shape in outs],
        in_specs=specs,
        out_specs=[spec] * len(outs),
        scratch_shapes=[pltpu.VMEM(shape, F32) for shape in scratch],
        compiler_params=pltpu.CompilerParams(vmem_limit_bytes=24 * 1024 * 1024),
    )(*args)


def local(tile_values, tile_vox, tile_slot, slot_block, ray_data):
    owned = ray_data.shape[0]
    send_map = slot_block[0]
    dense_index = tile_slot // CAP * owned + jnp.take(send_map, tile_slot, axis=0)
    slot_row = (tile_slot // CAP * PAD + tile_slot % CAP).reshape(1, TILE)
    vox_row = tile_vox.reshape(1, TILE)
    extra = jnp.pad(
        send_map.astype(F32).reshape(N_VOX, 1, CAP), ((0, 0), (HEAD, PAD - HEAD - 1), (0, TILE - CAP))
    ).reshape(N_VOX * PAD, TILE)

    block = (TILE, TILE)
    sent = (N_VOX * PAD, TILE)
    field = (VT_DEV, TILE)
    scalar = (8, TILE)
    exchange = (N_ROW, EXCH, TILE)
    rays = (owned, TILE)

    def over_vox(array):
        return lax.all_to_all(array, "vox", 0, 0, tiled=True)

    def over_row(array):
        return lax.all_to_all(array, "row", 0, 0, tiled=True)

    copies = jnp.broadcast_to(ray_data[None], (N_VOX, owned, TILE)).reshape(N_VOX * owned, TILE)
    whole = over_vox(copies)
    tiles = jnp.transpose(tile_values, (1, 2, 0))

    (parts,) = call(back_first_kernel, [exchange], [block, block], (dense_index, whole, tiles, vox_row), smem=1)
    parts = over_row(parts)
    payload, normal0 = call(
        forward_first_kernel, [sent, field], [(TILE * 8, TILE)], (parts, tiles, slot_row, vox_row, extra)
    )
    payload, image0, gamma0 = call(owner_first_kernel, [sent, rays, scalar], [], (over_vox(payload),))
    (parts,) = call(back_kernel, [exchange], [block], (over_vox(payload), tiles, slot_row, vox_row))
    parts = over_row(parts)
    payload, normal1, step0 = call(
        forward_kernel,
        [sent, field, scalar],
        [(TILE * 8, TILE)],
        (parts, tiles, slot_row, vox_row, extra, normal0, gamma0),
    )
    payload, image1, gamma1 = call(owner_kernel, [sent, rays, scalar], [], (over_vox(payload), image0, gamma0))
    (parts,) = call(back_kernel, [exchange], [block], (over_vox(payload), tiles, slot_row, vox_row))
    parts = over_row(parts)
    return tuple(
        call(
            last_kernel,
            [field, rays, field],
            [],
            (parts, normal0, normal1, gamma0, gamma1, step0, image0, image1, ray_data),
        )
    )


def solution(mesh):
    return jax.shard_map(
        local,
        mesh=mesh,
        in_specs=(
            P(("vox", "row"), None, None),
            P(("vox", "row")),
            P(("vox", "row")),
            P(("vox", "row"), None),
            P(("vox", "row"), None),
        ),
        out_specs=(P("vox", None), P(("vox", "row"), None), P("vox", None)),
        check_vma=False,
    )
```

time: 902 us -> 160 us (0.18)
  waiting for transfers between devices: 514 us -> 23.2 us
  blocking collectives: 277 us -> 87.5 us
  matrix products: 58.9 us -> 0 us
  other arithmetic: 20.7 us -> 0.04 us
  between operations: 18.3 us -> 0.75 us
  starting transfers between devices: 0.73 us -> 15.9 us
  Pallas kernels: 0 us -> 10.8 us
    psum x4 -> x0, blocking collectives: 277 us -> none  [the longest x2 150 us: local(): step_size = norm_now / lax.psum(jnp.sum(result * result), ('vox', 'row'))]
    psum x3 -> x0, waiting for transfers between devices: 213 us -> none  [backward(): return lax.psum(local_sum, 'row')]
    reduce_scatter x2 -> x0, waiting for transfers between devices: 162 us -> none  [local(): result = lax.psum_scatter(term, 'vox', scatter_dimension=0, tiled=True)]
    all_gather x3 -> x0, waiting for transfers between devices: 138 us -> none  [backward(): whole = lax.all_gather(values, 'vox', axis=0, tiled=True)]
    all_to_all x0 -> x6, blocking collectives: none -> 87.5 us  [the longest x4 45.2 us: over_vox(): return lax.all_to_all(array, 'vox', 0, 0, tiled=True)]
    dot_general x5 -> x0, matrix products: 58.9 us -> none  [the longest x2 30.8 us: local(): jnp.einsum('tab,tb->ta', tile_values, gathered, precision=lax.Precision.H...]
    all_to_all x0 -> x2, waiting for transfers between devices: none -> 23.2 us  [the longest x1 17.1 us: over_row(): return lax.all_to_all(array, 'row', 0, 0, tiled=True)]
    all_to_all x0 -> x2, starting transfers between devices: none -> 15.9 us  [the longest x1 8.58 us: over_row(): return lax.all_to_all(array, 'row', 0, 0, tiled=True)]
  transfers between devices with their start and end apart: 8 -> 2, of which waited for: 8 -> 2; matrix products, arithmetic and copies ran while one was open for 1% -> 7% of each run, Pallas kernels for 0% -> 0%
where the time goes in v1:
time: 160 us; the launch traced here: 158 us
  blocking collectives  87.5 us (55%)
  waiting for transfers between devices  23.2 us (14%)
  local copies, waits for them, and re-layouts  19.4 us (12%)
  starting transfers between devices  15.9 us (10%)
  Pallas kernels  10.8 us (7%)
    all_to_all x4, blocking collectives, over_vox(): return lax.all_to_all(array, 'vox', 0, 0, tiled=True)  45.2 us
    all_to_all x2, blocking collectives, over_row(): return lax.all_to_all(array, 'row', 0, 0, tiled=True)  42.3 us
    all_to_all x1, waiting for transfers between devices, over_row(): return lax.all_to_all(array, 'row', 0, 0, tiled=True)  17.1 us
    unnamed x15, local copies, waits for them, and re-layouts  16.1 us
    pallas_call x8, Pallas kernels, call(): pl.pallas_call(kernel, out_shape=[jax.ShapeDtypeStruct(shape, F32) for sh...  10.8 us
    all_to_all x1, starting transfers between devices, over_row(): return lax.all_to_all(array, 'row', 0, 0, tiled=True)  8.58 us
    all_to_all x1, starting transfers between devices, over_vox(): return lax.all_to_all(array, 'vox', 0, 0, tiled=True)  7.32 us
    all_to_all x1, waiting for transfers between devices, over_vox(): return lax.all_to_all(array, 'vox', 0, 0, tiled=True)  6.14 us
  transfers between devices with their start and end apart: 2, of which 2 were waited for; matrix products, arithmetic and copies ran while one was open for 7% of the time, Pallas kernels for 0%

profile of v1, /device:TPU:32, one launch (start us, length us, event | category | flops | bytes accessed | tf_op | source)
XLA Modules:
  0.0 157.7 jit_solution(10863888403901116419)
XLA Ops:
  0.6 1.9 %broadcast_in_dim.16 = f32[32,64,128]{2,1,0:T(8,128)} broadcast(f32[64,128]{1,0:T(8,128)} %ray_ref.1), dimensions={1,2} | broadcast | bytes 1081344 | tf_op jit(solution)/shard_map/broadcast_in_dim | solution.py:228
  2.6 7.3 %all-to-all-start = ((f32[32,64,128]{2,1,0:T(8,128)}), f32[32,64,128]{2,1,0:T(8,128)S(1)}, u32[]{:S(2)}, u32[]{:S(2)}) async-start(f32[32,64,128]{2,1,0:T(8,128)} %broadcast_in_dim.16), calls=%async_computation | async-start | bytes 2097152 | tf_op jit(solution)/shard_map/all_to_all | solution.py:223
  9.9 0.0 copy-start.6
  9.9 0.0 copy-start.5
  9.9 0.0 copy-start.4
  9.9 9.3 %copy.10 = f32[128,128,128]{0,2,1:T(8,128)} copy(f32[128,128,128]{2,1,0:T(8,128)} %param.5) | data formatting | bytes 16777216 | tf_op args[0]
  19.3 0.0 copy-done.6
  19.3 0.0 copy-done.5
  19.3 1.2 gather_fusion
  20.6 6.1 %all-to-all-done = f32[32,64,128]{2,1,0:T(8,128)S(1)} async-done(((f32[32,64,128]{2,1,0:T(8,128)}), f32[32,64,128]{2,1,0:T(8,128)S(1)}, u32[]{:S(2)}, u32[]{:S(2)}) %all-to-all-start) | async-done | bytes 1048608 | tf_op jit(solution)/shard_map/all_to_all | solution.py:223
  26.7 0.0 copy-done.4
  26.7 0.0 copy-start
  26.7 3.4 %copy-done = f32[128,128,128]{0,2,1:T(8,128)S(1)} copy-done((f32[128,128,128]{0,2,1:T(8,128)S(1)}, f32[128,128,128]{0,2,1:T(8,128)}, u32[]{:S(2)}) %copy-start) | copy-done | bytes 8388632
  30.1 2.3 %shard_map.76 = f32[8,136,128]{2,1,0:T(8,128)} custom-call(s32[128]{0:T(128)S(1)} %fusion.1.dense_ref, f32[2048,128]{1,0:T(8,128)S(1)} %bitcast.22, f32[128,128,128]{2,1,0:T(8,128)S(1)} %bitcast.17, s32[1,128]{1,0:T(1,128)S(1)} %bitcast.31), custom_call_target="tpu_custom_call" | custom-call | tf_op jit(solution)/shard_map/pallas_call | solution.py:195
  32.4 8.6 %all-to-all-start.1 = ((f32[8,136,128]{2,1,0:T(8,128)}), f32[8,136,128]{2,1,0:T(8,128)S(1)}, u32[]{:S(2)}, u32[]{:S(2)}) async-start(f32[8,136,128]{2,1,0:T(8,128)} %shard_map.76), calls=%async_computation.1 | async-start | bytes 1114112 | tf_op jit(solution)/shard_map/all_to_all | solution.py:226
  41.0 0.1 convert_element_type.16
  41.2 17.1 %all-to-all-done.1.received_ref = f32[8,136,128]{2,1,0:T(8,128)S(1)} async-done(((f32[8,136,128]{2,1,0:T(8,128)}), f32[8,136,128]{2,1,0:T(8,128)S(1)}, u32[]{:S(2)}, u32[]{:S(2)}) %all-to-all-start.1) | async-done | bytes 557088 | tf_op jit(solution)/shard_map/all_to_all | solution.py:226
  58.3 0.0 copy-start.1
  58.3 3.4 %copy-done.1 = f32[128,128,128]{0,2,1:T(8,128)S(1)} copy-done((f32[128,128,128]{0,2,1:T(8,128)S(1)}, f32[128,128,128]{0,2,1:T(8,128)}, u32[]{:S(2)}) %copy-start.1) | copy-done | bytes 8388632
  61.6 0.0 copy-start.2
  61.6 2.0 %shard_map.77 = (f32[256,128]{1,0:T(8,128)S(1)}, f32[256,128]{1,0:T(8,128)S(1)}) custom-call(f32[8,136,128]{2,1,0:T(8,128)S(1)} %all-to-all-done.1.received_ref, f32[128,128,128]{2,1,0:T(8,128)S(1)} %bitcast.18, s32[1,128]{1,0:T(1,128)S(1)} %get-tuple-element.25.slot_ref, s32[1,128]{1,0:T(1,128)S(1)} %bitcast.32, f32[256,128]{1,0:T(8,128)S(1)} %pad_bitcast_fusion.extra_ref), custom_call_target="tpu_custom_call" | custom-call | tf_op jit(solution)/shard_map/pallas_call | solution.py:195
  63.7 11.5 %all_to_all.67 = f32[32,8,128]{2,1,0:T(8,128)S(1)} all-to-all(f32[32,8,128]{2,1,0:T(8,128)S(1)} %bitcast.30), channel_id=1, replica_groups=mesh['vox'=32,'row'=8] {'vox'}, dimensions={0} | all-to-all | bytes 262144 | tf_op jit(solution)/shard_map/all_to_all | solution.py:223
  75.2 0.6 shard_map.78
  75.8 11.3 %all_to_all.68 = f32[32,8,128]{2,1,0:T(8,128)S(1)} all-to-all(f32[32,8,128]{2,1,0:T(8,128)S(1)} %bitcast.28), channel_id=1, replica_groups=mesh['vox'=32,'row'=8] {'vox'}, dimensions={0} | all-to-all | bytes 262144 | tf_op jit(solution)/shard_map/all_to_all | solution.py:223
  87.1 0.0 copy-done.2
  87.1 1.0 shard_map.79
  88.1 21.2 %all_to_all.69.received_ref = f32[8,136,128]{2,1,0:T(8,128)S(1)} all-to-all(f32[8,136,128]{2,1,0:T(8,128)S(1)} %shard_map.79), channel_id=1, replica_groups=mesh['vox'=32,'row'=8] {'row'}, dimensions={0} | all-to-all | bytes 1114112 | tf_op jit(solution)/shard_map/all_to_all | solution.py:226
  109.3 0.0 copy-start.3
  109.3 2.0 %shard_map.80 = (f32[256,128]{1,0:T(8,128)S(1)}, f32[256,128]{1,0:T(8,128)S(1)}, f32[8,128]{1,0:T(8,128)S(1)}) custom-call(f32[8,136,128]{2,1,0:T(8,128)S(1)} %all_to_all.69.received_ref, f32[128,128,128]{2,1,0:T(8,128)S(1)} %bitcast.20, s32[1,128]{1,0:T(1,128)S(1)} %get-tuple-element.25.slot_ref, s32[1,128]{1,0:T(1,128)S(1)} %bitcast.34, ...), custom_call_target="tpu_custom_call" | custom-call | tf_op jit(solution)/shard_map/pallas_call | solution.py:195
  111.3 11.1 %all_to_all.70 = f32[32,8,128]{2,1,0:T(8,128)S(1)} all-to-all(f32[32,8,128]{2,1,0:T(8,128)S(1)} %bitcast.27), channel_id=1, replica_groups=mesh['vox'=32,'row'=8] {'vox'}, dimensions={0} | all-to-all | bytes 262144 | tf_op jit(solution)/shard_map/all_to_all | solution.py:223
  122.4 0.6 shard_map.81
  123.0 11.3 %all_to_all.71 = f32[32,8,128]{2,1,0:T(8,128)S(1)} all-to-all(f32[32,8,128]{2,1,0:T(8,128)S(1)} %bitcast.29), channel_id=1, replica_groups=mesh['vox'=32,'row'=8] {'vox'}, dimensions={0} | all-to-all | bytes 262144 | tf_op jit(solution)/shard_map/all_to_all | solution.py:223
  134.3 1.0 shard_map.82
  135.3 21.1 %all_to_all.72.received_ref = f32[8,136,128]{2,1,0:T(8,128)S(1)} all-to-all(f32[8,136,128]{2,1,0:T(8,128)S(1)} %shard_map.82), channel_id=1, replica_groups=mesh['vox'=32,'row'=8] {'row'}, dimensions={0} | all-to-all | bytes 1114112 | tf_op jit(solution)/shard_map/all_to_all | solution.py:226
  156.5 0.0 copy-done.3
  156.5 1.2 shard_map.83
  (5 shorter events, 0.1 us)
Async XLA Ops:
  2.6 24.1 %all-to-all-start = ((f32[32,64,128]{2,1,0:T(8,128)}), f32[32,64,128]{2,1,0:T(8,128)S(1)}, u32[]{:S(2)}, u32[]{:S(2)}) async-start(f32[32,64,128]{2,1,0:T(8,128)} %broadcast_in_dim.16), calls=%async_computation | async-start | bytes 2097152 | tf_op jit(solution)/shard_map/all_to_all | solution.py:223
  9.9 9.4 %copy-start.6 = (s32[128]{0:T(128)S(1)}, s32[128]{0:T(128)}, u32[]{:S(2)}) copy-start(s32[128]{0:T(128)} %param.7) | copy-start | bytes 1540
  9.9 9.4 %copy-start.5 = (s32[1,128]{1,0:T(1,128)S(1)}, s32[1,128]{1,0:T(1,128)}, u32[]{:S(2)}) copy-start(s32[1,128]{1,0:T(1,128)} %param.8) | copy-start | bytes 1540
  9.9 16.8 %copy-start.4 = (s32[128]{0:T(128)S(1)}, s32[128]{0:T(128)}, u32[]{:S(2)}) copy-start(s32[128]{0:T(128)} %param.6) | copy-start | bytes 1540
  26.7 3.4 %copy-start = (f32[128,128,128]{0,2,1:T(8,128)S(1)}, f32[128,128,128]{0,2,1:T(8,128)}, u32[]{:S(2)}) copy-start(f32[128,128,128]{0,2,1:T(8,128)} %copy.10) | copy-start | bytes 25165828
  32.4 25.8 %all-to-all-start.1 = ((f32[8,136,128]{2,1,0:T(8,128)}), f32[8,136,128]{2,1,0:T(8,128)S(1)}, u32[]{:S(2)}, u32[]{:S(2)}) async-start(f32[8,136,128]{2,1,0:T(8,128)} %shard_map.76), calls=%async_computation.1 | async-start | bytes 1114112 | tf_op jit(solution)/shard_map/all_to_all | solution.py:226
  58.3 3.4 %copy-start.1 = (f32[128,128,128]{0,2,1:T(8,128)S(1)}, f32[128,128,128]{0,2,1:T(8,128)}, u32[]{:S(2)}) copy-start(f32[128,128,128]{0,2,1:T(8,128)} %copy.10) | copy-start | bytes 25165828
  61.6 25.4 %copy-start.2 = (f32[128,128,128]{0,2,1:T(8,128)S(1)}, f32[128,128,128]{0,2,1:T(8,128)}, u32[]{:S(2)}) copy-start(f32[128,128,128]{0,2,1:T(8,128)} %copy.10) | copy-start | bytes 25165828
  109.3 47.2 %copy-start.3 = (f32[64,128]{1,0:T(8,128)S(1)}, f32[64,128]{1,0:T(8,128)}, u32[]{:S(2)}) copy-start(f32[64,128]{1,0:T(8,128)} %ray_ref.1) | copy-start | bytes 98308

commit v2 on v1

v2 whole, which is shorter than its diff:
```python
import functools

import jax
import jax.numpy as jnp
from jax import lax
from jax.experimental import pallas as pl
from jax.experimental.pallas import tpu as pltpu
from jax.sharding import PartitionSpec as P

TILE = 128
VT_DEV = 256
CAP = 4
N_VOX = 32
N_ROW = 8
CORES = 2
CHIPS = N_VOX // CORES
CHUNKS = 8
PAD = 8
MAP = CAP
NORM = CAP + 1
SENT = N_VOX * PAD
PART = TILE + 8
SUM = VT_DEV + 8

F32 = jnp.float32
BF16 = jnp.bfloat16


def iota(shape, dim):
    return lax.broadcasted_iota(jnp.int32, shape, dim)


def select_rows(choice, values):
    high = values.astype(BF16)
    rest = values - high.astype(F32)
    middle = rest.astype(BF16)
    low = (rest - middle.astype(F32)).astype(BF16)
    total = jnp.dot(choice, low, preferred_element_type=F32)
    total = total + jnp.dot(choice, middle, preferred_element_type=F32)
    return total + jnp.dot(choice, high, preferred_element_type=F32)


def select_columns(values, choice):
    high = values.astype(BF16)
    rest = values - high.astype(F32)
    middle = rest.astype(BF16)
    low = (rest - middle.astype(F32)).astype(BF16)
    total = jnp.dot(low, choice, preferred_element_type=F32)
    total = total + jnp.dot(middle, choice, preferred_element_type=F32)
    return total + jnp.dot(high, choice, preferred_element_type=F32)


def one_hot(rows, index):
    return jnp.where(iota((rows, TILE), 0) == index, 1.0, 0.0).astype(BF16)


def copies_kernel(ray_hbm, copies_ref, ray_ref, sem):
    move = pltpu.make_async_copy(ray_hbm, ray_ref, sem)
    move.start()
    move.wait()
    owned = ray_ref.shape[0]
    rays = ray_ref[...]
    for chip in range(CHIPS):
        copies_ref[chip * owned : (chip + 1) * owned, :] = rays


def index_kernel(slot_ref, map_ref, row_ref, extra_ref, index_ref, *, owned):
    slot = slot_ref[...]
    target, place = lax.shift_right_logical(slot, 2), slot & (CAP - 1)
    row_ref[...] = target * PAD + place
    sub, lane = iota((TILE, TILE), 0), iota((TILE, TILE), 1)
    column = jnp.transpose(jnp.broadcast_to(map_ref[...].astype(F32), (TILE, TILE)))
    block = jnp.sum(jnp.where(sub == slot, column, 0.0), axis=0, keepdims=True).astype(jnp.int32)
    mine = lax.axis_index("vox") & (CORES - 1)
    other = (target & (CORES - 1)) ^ mine
    index_ref[...] = (other * CHIPS + lax.shift_right_logical(target, 1)) * owned + block
    values = jnp.where((sub & (CAP - 1)) == lane, column, 0.0).astype(BF16)
    sub, lane = iota((SENT, TILE), 0), iota((SENT, TILE), 1)
    hit = ((sub & (PAD - 1)) == MAP) & (lax.shift_right_logical(lane, 2) == lax.shift_right_logical(sub, 3))
    choice = jnp.where(hit, 1.0, 0.0).astype(BF16)
    extra_ref[...] = jnp.dot(choice, values, preferred_element_type=F32)


def relay_kernel(natural_ref, tiles_ref):
    def step(index, unused):
        block = natural_ref[:, pl.ds(pl.multiple_of(index * 8, 8), 8), :]
        block = jnp.swapaxes(block, 0, 1)
        for inner in range(8):
            tiles_ref[index * 8 + inner] = jnp.transpose(block[inner])
        return unused

    lax.fori_loop(0, TILE // 8, step, 0)


def back_tiles(tiles_ref, weight_ref):
    def step(index, total):
        for inner in range(8):
            ray = index * 8 + inner
            total = total + tiles_ref[ray] * weight_ref[pl.ds(ray, 1), :]
        return total

    return lax.fori_loop(0, TILE // 8, step, jnp.zeros((TILE, TILE), F32))


def write_tail(part_ref, vox_row, square):
    sub = iota((8, TILE), 0)
    tail = jnp.where(sub == 0, jnp.broadcast_to(vox_row.astype(F32), (8, TILE)), 0.0)
    part_ref[TILE:PART, :] = tail + jnp.where(sub == 1, jnp.broadcast_to(square, (8, TILE)), 0.0)


def back_first_kernel(index_ref, tiles_hbm, same_ref, other_ref, vox_ref, part_ref, natural_ref, picked_ref, sems):
    size = TILE // CHUNKS
    moves = []
    for chunk in range(CHUNKS):
        where = pl.ds(chunk * size, size)
        moves.append(pltpu.make_async_copy(tiles_hbm.at[where], natural_ref.at[where], sems.at[chunk]))
    for move in moves:
        move.start()
    half = same_ref.shape[0]
    for tile in range(TILE):
        index = index_ref[0, tile]
        here = index < half
        row = jnp.where(here, index, index - half)
        picked_ref[tile : tile + 1, :] = jnp.where(here, same_ref[pl.ds(row, 1), :], other_ref[pl.ds(row, 1), :])
    weight = jnp.transpose(picked_ref[...])
    write_tail(part_ref, vox_ref[...], jnp.zeros((1, TILE), F32))
    for group in range(TILE // 8):
        if group * 8 % size == 0:
            moves[group * 8 // size].wait()
        rows = []
        for tile in range(group * 8, group * 8 + 8):
            rows.append(jnp.sum(natural_ref[tile] * weight[:, tile : tile + 1], axis=0, keepdims=True))
        part_ref[group * 8 : group * 8 + 8, :] = jnp.concatenate(rows, axis=0)


def back_kernel(received_ref, tiles_ref, row_ref, vox_ref, part_ref, weight_ref):
    received = received_ref[...]
    weight_ref[...] = select_columns(jnp.transpose(received), one_hot(SENT, row_ref[...]))
    square = jnp.sum(received.reshape(N_VOX, PAD, TILE), axis=0)[NORM : NORM + 1, :]
    part_ref[0:TILE, :] = jnp.transpose(back_tiles(tiles_ref, weight_ref))
    write_tail(part_ref, vox_ref[...], square)


def quad_kernel(own_ref, one_ref, two_ref, three_ref, sum_ref):
    def spread(ref):
        where = ref[TILE : TILE + 1, :].astype(jnp.int32)
        return select_rows(one_hot(VT_DEV, where), ref[0:TILE, :])

    sum_ref[0:VT_DEV, :] = (spread(own_ref) + spread(one_ref)) + (spread(two_ref) + spread(three_ref))
    tail = slice(TILE, PART)
    sum_ref[VT_DEV:SUM, :] = (own_ref[tail, :] + one_ref[tail, :]) + (two_ref[tail, :] + three_ref[tail, :])


def whole_sum(near_ref, far_ref):
    field = near_ref[0:VT_DEV, :] + far_ref[0:VT_DEV, :]
    tail = near_ref[VT_DEV:SUM, :] + far_ref[VT_DEV:SUM, :]
    return field, jnp.sum(tail[1:2, :], axis=1, keepdims=True)


def forward_tiles(field, tiles_ref, row_ref, vox_ref, extra_ref, payload_ref, sums_ref):
    values = select_columns(jnp.transpose(field), one_hot(VT_DEV, vox_ref[...]))

    def step(index, unused):
        for inner in range(8):
            ray = index * 8 + inner
            product = tiles_ref[ray] * values
            sums_ref[pl.ds(pl.multiple_of(ray * 8, 8), 8), :] = jnp.sum(product.reshape(TILE // 8, 8, TILE), axis=0)
        return unused

    lax.fori_loop(0, TILE // 8, step, 0)
    rays = sums_ref[pl.ds(0, TILE, stride=8), :]
    for inner in range(1, 8):
        rays = rays + sums_ref[pl.ds(inner, TILE, stride=8), :]
    square = jnp.sum(field * field, axis=0, keepdims=True)
    head = jnp.where((iota((SENT, TILE), 0) & (PAD - 1)) == NORM, square, extra_ref[...])
    payload_ref[...] = select_rows(one_hot(SENT, row_ref[...]), jnp.transpose(rays)) + head


def forward_first_kernel(near_ref, far_ref, tiles_ref, row_ref, vox_ref, extra_ref, payload_ref, normal_ref, sums_ref):
    field, unused = whole_sum(near_ref, far_ref)
    normal_ref[...] = field
    forward_tiles(field, tiles_ref, row_ref, vox_ref, extra_ref, payload_ref, sums_ref)


def forward_kernel(
    near_ref, far_ref, tiles_ref, row_ref, vox_ref, extra_ref, normal0_ref, gamma_ref,
    payload_ref, normal_ref, step_ref, sums_ref,
):
    field, square = whole_sum(near_ref, far_ref)
    step_size = gamma_ref[...] / square
    normal = normal0_ref[...] - step_size[0:1, :] * field
    normal_ref[...] = normal
    step_ref[...] = step_size
    forward_tiles(normal, tiles_ref, row_ref, vox_ref, extra_ref, payload_ref, sums_ref)


def owner_parts(received_ref):
    received = received_ref[...]
    blocks = received.reshape(N_VOX, PAD, TILE)
    head = jnp.broadcast_to(blocks[:, MAP : MAP + 1, :], (N_VOX, PAD, TILE)).reshape(SENT, TILE)
    place, lane = iota((SENT, TILE), 0) & (PAD - 1), iota((SENT, TILE), 1)
    column = jnp.sum(jnp.where((lane == place) & (place < CAP), head, 0.0), axis=1, keepdims=True)
    hit = (column.astype(jnp.int32) == lane) & (place < CAP)
    choice = jnp.where(hit, 1.0, 0.0)
    image = select_rows(jnp.transpose(choice).astype(BF16), received)
    gamma = jnp.sum(jnp.sum(blocks, axis=0)[NORM : NORM + 1, :], axis=1, keepdims=True)
    return choice.astype(BF16), image, jnp.broadcast_to(gamma, (8, TILE))


def write_owner(choice, image, owned, payload_ref):
    square = jnp.where(iota((TILE, TILE), 0) < owned, image * image, 0.0)
    square = jnp.sum(square, axis=0, keepdims=True)
    head = jnp.where((iota((SENT, TILE), 0) & (PAD - 1)) == NORM, square, 0.0)
    payload_ref[...] = select_rows(choice, image) + head


def owner_first_kernel(received_ref, payload_ref, image_ref, gamma_ref):
    choice, image, gamma = owner_parts(received_ref)
    owned = image_ref.shape[0]
    image_ref[...] = image[0:owned, :]
    gamma_ref[...] = gamma
    write_owner(choice, image, owned, payload_ref)


def owner_kernel(received_ref, image0_ref, gamma0_ref, payload_ref, image_ref, gamma_ref):
    choice, image, gamma = owner_parts(received_ref)
    owned = image_ref.shape[0]
    ratio = gamma / gamma0_ref[...]
    gamma_ref[...] = gamma
    lower = image[0:owned, :] + ratio[0:1, :] * image0_ref[...]
    image_ref[...] = lower
    image = jnp.concatenate([lower, jnp.zeros((TILE - owned, TILE), F32)], axis=0)
    write_owner(choice, image, owned, payload_ref)


def last_kernel(
    near_ref, far_ref, normal0_ref, normal1_ref, gamma0_ref, gamma1_ref, step0_ref, image0_ref, image1_ref, ray_ref,
    solution_ref, residual_ref, normal_ref,
):
    field, square = whole_sum(near_ref, far_ref)
    ratio = (gamma1_ref[...] / gamma0_ref[...])[0:1, :]
    step0 = step0_ref[0:1, :]
    step1 = (gamma1_ref[...] / square)[0:1, :]
    normal0, normal1 = normal0_ref[...], normal1_ref[...]
    direction = normal1 + ratio * normal0
    solution_ref[...] = step0 * normal0 + step1 * direction
    normal_ref[...] = normal1 - step1 * field
    residual_ref[...] = ray_ref[...] - step0 * image0_ref[...] - step1 * image1_ref[...]


def call(kernel, outs, scratch, args, smem=0, hbm=0, cost=None, limit=24):
    vmem = pl.BlockSpec(memory_space=pltpu.VMEM)
    specs = [pl.BlockSpec(memory_space=pltpu.SMEM)] * smem + [pl.BlockSpec(memory_space=pl.ANY)] * hbm
    outs = [out if isinstance(out, jax.ShapeDtypeStruct) else jax.ShapeDtypeStruct(out, F32) for out in outs]
    return pl.pallas_call(
        kernel,
        out_shape=outs,
        in_specs=specs + [vmem] * (len(args) - smem - hbm),
        out_specs=[vmem] * len(outs),
        scratch_shapes=[pltpu.VMEM(shape, F32) if isinstance(shape, tuple) else shape for shape in scratch],
        cost_estimate=cost,
        compiler_params=pltpu.CompilerParams(vmem_limit_bytes=limit * 1024 * 1024),
    )(*args)


def local(tile_values, tile_vox, tile_slot, slot_block, ray_data):
    owned = ray_data.shape[0]
    block = (TILE, TILE)
    sent = (SENT, TILE)
    field = (VT_DEV, TILE)
    scalar = (8, TILE)
    part = (PART, TILE)
    sums = (TILE * 8, TILE)
    rays = (owned, TILE)
    indices = jax.ShapeDtypeStruct((1, TILE), jnp.int32)

    def over_vox(array):
        return lax.all_to_all(array, "vox", 0, 0, tiled=True)

    def across(array, distance):
        return lax.ppermute(array, "row", [(index, index ^ distance) for index in range(N_ROW)])

    def quad(own):
        others = [across(own, distance) for distance in (1, 2, 3)]
        return call(quad_kernel, [(SUM, TILE)], [], (own, *others))[0]

    def over_row(own):
        near = quad(own)
        return near, across(near, 6)

    (copies,) = call(
        copies_kernel,
        [(CHIPS * owned, TILE)],
        [rays, pltpu.SemaphoreType.DMA],
        (ray_data,),
        hbm=1,
        limit=60,
    )
    chips = [[chip * CORES + core for chip in range(CHIPS)] for core in range(CORES)]
    same = lax.all_to_all(copies, "vox", 0, 0, tiled=True, axis_index_groups=chips)
    same, tile_vox, tile_slot, slot_block = lax.optimization_barrier((same, tile_vox, tile_slot, slot_block))
    other = lax.ppermute(same, "vox", [(device, device ^ 1) for device in range(N_VOX)])
    vox_row = tile_vox.reshape(1, TILE)
    slot_row, extra, index = call(
        functools.partial(index_kernel, owned=owned),
        [indices, sent, indices],
        [],
        (tile_slot.reshape(1, TILE), slot_block),
    )
    parts, natural = call(
        back_first_kernel,
        [part, (TILE, TILE, TILE)],
        [block, pltpu.SemaphoreType.DMA((CHUNKS,))],
        (index, tile_values, same, other, vox_row),
        smem=1,
        hbm=1,
        limit=42,
    )
    near = quad(parts)
    near, natural = lax.optimization_barrier((near, natural))
    far = across(near, 6)
    (tiles,) = call(
        relay_kernel,
        [(TILE, TILE, TILE)],
        [],
        (natural,),
        cost=pl.CostEstimate(flops=0, bytes_accessed=2**24, transcendentals=0),
    )
    payload, normal0 = call(
        forward_first_kernel, [sent, field], [sums], (near, far, tiles, slot_row, vox_row, extra)
    )
    payload, image0, gamma0 = call(owner_first_kernel, [sent, rays, scalar], [], (over_vox(payload),))
    (parts,) = call(back_kernel, [part], [block], (over_vox(payload), tiles, slot_row, vox_row))
    near, far = over_row(parts)
    payload, normal1, step0 = call(
        forward_kernel,
        [sent, field, scalar],
        [sums],
        (near, far, tiles, slot_row, vox_row, extra, normal0, gamma0),
    )
    payload, image1, gamma1 = call(owner_kernel, [sent, rays, scalar], [], (over_vox(payload), image0, gamma0))
    (parts,) = call(back_kernel, [part], [block], (over_vox(payload), tiles, slot_row, vox_row))
    near, far = over_row(parts)
    return tuple(
        call(
            last_kernel,
            [field, rays, field],
            [],
            (near, far, normal0, normal1, gamma0, gamma1, step0, image0, image1, ray_data),
        )
    )


def solution(mesh):
    return jax.shard_map(
        local,
        mesh=mesh,
        in_specs=(
            P(("vox", "row"), None, None),
            P(("vox", "row")),
            P(("vox", "row")),
            P(("vox", "row"), None),
            P(("vox", "row"), None),
        ),
        out_specs=(P("vox", None), P(("vox", "row"), None), P("vox", None)),
        check_vma=False,
    )
```

time: 160 us -> 139 us (0.87); the launches traced: 158 us -> 139 us
  blocking collectives: 87.5 us -> 63.7 us
  local copies, waits for them, and re-layouts: 19.4 us -> 1.98 us
  starting transfers between devices: 15.9 us -> 26.2 us
  Pallas kernels: 10.8 us -> 19.1 us
  waiting for transfers between devices: 23.2 us -> 27 us
    ppermute x0 -> x13, waiting for transfers between devices: none -> 27 us  [the longest x12 26.7 us: across(): lax.ppermute(array, 'row', [(index, index ^ distance) for index in range(...]
    ppermute x0 -> x13, starting transfers between devices: none -> 26.2 us  [the longest x12 26.2 us: across(): lax.ppermute(array, 'row', [(index, index ^ distance) for index in range(...]
    all_to_all x2 -> x1, blocking collectives: 42.3 us -> 18.5 us  [local(): lax.all_to_all(copies, 'vox', 0, 0, tiled=True, axis_index_groups=chips)]
    all_to_all x2 -> x0, waiting for transfers between devices: 23.2 us -> none  [the longest x1 17.1 us: over_row(): return lax.all_to_all(array, 'row', 0, 0, tiled=True)]
    all_to_all x2 -> x0, starting transfers between devices: 15.9 us -> none  [the longest x1 8.58 us: over_row(): return lax.all_to_all(array, 'row', 0, 0, tiled=True)]
    unnamed x15 -> x10, local copies, waits for them, and re-layouts: 16.1 us -> 1.98 us
    pallas_call x8 -> x14, Pallas kernels: 10.8 us -> 19.1 us  [call(): pl.pallas_call(kernel, out_shape=outs, in_specs=specs + [vmem] * (len(arg...]
    broadcast_in_dim x1 -> x0, local copies, waits for them, and re-layouts: 1.95 us -> none  [local(): jnp.broadcast_to(ray_data[None], (N_VOX, owned, TILE))]
  transfers between devices with their start and end apart: 2 -> 13, of which waited for: 2 -> 11; matrix products, arithmetic and copies ran while one was open for 7% -> 0% of each run, Pallas kernels for 0% -> 3%
where the time goes in v2:
time: 139 us
  blocking collectives  63.7 us (46%)
  waiting for transfers between devices  27 us (19%)
  starting transfers between devices  26.2 us (19%)
  Pallas kernels  19.1 us (14%)
  local copies, waits for them, and re-layouts  1.98 us (1%)
    all_to_all x4, blocking collectives, over_vox(): return lax.all_to_all(array, 'vox', 0, 0, tiled=True)  45.1 us
    ppermute x12, waiting for transfers between devices, across(): lax.ppermute(array, 'row', [(index, index ^ distance) for index in range(...  26.7 us
    ppermute x12, starting transfers between devices, across(): lax.ppermute(array, 'row', [(index, index ^ distance) for index in range(...  26.2 us
    pallas_call x14, Pallas kernels, call(): pl.pallas_call(kernel, out_shape=outs, in_specs=specs + [vmem] * (len(arg...  19.1 us
    all_to_all x1, blocking collectives, local(): lax.all_to_all(copies, 'vox', 0, 0, tiled=True, axis_index_groups=chips)  18.5 us
  transfers between devices with their start and end apart: 13, of which 11 were waited for; matrix products, arithmetic and copies ran while one was open for 0% of the time, Pallas kernels for 3%

profile of v2, /device:TPU:32, one launch (start us, length us, event | category | flops | bytes accessed | tf_op | source)
XLA Modules:
  0.0 138.7 jit_solution(16779934306742162410)
XLA Ops:
  0.6 1.6 %shard_map.76 = f32[1024,128]{1,0:T(8,128)} custom-call(f32[64,128]{1,0:T(8,128)} %ray_ref.1), custom_call_target="tpu_custom_call" | custom-call | tf_op jit(solution)/shard_map/pallas_call | solution.py:255
  2.3 18.5 %all_to_all.56 = f32[16,64,128]{2,1,0:T(8,128)S(1)} all-to-all(f32[16,64,128]{2,1,0:T(8,128)} %bitcast.28), channel_id=1, replica_groups={{0,16,32,48,64,80,96,112,128,144,160,176,192,208,224,240},{8,24,40,56,7..., dimensions={0} | all-to-all | bytes 1048576 | tf_op jit(solution)/shard_map/all_to_all | solution.py:300
  20.8 0.0 collective-permute-start
  20.8 0.7 copy-done.3
  21.5 0.7 copy-done.4
  22.1 0.2 shard_map.77
  22.3 0.4 collective-permute-done.other_ref
  22.7 0.7 copy-done.1
  23.4 5.2 %shard_map.78 = (f32[136,128]{1,0:T(8,128)S(1)}, f32[128,128,128]{2,1,0:T(8,128)S(1)}) custom-call(s32[1,128]{1,0:T(1,128)S(1)} %get-tuple-element.27.index_ref, f32[128,128,128]{2,1,0:T(8,128)} %tiles_hbm.1, f32[1024,128]{1,0:T(8,128)S(1)} %bitcast.13, f32[1024,128]{1,0:T(8,128)S(1)} %collective-permute-done.other_ref, s32[1,128]{1,0:T(1,128)S(1)} %bitcast.22), custom_call_target="tpu_custom_call" | custom-call | tf_op jit(solution)/shard_map/pallas_call | solution.py:255
  28.5 2.0 %collective-permute-start.3 = (f32[136,128]{1,0:T(8,128)S(1)}, f32[136,128]{1,0:T(8,128)S(1)}, u32[]{:S(2)}, u32[]{:S(2)}) collective-permute-start(f32[136,128]{1,0:T(8,128)S(1)} %get-tuple-element.30.own_ref), channel_id=1, source_target_pairs={{0,3},{1,2},{2,1},{3,0},{4,7},{5,6},{6,5},{7,4},{8,11},{9,10},{10,... | collective-permute-start | bytes 208904 | tf_op jit(solution)/shard_map/ppermute | solution.py:281
  30.5 1.5 %collective-permute-start.2 = (f32[136,128]{1,0:T(8,128)S(1)}, f32[136,128]{1,0:T(8,128)S(1)}, u32[]{:S(2)}, u32[]{:S(2)}) collective-permute-start(f32[136,128]{1,0:T(8,128)S(1)} %get-tuple-element.30.own_ref), channel_id=1, source_target_pairs={{0,2},{1,3},{2,0},{3,1},{4,6},{5,7},{6,4},{7,5},{8,10},{9,11},{10,... | collective-permute-start | bytes 208904 | tf_op jit(solution)/shard_map/ppermute | solution.py:281
  32.0 1.4 collective-permute-start.1
  33.4 2.7 %collective-permute-done.3.three_ref = f32[136,128]{1,0:T(8,128)S(1)} collective-permute-done((f32[136,128]{1,0:T(8,128)S(1)}, f32[136,128]{1,0:T(8,128)S(1)}, u32[]{:S(2)}, u32[]{:S(2)}) %collective-permute-start.3) | collective-permute-done | bytes 69664 | tf_op jit(solution)/shard_map/ppermute | solution.py:281
  36.0 0.6 collective-permute-done.2.two_ref
  36.7 1.9 %collective-permute-done.1.one_ref = f32[136,128]{1,0:T(8,128)S(1)} collective-permute-done((f32[136,128]{1,0:T(8,128)S(1)}, f32[136,128]{1,0:T(8,128)S(1)}, u32[]{:S(2)}, u32[]{:S(2)}) %collective-permute-start.1) | collective-permute-done | bytes 69664 | tf_op jit(solution)/shard_map/ppermute | solution.py:281
  38.6 0.4 shard_map.79.near_ref
  39.0 0.0 copy-start.2
  39.0 4.7 %collective-permute-start.4 = (f32[264,128]{1,0:T(8,128)S(1)}, f32[264,128]{1,0:T(8,128)S(1)}, u32[]{:S(2)}, u32[]{:S(2)}) collective-permute-start(f32[264,128]{1,0:T(8,128)S(1)} %shard_map.79.near_ref), channel_id=1, source_target_pairs={{0,6},{1,7},{2,4},{3,5},{4,2},{5,3},{6,0},{7,1},{8,14},{9,15},{10,... | collective-permute-start | bytes 405512 | tf_op jit(solution)/shard_map/ppermute | solution.py:281
  43.7 4.2 %shard_map.80.tiles_ref = f32[128,128,128]{2,1,0:T(8,128)S(1)} custom-call(f32[128,128,128]{2,1,0:T(8,128)S(1)} %get-tuple-element.33.natural_ref), custom_call_target="tpu_custom_call" | custom-call | bytes 16777216 | tf_op jit(solution)/shard_map/pallas_call | solution.py:255
  48.0 1.2 collective-permute-done.4.far_ref
  49.2 1.4 shard_map.81
  50.6 11.4 %all_to_all.57 = f32[32,8,128]{2,1,0:T(8,128)S(1)} all-to-all(f32[32,8,128]{2,1,0:T(8,128)S(1)} %bitcast.19), channel_id=1, replica_groups=mesh['vox'=32,'row'=8] {'vox'}, dimensions={0} | all-to-all | bytes 262144 | tf_op jit(solution)/shard_map/all_to_all | solution.py:278
  62.0 0.6 shard_map.82
  62.6 11.3 %all_to_all.58 = f32[32,8,128]{2,1,0:T(8,128)S(1)} all-to-all(f32[32,8,128]{2,1,0:T(8,128)S(1)} %bitcast.20), channel_id=1, replica_groups=mesh['vox'=32,'row'=8] {'vox'}, dimensions={0} | all-to-all | bytes 262144 | tf_op jit(solution)/shard_map/all_to_all | solution.py:278
  73.9 1.0 shard_map.83.own_ref
  74.9 1.6 %collective-permute-start.7 = (f32[136,128]{1,0:T(8,128)S(1)}, f32[136,128]{1,0:T(8,128)S(1)}, u32[]{:S(2)}, u32[]{:S(2)}) collective-permute-start(f32[136,128]{1,0:T(8,128)S(1)} %shard_map.83.own_ref), channel_id=1, source_target_pairs={{0,3},{1,2},{2,1},{3,0},{4,7},{5,6},{6,5},{7,4},{8,11},{9,10},{10,... | collective-permute-start | bytes 208904 | tf_op jit(solution)/shard_map/ppermute | solution.py:281
  76.5 0.7 collective-permute-start.6
  77.3 1.2 collective-permute-start.5
  78.5 4.0 %collective-permute-done.7.three_ref = f32[136,128]{1,0:T(8,128)S(1)} collective-permute-done((f32[136,128]{1,0:T(8,128)S(1)}, f32[136,128]{1,0:T(8,128)S(1)}, u32[]{:S(2)}, u32[]{:S(2)}) %collective-permute-start.7) | collective-permute-done | bytes 69664 | tf_op jit(solution)/shard_map/ppermute | solution.py:281
  82.5 0.0 collective-permute-done.6.two_ref
  82.5 0.0 collective-permute-done.5.one_ref
  82.5 0.4 shard_map.84.near_ref
  82.9 5.2 %collective-permute-start.8 = (f32[264,128]{1,0:T(8,128)S(1)}, f32[264,128]{1,0:T(8,128)S(1)}, u32[]{:S(2)}, u32[]{:S(2)}) collective-permute-start(f32[264,128]{1,0:T(8,128)S(1)} %shard_map.84.near_ref), channel_id=1, source_target_pairs={{0,6},{1,7},{2,4},{3,5},{4,2},{5,3},{6,0},{7,1},{8,14},{9,15},{10,... | collective-permute-start | bytes 405512 | tf_op jit(solution)/shard_map/ppermute | solution.py:281
  88.0 6.5 %collective-permute-done.8.far_ref = f32[264,128]{1,0:T(8,128)S(1)} collective-permute-done((f32[264,128]{1,0:T(8,128)S(1)}, f32[264,128]{1,0:T(8,128)S(1)}, u32[]{:S(2)}, u32[]{:S(2)}) %collective-permute-start.8) | collective-permute-done | bytes 135200 | tf_op jit(solution)/shard_map/ppermute | solution.py:281
  94.5 1.4 %shard_map.85 = (f32[256,128]{1,0:T(8,128)S(1)}, f32[256,128]{1,0:T(8,128)S(1)}, f32[8,128]{1,0:T(8,128)S(1)}) custom-call(f32[264,128]{1,0:T(8,128)S(1)} %shard_map.84.near_ref, f32[264,128]{1,0:T(8,128)S(1)} %collective-permute-done.8.far_ref, f32[128,128,128]{2,1,0:T(8,128)S(1)} %shard_map.80.tiles_ref, s32[1,128]{1,0:T(1,128)S(1)} %get-tuple-element.34.row_ref, ...), custom_call_target="tpu_custom_call" | custom-call | tf_op jit(solution)/shard_map/pallas_call | solution.py:255
  96.0 11.1 %all_to_all.59 = f32[32,8,128]{2,1,0:T(8,128)S(1)} all-to-all(f32[32,8,128]{2,1,0:T(8,128)S(1)} %bitcast.18), channel_id=1, replica_groups=mesh['vox'=32,'row'=8] {'vox'}, dimensions={0} | all-to-all | bytes 262144 | tf_op jit(solution)/shard_map/all_to_all | solution.py:278
  107.1 0.6 shard_map.86
  107.7 11.3 %all_to_all.60 = f32[32,8,128]{2,1,0:T(8,128)S(1)} all-to-all(f32[32,8,128]{2,1,0:T(8,128)S(1)} %bitcast.21), channel_id=1, replica_groups=mesh['vox'=32,'row'=8] {'vox'}, dimensions={0} | all-to-all | bytes 262144 | tf_op jit(solution)/shard_map/all_to_all | solution.py:278
  119.0 1.0 shard_map.87.own_ref
  120.0 1.1 collective-permute-start.11
  121.1 2.4 %collective-permute-start.9 = (f32[136,128]{1,0:T(8,128)S(1)}, f32[136,128]{1,0:T(8,128)S(1)}, u32[]{:S(2)}, u32[]{:S(2)}) collective-permute-start(f32[136,128]{1,0:T(8,128)S(1)} %shard_map.87.own_ref), channel_id=1, source_target_pairs={{0,1},{1,0},{2,3},{3,2},{4,5},{5,4},{6,7},{7,6},{8,9},{9,8},{10,11... | collective-permute-start | bytes 208904 | tf_op jit(solution)/shard_map/ppermute | solution.py:281
  123.6 2.5 %collective-permute-done.11.three_ref = f32[136,128]{1,0:T(8,128)S(1)} collective-permute-done((f32[136,128]{1,0:T(8,128)S(1)}, f32[136,128]{1,0:T(8,128)S(1)}, u32[]{:S(2)}, u32[]{:S(2)}) %collective-permute-start.11) | collective-permute-done | bytes 69664 | tf_op jit(solution)/shard_map/ppermute | solution.py:281
  126.1 0.6 collective-permute-done.10.two_ref
  126.7 0.3 collective-permute-done.9.one_ref
  127.0 0.4 shard_map.88.near_ref
  127.3 4.3 %collective-permute-start.12 = (f32[264,128]{1,0:T(8,128)S(1)}, f32[264,128]{1,0:T(8,128)S(1)}, u32[]{:S(2)}, u32[]{:S(2)}) collective-permute-start(f32[264,128]{1,0:T(8,128)S(1)} %shard_map.88.near_ref), channel_id=1, source_target_pairs={{0,6},{1,7},{2,4},{3,5},{4,2},{5,3},{6,0},{7,1},{8,14},{9,15},{10,... | collective-permute-start | bytes 405512 | tf_op jit(solution)/shard_map/ppermute | solution.py:281
  131.6 6.3 %collective-permute-done.12.far_ref = f32[264,128]{1,0:T(8,128)S(1)} collective-permute-done((f32[264,128]{1,0:T(8,128)S(1)}, f32[264,128]{1,0:T(8,128)S(1)}, u32[]{:S(2)}, u32[]{:S(2)}) %collective-permute-start.12) | collective-permute-done | bytes 135200 | tf_op jit(solution)/shard_map/ppermute | solution.py:281
  137.9 0.8 shard_map.89
  (7 shorter events, 0.0 us)
Async XLA Ops:
  20.8 1.9 %collective-permute-start = (f32[1024,128]{1,0:T(8,128)S(1)}, f32[1024,128]{1,0:T(8,128)S(1)}, u32[]{:S(2)}, u32[]{:S(2)}) collective-permute-start(f32[1024,128]{1,0:T(8,128)S(1)} %bitcast.12), channel_id=1, source_target_pairs={{0,8},{8,0},{16,24},{24,16},{32,40},{40,32},{48,56},{56,48},{64,72... | collective-permute-start | bytes 1572872 | tf_op jit(solution)/shard_map/ppermute | solution.py:302
  20.8 0.7 copy-start.3
  21.5 0.7 copy-start.4
  22.7 0.7 copy-start.1
  28.5 7.5 %collective-permute-start.3 = (f32[136,128]{1,0:T(8,128)S(1)}, f32[136,128]{1,0:T(8,128)S(1)}, u32[]{:S(2)}, u32[]{:S(2)}) collective-permute-start(f32[136,128]{1,0:T(8,128)S(1)} %get-tuple-element.30.own_ref), channel_id=1, source_target_pairs={{0,3},{1,2},{2,1},{3,0},{4,7},{5,6},{6,5},{7,4},{8,11},{9,10},{10,... | collective-permute-start | bytes 208904 | tf_op jit(solution)/shard_map/ppermute | solution.py:281
  30.5 6.1 %collective-permute-start.2 = (f32[136,128]{1,0:T(8,128)S(1)}, f32[136,128]{1,0:T(8,128)S(1)}, u32[]{:S(2)}, u32[]{:S(2)}) collective-permute-start(f32[136,128]{1,0:T(8,128)S(1)} %get-tuple-element.30.own_ref), channel_id=1, source_target_pairs={{0,2},{1,3},{2,0},{3,1},{4,6},{5,7},{6,4},{7,5},{8,10},{9,11},{10,... | collective-permute-start | bytes 208904 | tf_op jit(solution)/shard_map/ppermute | solution.py:281
  32.0 6.6 %collective-permute-start.1 = (f32[136,128]{1,0:T(8,128)S(1)}, f32[136,128]{1,0:T(8,128)S(1)}, u32[]{:S(2)}, u32[]{:S(2)}) collective-permute-start(f32[136,128]{1,0:T(8,128)S(1)} %get-tuple-element.30.own_ref), channel_id=1, source_target_pairs={{0,1},{1,0},{2,3},{3,2},{4,5},{5,4},{6,7},{7,6},{8,9},{9,8},{10,11... | collective-permute-start | bytes 208904 | tf_op jit(solution)/shard_map/ppermute | solution.py:281
  39.0 10.2 %copy-start.2 = (s32[128]{0:T(128)S(1)}, s32[128]{0:T(128)}, u32[]{:S(2)}) copy-start(s32[128]{0:T(128)} %param.6) | copy-start | bytes 1540
  39.0 10.2 %collective-permute-start.4 = (f32[264,128]{1,0:T(8,128)S(1)}, f32[264,128]{1,0:T(8,128)S(1)}, u32[]{:S(2)}, u32[]{:S(2)}) collective-permute-start(f32[264,128]{1,0:T(8,128)S(1)} %shard_map.79.near_ref), channel_id=1, source_target_pairs={{0,6},{1,7},{2,4},{3,5},{4,2},{5,3},{6,0},{7,1},{8,14},{9,15},{10,... | collective-permute-start | bytes 405512 | tf_op jit(solution)/shard_map/ppermute | solution.py:281
  74.9 7.6 %collective-permute-start.7 = (f32[136,128]{1,0:T(8,128)S(1)}, f32[136,128]{1,0:T(8,128)S(1)}, u32[]{:S(2)}, u32[]{:S(2)}) collective-permute-start(f32[136,128]{1,0:T(8,128)S(1)} %shard_map.83.own_ref), channel_id=1, source_target_pairs={{0,3},{1,2},{2,1},{3,0},{4,7},{5,6},{6,5},{7,4},{8,11},{9,10},{10,... | collective-permute-start | bytes 208904 | tf_op jit(solution)/shard_map/ppermute | solution.py:281
  76.5 6.0 %collective-permute-start.6 = (f32[136,128]{1,0:T(8,128)S(1)}, f32[136,128]{1,0:T(8,128)S(1)}, u32[]{:S(2)}, u32[]{:S(2)}) collective-permute-start(f32[136,128]{1,0:T(8,128)S(1)} %shard_map.83.own_ref), channel_id=1, source_target_pairs={{0,2},{1,3},{2,0},{3,1},{4,6},{5,7},{6,4},{7,5},{8,10},{9,11},{10,... | collective-permute-start | bytes 208904 | tf_op jit(solution)/shard_map/ppermute | solution.py:281
  77.3 5.2 %collective-permute-start.5 = (f32[136,128]{1,0:T(8,128)S(1)}, f32[136,128]{1,0:T(8,128)S(1)}, u32[]{:S(2)}, u32[]{:S(2)}) collective-permute-start(f32[136,128]{1,0:T(8,128)S(1)} %shard_map.83.own_ref), channel_id=1, source_target_pairs={{0,1},{1,0},{2,3},{3,2},{4,5},{5,4},{6,7},{7,6},{8,9},{9,8},{10,11... | collective-permute-start | bytes 208904 | tf_op jit(solution)/shard_map/ppermute | solution.py:281
  82.9 11.7 %collective-permute-start.8 = (f32[264,128]{1,0:T(8,128)S(1)}, f32[264,128]{1,0:T(8,128)S(1)}, u32[]{:S(2)}, u32[]{:S(2)}) collective-permute-start(f32[264,128]{1,0:T(8,128)S(1)} %shard_map.84.near_ref), channel_id=1, source_target_pairs={{0,6},{1,7},{2,4},{3,5},{4,2},{5,3},{6,0},{7,1},{8,14},{9,15},{10,... | collective-permute-start | bytes 405512 | tf_op jit(solution)/shard_map/ppermute | solution.py:281
  94.5 43.4 %copy-start = (f32[64,128]{1,0:T(8,128)S(1)}, f32[64,128]{1,0:T(8,128)}, u32[]{:S(2)}) copy-start(f32[64,128]{1,0:T(8,128)} %ray_ref.1) | copy-start | bytes 98308
  120.0 6.1 %collective-permute-start.11 = (f32[136,128]{1,0:T(8,128)S(1)}, f32[136,128]{1,0:T(8,128)S(1)}, u32[]{:S(2)}, u32[]{:S(2)}) collective-permute-start(f32[136,128]{1,0:T(8,128)S(1)} %shard_map.87.own_ref), channel_id=1, source_target_pairs={{0,3},{1,2},{2,1},{3,0},{4,7},{5,6},{6,5},{7,4},{8,11},{9,10},{10,... | collective-permute-start | bytes 208904 | tf_op jit(solution)/shard_map/ppermute | solution.py:281
  121.1 5.6 %collective-permute-start.10 = (f32[136,128]{1,0:T(8,128)S(1)}, f32[136,128]{1,0:T(8,128)S(1)}, u32[]{:S(2)}, u32[]{:S(2)}) collective-permute-start(f32[136,128]{1,0:T(8,128)S(1)} %shard_map.87.own_ref), channel_id=1, source_target_pairs={{0,2},{1,3},{2,0},{3,1},{4,6},{5,7},{6,4},{7,5},{8,10},{9,11},{10,... | collective-permute-start | bytes 208904 | tf_op jit(solution)/shard_map/ppermute | solution.py:281
  121.1 5.8 %collective-permute-start.9 = (f32[136,128]{1,0:T(8,128)S(1)}, f32[136,128]{1,0:T(8,128)S(1)}, u32[]{:S(2)}, u32[]{:S(2)}) collective-permute-start(f32[136,128]{1,0:T(8,128)S(1)} %shard_map.87.own_ref), channel_id=1, source_target_pairs={{0,1},{1,0},{2,3},{3,2},{4,5},{5,4},{6,7},{7,6},{8,9},{9,8},{10,11... | collective-permute-start | bytes 208904 | tf_op jit(solution)/shard_map/ppermute | solution.py:281
  127.3 10.6 %collective-permute-start.12 = (f32[264,128]{1,0:T(8,128)S(1)}, f32[264,128]{1,0:T(8,128)S(1)}, u32[]{:S(2)}, u32[]{:S(2)}) collective-permute-start(f32[264,128]{1,0:T(8,128)S(1)} %shard_map.88.near_ref), channel_id=1, source_target_pairs={{0,6},{1,7},{2,4},{3,5},{4,2},{5,3},{6,0},{7,1},{8,14},{9,15},{10,... | collective-permute-start | bytes 405512 | tf_op jit(solution)/shard_map/ppermute | solution.py:281

commit v3 on v2

v3 whole, which is shorter than its diff:
```python
import jax
import jax.numpy as jnp
from jax import lax
from jax.experimental import pallas as pl
from jax.experimental.pallas import tpu as pltpu
from jax.sharding import PartitionSpec as P

TILE = 128
VT_DEV = 256
CAP = 4
N_VOX = 32
N_ROW = 8
CORES = 2
CHIPS = N_VOX // CORES
CHUNKS = 8
PAD = 8
MAP = CAP
NORM = CAP + 1
NORM2 = CAP + 2
SENT = N_VOX * PAD
PART = TILE + 8
SUM = VT_DEV + 8
IDS, IMAGE, GAMMA, CROSS = 0, 1, 2, 3

F32 = jnp.float32
BF16 = jnp.bfloat16


def iota(shape, dim):
    return lax.broadcasted_iota(jnp.int32, shape, dim)


def select_rows(choice, values):
    high = values.astype(BF16)
    rest = values - high.astype(F32)
    middle = rest.astype(BF16)
    low = (rest - middle.astype(F32)).astype(BF16)
    total = jnp.dot(choice, low, preferred_element_type=F32)
    total = total + jnp.dot(choice, middle, preferred_element_type=F32)
    return total + jnp.dot(choice, high, preferred_element_type=F32)


def select_columns(values, choice):
    high = values.astype(BF16)
    rest = values - high.astype(F32)
    middle = rest.astype(BF16)
    low = (rest - middle.astype(F32)).astype(BF16)
    total = jnp.dot(low, choice, preferred_element_type=F32)
    total = total + jnp.dot(middle, choice, preferred_element_type=F32)
    return total + jnp.dot(high, choice, preferred_element_type=F32)


def one_hot(rows, index):
    return jnp.where(iota((rows, TILE), 0) == index, 1.0, 0.0).astype(BF16)


def copies_kernel(ray_ref, copies_ref):
    owned = ray_ref.shape[0]
    rays = ray_ref[...]
    for chip in range(CHIPS):
        copies_ref[chip * owned : (chip + 1) * owned, :] = rays


def pack_kernel(slot_ref, map_ref, vox_ref, pack_ref):
    pack_ref[...] = jnp.zeros_like(pack_ref)
    pack_ref[0:1, :] = slot_ref[...]
    pack_ref[1:2, :] = map_ref[...]
    pack_ref[2:3, :] = vox_ref[...]


def relay_kernel(natural_ref, tiles_ref):
    def step(index, unused):
        block = natural_ref[:, pl.ds(pl.multiple_of(index * 8, 8), 8), :]
        block = jnp.swapaxes(block, 0, 1)
        for inner in range(8):
            tiles_ref[index * 8 + inner] = jnp.transpose(block[inner])
        return unused

    lax.fori_loop(0, TILE // 8, step, 0)


def back_tiles(tiles_ref, weight_ref):
    def step(index, total):
        for inner in range(8):
            ray = index * 8 + inner
            total = total + tiles_ref[ray] * weight_ref[pl.ds(ray, 1), :]
        return total

    return lax.fori_loop(0, TILE // 8, step, jnp.zeros((TILE, TILE), F32))


def write_tail(part_ref, vox_row, image, gamma, cross):
    sub = iota((8, TILE), 0)
    tail = jnp.where(sub == IDS, jnp.broadcast_to(vox_row.astype(F32), (8, TILE)), 0.0)
    for place, row in ((IMAGE, image), (GAMMA, gamma), (CROSS, cross)):
        if row is not None:
            tail = tail + jnp.where(sub == place, jnp.broadcast_to(row, (8, TILE)), 0.0)
    part_ref[TILE:PART, :] = tail


def back_first_kernel(
    tiles_hbm, same_ref, other_ref, pack_ref,
    part_ref, share_ref, natural_ref, row_ref, vox_ref, extra_ref, ids_ref,
    picked_ref, index_ref, place_ref, sems,
):
    size = TILE // CHUNKS
    moves = []
    for chunk in range(CHUNKS):
        where = pl.ds(chunk * size, size)
        moves.append(pltpu.make_async_copy(tiles_hbm.at[where], natural_ref.at[where], sems.at[chunk]))
    for move in moves:
        move.start()

    owned = same_ref.shape[0] // CHIPS
    slot, vox = pack_ref[0:1, :], pack_ref[2:3, :]
    target, place = lax.shift_right_logical(slot, 2), slot & (CAP - 1)
    sub, lane = iota((TILE, TILE), 0), iota((TILE, TILE), 1)
    column = jnp.transpose(jnp.broadcast_to(pack_ref[1:2, :].astype(F32), (TILE, TILE)))
    block = jnp.sum(jnp.where(sub == slot, column, 0.0), axis=0, keepdims=True).astype(jnp.int32)
    mine = lax.axis_index("vox") & (CORES - 1)
    other = (target & (CORES - 1)) ^ mine
    index_ref[...] = (other * CHIPS + lax.shift_right_logical(target, 1)) * owned + block
    move = pltpu.make_async_copy(index_ref, place_ref, sems.at[CHUNKS])
    move.start()

    row_ref[...] = target * PAD + place
    vox_ref[...] = vox
    ids_ref[...] = jnp.broadcast_to(vox.astype(F32), (8, TILE))
    write_tail(part_ref, vox, None, None, None)
    values = jnp.where((sub & (CAP - 1)) == lane, column, 0.0).astype(BF16)
    sub, lane = iota((SENT, TILE), 0), iota((SENT, TILE), 1)
    hit = ((sub & (PAD - 1)) == MAP) & (lax.shift_right_logical(lane, 2) == lax.shift_right_logical(sub, 3))
    choice = jnp.where(hit, 1.0, 0.0).astype(BF16)
    extra_ref[...] = jnp.dot(choice, values, preferred_element_type=F32)

    move.wait()
    half = same_ref.shape[0]
    for tile in range(TILE):
        index = place_ref[0, tile]
        here = index < half
        row = jnp.where(here, index, index - half)
        picked_ref[tile : tile + 1, :] = jnp.where(here, same_ref[pl.ds(row, 1), :], other_ref[pl.ds(row, 1), :])
    weight = jnp.transpose(picked_ref[...])
    for group in range(TILE // 8):
        if group * 8 % size == 0:
            moves[group * 8 // size].wait()
        rows = []
        for tile in range(group * 8, group * 8 + 8):
            rows.append(jnp.sum(natural_ref[tile] * weight[:, tile : tile + 1], axis=0, keepdims=True))
        part_ref[group * 8 : group * 8 + 8, :] = jnp.concatenate(rows, axis=0)
    share_ref[...] = jnp.transpose(part_ref[0:TILE, :])


def back_share(received_ref, tiles_ref, row_ref, vox_ref, gamma_ref, part_ref, weight_ref):
    received = received_ref[...]
    weight_ref[...] = select_columns(jnp.transpose(received), one_hot(SENT, row_ref[...]))
    heads = jnp.sum(received.reshape(N_VOX, PAD, TILE), axis=0)
    share = back_tiles(tiles_ref, weight_ref)
    part_ref[0:TILE, :] = jnp.transpose(share)
    write_tail(part_ref, vox_ref[...], heads[NORM : NORM + 1, :], gamma_ref[0:1, :], heads[NORM2 : NORM2 + 1, :])
    return share


def back_kernel(received_ref, tiles_ref, row_ref, vox_ref, gamma_ref, part_ref, share_ref, weight_ref):
    share_ref[...] = back_share(received_ref, tiles_ref, row_ref, vox_ref, gamma_ref, part_ref, weight_ref)


def back_last_kernel(received_ref, tiles_ref, row_ref, vox_ref, gamma_ref, part_ref, weight_ref):
    back_share(received_ref, tiles_ref, row_ref, vox_ref, gamma_ref, part_ref, weight_ref)


def quad_sum(own_ref, one_ref, two_ref, three_ref):
    def spread(ref):
        where = ref[TILE + IDS : TILE + IDS + 1, :].astype(jnp.int32)
        return select_rows(one_hot(VT_DEV, where), ref[0:TILE, :])

    field = (spread(own_ref) + spread(one_ref)) + (spread(two_ref) + spread(three_ref))
    tail = slice(TILE, PART)
    return field, (own_ref[tail, :] + one_ref[tail, :]) + (two_ref[tail, :] + three_ref[tail, :])


def read_tiles(field, tail, own_ref, ids_ref, mine_ref, send_ref):
    here = one_hot(VT_DEV, own_ref[TILE + IDS : TILE + IDS + 1, :].astype(jnp.int32))
    there = one_hot(VT_DEV, ids_ref[0:1, :].astype(jnp.int32))
    both = select_columns(jnp.transpose(field), jnp.concatenate([here, there], axis=1))
    mine_ref[...] = both[:, 0:TILE]
    send_ref[0:TILE, :] = both[:, TILE : 2 * TILE]
    send_ref[TILE:PART, :] = tail


def quad_first_kernel(own_ref, one_ref, two_ref, three_ref, ids_ref, near_ref, mine_ref, send_ref):
    field, tail = quad_sum(own_ref, one_ref, two_ref, three_ref)
    read_tiles(field, tail, own_ref, ids_ref, mine_ref, send_ref)
    near_ref[...] = field


def quad_kernel(own_ref, one_ref, two_ref, three_ref, ids_ref, before_ref, near_ref, mine_ref, send_ref):
    field, tail = quad_sum(own_ref, one_ref, two_ref, three_ref)
    read_tiles(field, tail, own_ref, ids_ref, mine_ref, send_ref)
    near_ref[0:VT_DEV, :] = before_ref[...]
    near_ref[VT_DEV:, :] = field


def quad_last_kernel(own_ref, one_ref, two_ref, three_ref, near_ref):
    field, tail = quad_sum(own_ref, one_ref, two_ref, three_ref)
    near_ref[0:VT_DEV, :] = field
    near_ref[VT_DEV:SUM, :] = tail


def forward_tiles(values, share, tiles_ref, row_ref, extra_ref, payload_ref, sums_ref):
    def step(index, unused):
        for inner in range(8):
            ray = index * 8 + inner
            product = tiles_ref[ray] * values
            sums_ref[pl.ds(pl.multiple_of(ray * 8, 8), 8), :] = jnp.sum(product.reshape(TILE // 8, 8, TILE), axis=0)
        return unused

    lax.fori_loop(0, TILE // 8, step, 0)
    rays = sums_ref[pl.ds(0, TILE, stride=8), :]
    for inner in range(1, 8):
        rays = rays + sums_ref[pl.ds(inner, TILE, stride=8), :]
    gamma = jnp.sum(values * share, axis=0, keepdims=True)
    head = jnp.where((iota((SENT, TILE), 0) & (PAD - 1)) == NORM, gamma, extra_ref[...])
    payload_ref[...] = select_rows(one_hot(SENT, row_ref[...]), jnp.transpose(rays)) + head


def forward_first_kernel(mine_ref, far_ref, share_ref, tiles_ref, row_ref, extra_ref, payload_ref, values_ref, sums_ref):
    values = mine_ref[...] + far_ref[0:TILE, :]
    values_ref[...] = values
    forward_tiles(values, share_ref[...], tiles_ref, row_ref, extra_ref, payload_ref, sums_ref)


def lane_sum(tail, place):
    return jnp.sum(tail[place : place + 1, :], axis=1, keepdims=True)


def forward_kernel(
    mine_ref, send_ref, far_ref, share_ref, values0_ref, share0_ref, tiles_ref, row_ref, extra_ref,
    payload_ref, scalars_ref, sums_ref,
):
    tail = send_ref[TILE:PART, :] + far_ref[TILE:PART, :]
    gamma, square = lane_sum(tail, GAMMA), lane_sum(tail, IMAGE)
    step = gamma / square
    sub = iota((8, TILE), 0)
    scalars_ref[...] = jnp.where(sub == 0, gamma, jnp.where(sub == 1, square, step))
    values = values0_ref[...] - step * (mine_ref[...] + far_ref[0:TILE, :])
    share = share0_ref[...] - step * share_ref[...]
    forward_tiles(values, share, tiles_ref, row_ref, extra_ref, payload_ref, sums_ref)


def owner_parts(received_ref):
    received = received_ref[...]
    blocks = received.reshape(N_VOX, PAD, TILE)
    head = jnp.broadcast_to(blocks[:, MAP : MAP + 1, :], (N_VOX, PAD, TILE)).reshape(SENT, TILE)
    place, lane = iota((SENT, TILE), 0) & (PAD - 1), iota((SENT, TILE), 1)
    column = jnp.sum(jnp.where((lane == place) & (place < CAP), head, 0.0), axis=1, keepdims=True)
    hit = (column.astype(jnp.int32) == lane) & (place < CAP)
    choice = jnp.where(hit, 1.0, 0.0)
    image = select_rows(jnp.transpose(choice).astype(BF16), received)
    gamma = jnp.sum(blocks, axis=0)[NORM : NORM + 1, :]
    return choice.astype(BF16), image, jnp.broadcast_to(gamma, (8, TILE))


def owner_first_kernel(received_ref, payload_ref, image_ref, gamma_ref):
    choice, image, gamma_ref[...] = owner_parts(received_ref)
    owned = image_ref.shape[0]
    lower = image[0:owned, :]
    image_ref[...] = lower
    square = jnp.sum(lower * lower, axis=0, keepdims=True)
    place = iota((SENT, TILE), 0) & (PAD - 1)
    payload_ref[...] = select_rows(choice, image) + jnp.where(place == NORM, square, 0.0)


def owner_kernel(received_ref, image0_ref, payload_ref, image_ref, gamma_ref):
    choice, image, gamma_ref[...] = owner_parts(received_ref)
    owned = image_ref.shape[0]
    lower = image[0:owned, :]
    image_ref[...] = lower
    square = jnp.sum(lower * lower, axis=0, keepdims=True)
    cross = jnp.sum(lower * image0_ref[...], axis=0, keepdims=True)
    place = iota((SENT, TILE), 0) & (PAD - 1)
    head = jnp.where(place == NORM, square, jnp.where(place == NORM2, cross, 0.0))
    payload_ref[...] = select_rows(choice, image) + head


def last_kernel(
    near_ref, far_ref, inner_near_ref, inner_far_ref, scalars_ref, image0_ref, image1_ref, ray_ref,
    solution_ref, residual_ref, normal_ref,
):
    tail = near_ref[VT_DEV:SUM, :] + far_ref[VT_DEV:SUM, :]
    gamma0, square0, step0 = scalars_ref[0:1, :], scalars_ref[1:2, :], scalars_ref[2:3, :]
    gamma1 = lane_sum(tail, GAMMA)
    ratio = gamma1 / gamma0
    square1 = lane_sum(tail, IMAGE) + 2.0 * ratio * lane_sum(tail, CROSS) + ratio * ratio * square0
    step1 = gamma1 / square1
    normal0 = inner_near_ref[0:VT_DEV, :] + inner_far_ref[0:VT_DEV, :]
    change0 = inner_near_ref[VT_DEV:, :] + inner_far_ref[VT_DEV:, :]
    normal1 = normal0 - step0 * change0
    change1 = near_ref[0:VT_DEV, :] + far_ref[0:VT_DEV, :] + ratio * change0
    solution_ref[...] = step0 * normal0 + step1 * (normal1 + ratio * normal0)
    normal_ref[...] = normal1 - step1 * change1
    image0 = image0_ref[...]
    residual_ref[...] = ray_ref[...] - step0 * image0 - step1 * (image1_ref[...] + ratio * image0)


def call(kernel, outs, scratch, args, hbm=0, cost=None, limit=24):
    vmem = pl.BlockSpec(memory_space=pltpu.VMEM)
    specs = [pl.BlockSpec(memory_space=pl.ANY)] * hbm
    outs = [out if isinstance(out, jax.ShapeDtypeStruct) else jax.ShapeDtypeStruct(out, F32) for out in outs]
    return pl.pallas_call(
        kernel,
        out_shape=outs,
        in_specs=specs + [vmem] * (len(args) - hbm),
        out_specs=[vmem] * len(outs),
        scratch_shapes=[pltpu.VMEM(shape, F32) if isinstance(shape, tuple) else shape for shape in scratch],
        cost_estimate=cost,
        compiler_params=pltpu.CompilerParams(vmem_limit_bytes=limit * 1024 * 1024),
    )(*args)


def local(tile_values, tile_vox, tile_slot, slot_block, ray_data):
    owned = ray_data.shape[0]
    block = (TILE, TILE)
    sent = (SENT, TILE)
    field = (VT_DEV, TILE)
    scalar = (8, TILE)
    part = (PART, TILE)
    sums = (TILE * 8, TILE)
    rays = (owned, TILE)
    indices = jax.ShapeDtypeStruct((1, TILE), jnp.int32)

    def over_vox(array):
        return lax.all_to_all(array, "vox", 0, 0, tiled=True)

    def across(array, distance):
        return lax.ppermute(array, "row", [(index, index ^ distance) for index in range(N_ROW)])

    def quad(own):
        return (own, *(across(own, distance) for distance in (1, 2, 3)))

    (copies,) = call(copies_kernel, [(CHIPS * owned, TILE)], [], (ray_data,))
    chips = [[chip * CORES + core for chip in range(CHIPS)] for core in range(CORES)]
    same = lax.all_to_all(copies, "vox", 0, 0, tiled=True, axis_index_groups=chips)
    same, tile_vox, tile_slot, slot_block = lax.optimization_barrier((same, tile_vox, tile_slot, slot_block))
    other = lax.ppermute(same, "vox", [(device, device ^ 1) for device in range(N_VOX)])
    (pack,) = call(
        pack_kernel,
        [jax.ShapeDtypeStruct(scalar, jnp.int32)],
        [],
        (tile_slot.reshape(1, TILE), slot_block, tile_vox.reshape(1, TILE)),
    )
    own, share0, natural, slot_row, vox_row, extra, ids = call(
        back_first_kernel,
        [part, block, (TILE, TILE, TILE), indices, indices, sent, scalar],
        [
            block,
            pltpu.VMEM((1, TILE), jnp.int32),
            pltpu.SMEM((1, TILE), jnp.int32),
            pltpu.SemaphoreType.DMA((CHUNKS + 1,)),
        ],
        (tile_values, same, other, pack),
        hbm=1,
        limit=42,
    )
    ids = across(ids, 6)
    near, mine, send = call(quad_first_kernel, [field, block, part], [], (*quad(own), ids))
    send, natural = lax.optimization_barrier((send, natural))
    far = across(send, 6)
    (tiles,) = call(
        relay_kernel,
        [(TILE, TILE, TILE)],
        [],
        (natural,),
        cost=pl.CostEstimate(flops=0, bytes_accessed=2**24, transcendentals=0),
    )
    payload, values0 = call(
        forward_first_kernel, [sent, block], [sums], (mine, far, share0, tiles, slot_row, extra)
    )
    payload, image0, gamma = call(owner_first_kernel, [sent, rays, scalar], [], (over_vox(payload),))
    own, share = call(back_kernel, [part, block], [block], (over_vox(payload), tiles, slot_row, vox_row, gamma))
    near, mine, send = call(
        quad_kernel, [(2 * VT_DEV, TILE), block, part], [], (*quad(own), ids, near)
    )
    far, near = lax.optimization_barrier((across(send, 6), near))
    inner_far = across(near, 6)
    payload, scalars = call(
        forward_kernel,
        [sent, scalar],
        [sums],
        (mine, send, far, share, values0, share0, tiles, slot_row, extra),
    )
    received, inner_far = lax.optimization_barrier((over_vox(payload), inner_far))
    payload, image1, gamma = call(owner_kernel, [sent, rays, scalar], [], (received, image0))
    (own,) = call(back_last_kernel, [part], [block], (over_vox(payload), tiles, slot_row, vox_row, gamma))
    (last,) = call(quad_last_kernel, [(SUM, TILE)], [], quad(own))
    return tuple(
        call(
            last_kernel,
            [field, rays, field],
            [],
            (last, across(last, 6), near, inner_far, scalars, image0, image1, ray_data),
        )
    )


def solution(mesh):
    return jax.shard_map(
        local,
        mesh=mesh,
        in_specs=(
            P(("vox", "row"), None, None),
            P(("vox", "row")),
            P(("vox", "row")),
            P(("vox", "row"), None),
            P(("vox", "row"), None),
        ),
        out_specs=(P("vox", None), P(("vox", "row"), None), P("vox", None)),
        check_vma=False,
    )
```

time: 139 us -> 136 us (0.978)
  waiting for transfers between devices: 27 us -> 20.9 us
  starting transfers between devices: 26.2 us -> 31.4 us
  Pallas kernels: 19.1 us -> 16.7 us
    ppermute x12 -> x14, waiting for transfers between devices: 26.7 us -> 20.9 us  [across(): lax.ppermute(array, 'row', [(index, index ^ distance) for index in range(...]
    ppermute x12 -> x14, starting transfers between devices: 26.2 us -> 31.4 us  [across(): lax.ppermute(array, 'row', [(index, index ^ distance) for index in range(...]
    pallas_call x14, Pallas kernels: 19.1 us -> 16.7 us  [call(): pl.pallas_call(kernel, out_shape=outs, in_specs=specs + [vmem] * (len(arg...]
  transfers between devices with their start and end apart: 13 -> 15, of which waited for: 11 -> 5; matrix products, arithmetic and copies ran while one was open for 0% -> 0% of each run, Pallas kernels for 3% -> 4%
where the time goes in v3:
time: 136 us
  blocking collectives  63.4 us (47%)
  starting transfers between devices  31.4 us (23%)
  waiting for transfers between devices  20.9 us (15%)
  Pallas kernels  16.7 us (12%)
  local copies, waits for them, and re-layouts  2.72 us (2%)
    all_to_all x4, blocking collectives, over_vox(): return lax.all_to_all(array, 'vox', 0, 0, tiled=True)  45.1 us
    ppermute x14, starting transfers between devices, across(): lax.ppermute(array, 'row', [(index, index ^ distance) for index in range(...  31.4 us
    ppermute x14, waiting for transfers between devices, across(): lax.ppermute(array, 'row', [(index, index ^ distance) for index in range(...  20.9 us
    all_to_all x1, blocking collectives, local(): lax.all_to_all(copies, 'vox', 0, 0, tiled=True, axis_index_groups=chips)  18.3 us
    pallas_call x14, Pallas kernels, call(): pl.pallas_call(kernel, out_shape=outs, in_specs=specs + [vmem] * (len(arg...  16.7 us
    unnamed x10, local copies, waits for them, and re-layouts  2.72 us
  transfers between devices with their start and end apart: 15, of which 5 were waited for; matrix products, arithmetic and copies ran while one was open for 0% of the time, Pallas kernels for 4%

profile of v3, /device:TPU:32, one launch (start us, length us, event | category | flops | bytes accessed | tf_op | source)
XLA Modules:
  0.0 135.9 jit_solution(15031318468051157298)
XLA Ops:
  0.6 0.0 copy-start
  0.6 0.7 copy-done
  1.4 18.3 %all_to_all.57 = f32[16,64,128]{2,1,0:T(8,128)S(1)} all-to-all(f32[16,64,128]{2,1,0:T(8,128)S(1)} %bitcast.14), channel_id=1, replica_groups={{0,16,32,48,64,80,96,112,128,144,160,176,192,208,224,240},{8,24,40,56,7..., dimensions={0} | all-to-all | bytes 1048576 | tf_op jit(solution)/shard_map/all_to_all | solution.py:343
  19.8 0.0 collective-permute-start
  19.8 0.7 copy-done.2
  20.4 0.7 copy-done.3
  21.1 0.7 copy-done.4
  21.7 4.4 %shard_map.78 = (f32[136,128]{1,0:T(8,128)S(1)}, f32[128,128]{1,0:T(8,128)S(1)}, f32[128,128,128]{2,1,0:T(8,128)S(1)}, s32[1,128]{1,0:T(1,128)S(1)}, s32[1,128]{...) custom-call(f32[128,128,128]{2,1,0:T(8,128)} %tiles_hbm.1, f32[1024,128]{1,0:T(8,128)S(1)} %bitcast.13, ...), custom_call_target="tpu_custom_call" | custom-call | tf_op jit(solution)/shard_map/pallas_call | solution.py:310
  26.2 2.0 %collective-permute-start.3 = (f32[136,128]{1,0:T(8,128)S(1)}, f32[136,128]{1,0:T(8,128)S(1)}, u32[]{:S(2)}, u32[]{:S(2)}) collective-permute-start(f32[136,128]{1,0:T(8,128)S(1)} %get-tuple-element.42.own_ref), channel_id=1, source_target_pairs={{0,3},{1,2},{2,1},{3,0},{4,7},{5,6},{6,5},{7,4},{8,11},{9,10},{10,... | collective-permute-start | bytes 208904 | tf_op jit(solution)/shard_map/ppermute | solution.py:336
  28.2 1.5 %collective-permute-start.2 = (f32[136,128]{1,0:T(8,128)S(1)}, f32[136,128]{1,0:T(8,128)S(1)}, u32[]{:S(2)}, u32[]{:S(2)}) collective-permute-start(f32[136,128]{1,0:T(8,128)S(1)} %get-tuple-element.42.own_ref), channel_id=1, source_target_pairs={{0,2},{1,3},{2,0},{3,1},{4,6},{5,7},{6,4},{7,5},{8,10},{9,11},{10,... | collective-permute-start | bytes 208904 | tf_op jit(solution)/shard_map/ppermute | solution.py:336
  29.7 1.4 %collective-permute-start.1 = (f32[136,128]{1,0:T(8,128)S(1)}, f32[136,128]{1,0:T(8,128)S(1)}, u32[]{:S(2)}, u32[]{:S(2)}) collective-permute-start(f32[136,128]{1,0:T(8,128)S(1)} %get-tuple-element.42.own_ref), channel_id=1, source_target_pairs={{0,1},{1,0},{2,3},{3,2},{4,5},{5,4},{6,7},{7,6},{8,9},{9,8},{10,11... | collective-permute-start | bytes 208904 | tf_op jit(solution)/shard_map/ppermute | solution.py:336
  31.0 5.1 %collective-permute-start.4 = (f32[8,128]{1,0:T(8,128)S(1)}, f32[8,128]{1,0:T(8,128)S(1)}, u32[]{:S(2)}, u32[]{:S(2)}) collective-permute-start(f32[8,128]{1,0:T(8,128)S(1)} %get-tuple-element.43), channel_id=1, source_target_pairs={{0,6},{1,7},{2,4},{3,5},{4,2},{5,3},{6,0},{7,1},{8,14},{9,15},{10,... | collective-permute-start | bytes 12296 | tf_op jit(solution)/shard_map/ppermute | solution.py:336
  36.1 1.6 %collective-permute-done.4.ids_ref = f32[8,128]{1,0:T(8,128)S(1)} collective-permute-done((f32[8,128]{1,0:T(8,128)S(1)}, f32[8,128]{1,0:T(8,128)S(1)}, u32[]{:S(2)}, u32[]{:S(2)}) %collective-permute-start.4) | collective-permute-done | bytes 4128 | tf_op jit(solution)/shard_map/ppermute | solution.py:336
  37.7 0.0 collective-permute-done.2.two_ref
  37.7 0.0 collective-permute-done.1.one_ref
  37.7 0.7 shard_map.79
  38.4 4.2 %collective-permute-start.5 = (f32[136,128]{1,0:T(8,128)S(1)}, f32[136,128]{1,0:T(8,128)S(1)}, u32[]{:S(2)}, u32[]{:S(2)}) collective-permute-start(f32[136,128]{1,0:T(8,128)S(1)} %get-tuple-element.47), channel_id=1, source_target_pairs={{0,6},{1,7},{2,4},{3,5},{4,2},{5,3},{6,0},{7,1},{8,14},{9,15},{10,... | collective-permute-start | bytes 208904 | tf_op jit(solution)/shard_map/ppermute | solution.py:336
  42.6 4.2 %shard_map.80.tiles_ref = f32[128,128,128]{2,1,0:T(8,128)S(1)} custom-call(f32[128,128,128]{2,1,0:T(8,128)S(1)} %get-tuple-element.49.natural_ref), custom_call_target="tpu_custom_call" | custom-call | bytes 16777216 | tf_op jit(solution)/shard_map/pallas_call | solution.py:310
  46.8 0.0 collective-permute-done.5.far_ref
  46.8 1.1 shard_map.81
  47.9 11.4 %all_to_all.58 = f32[32,8,128]{2,1,0:T(8,128)S(1)} all-to-all(f32[32,8,128]{2,1,0:T(8,128)S(1)} %bitcast.20), channel_id=1, replica_groups=mesh['vox'=32,'row'=8] {'vox'}, dimensions={0} | all-to-all | bytes 262144 | tf_op jit(solution)/shard_map/all_to_all | solution.py:333
  59.4 0.6 shard_map.82
  60.0 11.3 %all_to_all.59 = f32[32,8,128]{2,1,0:T(8,128)S(1)} all-to-all(f32[32,8,128]{2,1,0:T(8,128)S(1)} %bitcast.21), channel_id=1, replica_groups=mesh['vox'=32,'row'=8] {'vox'}, dimensions={0} | all-to-all | bytes 262144 | tf_op jit(solution)/shard_map/all_to_all | solution.py:333
  71.2 1.0 shard_map.83
  72.2 1.1 collective-permute-start.8
  73.3 1.8 %collective-permute-start.7 = (f32[136,128]{1,0:T(8,128)S(1)}, f32[136,128]{1,0:T(8,128)S(1)}, u32[]{:S(2)}, u32[]{:S(2)}) collective-permute-start(f32[136,128]{1,0:T(8,128)S(1)} %get-tuple-element.56.own_ref), channel_id=1, source_target_pairs={{0,2},{1,3},{2,0},{3,1},{4,6},{5,7},{6,4},{7,5},{8,10},{9,11},{10,... | collective-permute-start | bytes 208904 | tf_op jit(solution)/shard_map/ppermute | solution.py:336
  75.1 0.7 collective-permute-start.6
  75.8 4.4 %collective-permute-done.8.three_ref = f32[136,128]{1,0:T(8,128)S(1)} collective-permute-done((f32[136,128]{1,0:T(8,128)S(1)}, f32[136,128]{1,0:T(8,128)S(1)}, u32[]{:S(2)}, u32[]{:S(2)}) %collective-permute-start.8) | collective-permute-done | bytes 69664 | tf_op jit(solution)/shard_map/ppermute | solution.py:336
  80.2 0.0 collective-permute-done.7.two_ref
  80.2 0.0 collective-permute-done.6.one_ref
  80.2 0.7 shard_map.84
  80.9 4.1 %collective-permute-start.9 = (f32[136,128]{1,0:T(8,128)S(1)}, f32[136,128]{1,0:T(8,128)S(1)}, u32[]{:S(2)}, u32[]{:S(2)}) collective-permute-start(f32[136,128]{1,0:T(8,128)S(1)} %get-tuple-element.59.send_ref), channel_id=1, source_target_pairs={{0,6},{1,7},{2,4},{3,5},{4,2},{5,3},{6,0},{7,1},{8,14},{9,15},{10,... | collective-permute-start | bytes 208904 | tf_op jit(solution)/shard_map/ppermute | solution.py:336
  85.0 3.2 %collective-permute-done.9.far_ref = f32[136,128]{1,0:T(8,128)S(1)} collective-permute-done((f32[136,128]{1,0:T(8,128)S(1)}, f32[136,128]{1,0:T(8,128)S(1)}, u32[]{:S(2)}, u32[]{:S(2)}) %collective-permute-start.9) | collective-permute-done | bytes 69664 | tf_op jit(solution)/shard_map/ppermute | solution.py:336
  88.2 3.2 %collective-permute-start.10 = (f32[512,128]{1,0:T(8,128)S(1)}, f32[512,128]{1,0:T(8,128)S(1)}, u32[]{:S(2)}, u32[]{:S(2)}) collective-permute-start(f32[512,128]{1,0:T(8,128)S(1)} %get-tuple-element.65.inner_near_ref), channel_id=1, source_target_pairs={{0,6},{1,7},{2,4},{3,5},{4,2},{5,3},{6,0},{7,1},{8,14},{9,15},{10,... | collective-permute-start | bytes 786440 | tf_op jit(solution)/shard_map/ppermute | solution.py:336
  91.4 1.2 shard_map.85
  92.6 11.1 %all_to_all.60 = f32[32,8,128]{2,1,0:T(8,128)S(1)} all-to-all(f32[32,8,128]{2,1,0:T(8,128)S(1)} %bitcast.19), channel_id=1, replica_groups=mesh['vox'=32,'row'=8] {'vox'}, dimensions={0} | all-to-all | bytes 262144 | tf_op jit(solution)/shard_map/all_to_all | solution.py:333
  103.8 0.6 shard_map.86
  104.4 11.3 %all_to_all.61 = f32[32,8,128]{2,1,0:T(8,128)S(1)} all-to-all(f32[32,8,128]{2,1,0:T(8,128)S(1)} %bitcast.22), channel_id=1, replica_groups=mesh['vox'=32,'row'=8] {'vox'}, dimensions={0} | all-to-all | bytes 262144 | tf_op jit(solution)/shard_map/all_to_all | solution.py:333
  115.6 1.0 shard_map.87.own_ref
  116.7 1.1 collective-permute-start.13
  117.7 1.8 %collective-permute-start.12 = (f32[136,128]{1,0:T(8,128)S(1)}, f32[136,128]{1,0:T(8,128)S(1)}, u32[]{:S(2)}, u32[]{:S(2)}) collective-permute-start(f32[136,128]{1,0:T(8,128)S(1)} %shard_map.87.own_ref), channel_id=1, source_target_pairs={{0,2},{1,3},{2,0},{3,1},{4,6},{5,7},{6,4},{7,5},{8,10},{9,11},{10,... | collective-permute-start | bytes 208904 | tf_op jit(solution)/shard_map/ppermute | solution.py:336
  119.6 0.7 collective-permute-start.11
  120.2 4.4 %collective-permute-done.13.three_ref = f32[136,128]{1,0:T(8,128)S(1)} collective-permute-done((f32[136,128]{1,0:T(8,128)S(1)}, f32[136,128]{1,0:T(8,128)S(1)}, u32[]{:S(2)}, u32[]{:S(2)}) %collective-permute-start.13) | collective-permute-done | bytes 69664 | tf_op jit(solution)/shard_map/ppermute | solution.py:336
  124.6 0.0 collective-permute-done.12.two_ref
  124.7 0.4 shard_map.88.near_ref
  125.0 2.8 %collective-permute-start.14 = (f32[264,128]{1,0:T(8,128)S(1)}, f32[264,128]{1,0:T(8,128)S(1)}, u32[]{:S(2)}, u32[]{:S(2)}) collective-permute-start(f32[264,128]{1,0:T(8,128)S(1)} %shard_map.88.near_ref), channel_id=1, source_target_pairs={{0,6},{1,7},{2,4},{3,5},{4,2},{5,3},{6,0},{7,1},{8,14},{9,15},{10,... | collective-permute-start | bytes 405512 | tf_op jit(solution)/shard_map/ppermute | solution.py:336
  127.8 7.3 %collective-permute-done.14.far_ref = f32[264,128]{1,0:T(8,128)S(1)} collective-permute-done((f32[264,128]{1,0:T(8,128)S(1)}, f32[264,128]{1,0:T(8,128)S(1)}, u32[]{:S(2)}, u32[]{:S(2)}) %collective-permute-start.14) | collective-permute-done | bytes 135200 | tf_op jit(solution)/shard_map/ppermute | solution.py:336
  135.1 0.8 shard_map.89
  (11 shorter events, 0.1 us)
Async XLA Ops:
  0.6 0.8 copy-start
  19.8 2.0 %collective-permute-start = (f32[1024,128]{1,0:T(8,128)S(1)}, f32[1024,128]{1,0:T(8,128)S(1)}, u32[]{:S(2)}, u32[]{:S(2)}) collective-permute-start(f32[1024,128]{1,0:T(8,128)S(1)} %bitcast.12), channel_id=1, source_target_pairs={{0,8},{8,0},{16,24},{24,16},{32,40},{40,32},{48,56},{56,48},{64,72... | collective-permute-start | bytes 1572872 | tf_op jit(solution)/shard_map/ppermute | solution.py:345
  19.8 0.7 copy-start.2
  20.4 0.7 copy-start.3
  21.1 0.7 copy-start.4
  26.2 11.5 %collective-permute-start.3 = (f32[136,128]{1,0:T(8,128)S(1)}, f32[136,128]{1,0:T(8,128)S(1)}, u32[]{:S(2)}, u32[]{:S(2)}) collective-permute-start(f32[136,128]{1,0:T(8,128)S(1)} %get-tuple-element.42.own_ref), channel_id=1, source_target_pairs={{0,3},{1,2},{2,1},{3,0},{4,7},{5,6},{6,5},{7,4},{8,11},{9,10},{10,... | collective-permute-start | bytes 208904 | tf_op jit(solution)/shard_map/ppermute | solution.py:336
  28.2 9.5 %collective-permute-start.2 = (f32[136,128]{1,0:T(8,128)S(1)}, f32[136,128]{1,0:T(8,128)S(1)}, u32[]{:S(2)}, u32[]{:S(2)}) collective-permute-start(f32[136,128]{1,0:T(8,128)S(1)} %get-tuple-element.42.own_ref), channel_id=1, source_target_pairs={{0,2},{1,3},{2,0},{3,1},{4,6},{5,7},{6,4},{7,5},{8,10},{9,11},{10,... | collective-permute-start | bytes 208904 | tf_op jit(solution)/shard_map/ppermute | solution.py:336
  29.7 8.0 %collective-permute-start.1 = (f32[136,128]{1,0:T(8,128)S(1)}, f32[136,128]{1,0:T(8,128)S(1)}, u32[]{:S(2)}, u32[]{:S(2)}) collective-permute-start(f32[136,128]{1,0:T(8,128)S(1)} %get-tuple-element.42.own_ref), channel_id=1, source_target_pairs={{0,1},{1,0},{2,3},{3,2},{4,5},{5,4},{6,7},{7,6},{8,9},{9,8},{10,11... | collective-permute-start | bytes 208904 | tf_op jit(solution)/shard_map/ppermute | solution.py:336
  31.0 6.6 %collective-permute-start.4 = (f32[8,128]{1,0:T(8,128)S(1)}, f32[8,128]{1,0:T(8,128)S(1)}, u32[]{:S(2)}, u32[]{:S(2)}) collective-permute-start(f32[8,128]{1,0:T(8,128)S(1)} %get-tuple-element.43), channel_id=1, source_target_pairs={{0,6},{1,7},{2,4},{3,5},{4,2},{5,3},{6,0},{7,1},{8,14},{9,15},{10,... | collective-permute-start | bytes 12296 | tf_op jit(solution)/shard_map/ppermute | solution.py:336
  38.4 8.5 %collective-permute-start.5 = (f32[136,128]{1,0:T(8,128)S(1)}, f32[136,128]{1,0:T(8,128)S(1)}, u32[]{:S(2)}, u32[]{:S(2)}) collective-permute-start(f32[136,128]{1,0:T(8,128)S(1)} %get-tuple-element.47), channel_id=1, source_target_pairs={{0,6},{1,7},{2,4},{3,5},{4,2},{5,3},{6,0},{7,1},{8,14},{9,15},{10,... | collective-permute-start | bytes 208904 | tf_op jit(solution)/shard_map/ppermute | solution.py:336
  72.2 8.0 %collective-permute-start.8 = (f32[136,128]{1,0:T(8,128)S(1)}, f32[136,128]{1,0:T(8,128)S(1)}, u32[]{:S(2)}, u32[]{:S(2)}) collective-permute-start(f32[136,128]{1,0:T(8,128)S(1)} %get-tuple-element.56.own_ref), channel_id=1, source_target_pairs={{0,3},{1,2},{2,1},{3,0},{4,7},{5,6},{6,5},{7,4},{8,11},{9,10},{10,... | collective-permute-start | bytes 208904 | tf_op jit(solution)/shard_map/ppermute | solution.py:336
  73.3 6.9 %collective-permute-start.7 = (f32[136,128]{1,0:T(8,128)S(1)}, f32[136,128]{1,0:T(8,128)S(1)}, u32[]{:S(2)}, u32[]{:S(2)}) collective-permute-start(f32[136,128]{1,0:T(8,128)S(1)} %get-tuple-element.56.own_ref), channel_id=1, source_target_pairs={{0,2},{1,3},{2,0},{3,1},{4,6},{5,7},{6,4},{7,5},{8,10},{9,11},{10,... | collective-permute-start | bytes 208904 | tf_op jit(solution)/shard_map/ppermute | solution.py:336
  75.1 5.1 %collective-permute-start.6 = (f32[136,128]{1,0:T(8,128)S(1)}, f32[136,128]{1,0:T(8,128)S(1)}, u32[]{:S(2)}, u32[]{:S(2)}) collective-permute-start(f32[136,128]{1,0:T(8,128)S(1)} %get-tuple-element.56.own_ref), channel_id=1, source_target_pairs={{0,1},{1,0},{2,3},{3,2},{4,5},{5,4},{6,7},{7,6},{8,9},{9,8},{10,11... | collective-permute-start | bytes 208904 | tf_op jit(solution)/shard_map/ppermute | solution.py:336
  80.9 7.3 %collective-permute-start.9 = (f32[136,128]{1,0:T(8,128)S(1)}, f32[136,128]{1,0:T(8,128)S(1)}, u32[]{:S(2)}, u32[]{:S(2)}) collective-permute-start(f32[136,128]{1,0:T(8,128)S(1)} %get-tuple-element.59.send_ref), channel_id=1, source_target_pairs={{0,6},{1,7},{2,4},{3,5},{4,2},{5,3},{6,0},{7,1},{8,14},{9,15},{10,... | collective-permute-start | bytes 208904 | tf_op jit(solution)/shard_map/ppermute | solution.py:336
  88.2 15.6 %collective-permute-start.10 = (f32[512,128]{1,0:T(8,128)S(1)}, f32[512,128]{1,0:T(8,128)S(1)}, u32[]{:S(2)}, u32[]{:S(2)}) collective-permute-start(f32[512,128]{1,0:T(8,128)S(1)} %get-tuple-element.65.inner_near_ref), channel_id=1, source_target_pairs={{0,6},{1,7},{2,4},{3,5},{4,2},{5,3},{6,0},{7,1},{8,14},{9,15},{10,... | collective-permute-start | bytes 786440 | tf_op jit(solution)/shard_map/ppermute | solution.py:336
  91.4 43.7 %copy-start.1 = (f32[64,128]{1,0:T(8,128)S(1)}, f32[64,128]{1,0:T(8,128)}, u32[]{:S(2)}) copy-start(f32[64,128]{1,0:T(8,128)} %ray_ref.3) | copy-start | bytes 98308
  116.7 8.0 %collective-permute-start.13 = (f32[136,128]{1,0:T(8,128)S(1)}, f32[136,128]{1,0:T(8,128)S(1)}, u32[]{:S(2)}, u32[]{:S(2)}) collective-permute-start(f32[136,128]{1,0:T(8,128)S(1)} %shard_map.87.own_ref), channel_id=1, source_target_pairs={{0,3},{1,2},{2,1},{3,0},{4,7},{5,6},{6,5},{7,4},{8,11},{9,10},{10,... | collective-permute-start | bytes 208904 | tf_op jit(solution)/shard_map/ppermute | solution.py:336
  117.7 6.9 %collective-permute-start.12 = (f32[136,128]{1,0:T(8,128)S(1)}, f32[136,128]{1,0:T(8,128)S(1)}, u32[]{:S(2)}, u32[]{:S(2)}) collective-permute-start(f32[136,128]{1,0:T(8,128)S(1)} %shard_map.87.own_ref), channel_id=1, source_target_pairs={{0,2},{1,3},{2,0},{3,1},{4,6},{5,7},{6,4},{7,5},{8,10},{9,11},{10,... | collective-permute-start | bytes 208904 | tf_op jit(solution)/shard_map/ppermute | solution.py:336
  119.6 5.1 %collective-permute-start.11 = (f32[136,128]{1,0:T(8,128)S(1)}, f32[136,128]{1,0:T(8,128)S(1)}, u32[]{:S(2)}, u32[]{:S(2)}) collective-permute-start(f32[136,128]{1,0:T(8,128)S(1)} %shard_map.87.own_ref), channel_id=1, source_target_pairs={{0,1},{1,0},{2,3},{3,2},{4,5},{5,4},{6,7},{7,6},{8,9},{9,8},{10,11... | collective-permute-start | bytes 208904 | tf_op jit(solution)/shard_map/ppermute | solution.py:336
  125.0 10.1 %collective-permute-start.14 = (f32[264,128]{1,0:T(8,128)S(1)}, f32[264,128]{1,0:T(8,128)S(1)}, u32[]{:S(2)}, u32[]{:S(2)}) collective-permute-start(f32[264,128]{1,0:T(8,128)S(1)} %shard_map.88.near_ref), channel_id=1, source_target_pairs={{0,6},{1,7},{2,4},{3,5},{4,2},{5,3},{6,0},{7,1},{8,14},{9,15},{10,... | collective-permute-start | bytes 405512 | tf_op jit(solution)/shard_map/ppermute | solution.py:336

commit v4 on v3

--- a/solution.py
+++ b/solution.py
@@ -15,8 +15,7 @@
 CHUNKS = 8
 PAD = 8
 MAP = CAP
-NORM = CAP + 1
-NORM2 = CAP + 2
+NORM, LOCAL, OTHER = CAP, CAP + 1, CAP + 2
 SENT = N_VOX * PAD
 PART = TILE + 8
 SUM = VT_DEV + 8
@@ -32,21 +31,15 @@
 
 def select_rows(choice, values):
     high = values.astype(BF16)
-    rest = values - high.astype(F32)
-    middle = rest.astype(BF16)
-    low = (rest - middle.astype(F32)).astype(BF16)
-    total = jnp.dot(choice, low, preferred_element_type=F32)
-    total = total + jnp.dot(choice, middle, preferred_element_type=F32)
+    middle = (values - high.astype(F32)).astype(BF16)
+    total = jnp.dot(choice, middle, preferred_element_type=F32)
     return total + jnp.dot(choice, high, preferred_element_type=F32)
 
 
 def select_columns(values, choice):
     high = values.astype(BF16)
-    rest = values - high.astype(F32)
-    middle = rest.astype(BF16)
-    low = (rest - middle.astype(F32)).astype(BF16)
-    total = jnp.dot(low, choice, preferred_element_type=F32)
-    total = total + jnp.dot(middle, choice, preferred_element_type=F32)
+    middle = (values - high.astype(F32)).astype(BF16)
+    total = jnp.dot(middle, choice, preferred_element_type=F32)
     return total + jnp.dot(high, choice, preferred_element_type=F32)
 
 
@@ -100,7 +93,7 @@
 
 def back_first_kernel(
     tiles_hbm, same_ref, other_ref, pack_ref,
-    part_ref, share_ref, natural_ref, row_ref, vox_ref, extra_ref, ids_ref,
+    part_ref, share_ref, natural_ref, row_ref, slot_ref, vox_ref, extra_ref, ids_ref,
     picked_ref, index_ref, place_ref, sems,
 ):
     size = TILE // CHUNKS
@@ -124,6 +117,7 @@
     move.start()
 
     row_ref[...] = target * PAD + place
+    slot_ref[...] = slot
     vox_ref[...] = vox
     ids_ref[...] = jnp.broadcast_to(vox.astype(F32), (8, TILE))
     write_tail(part_ref, vox, None, None, None)
@@ -151,22 +145,22 @@
     share_ref[...] = jnp.transpose(part_ref[0:TILE, :])
 
 
-def back_share(received_ref, tiles_ref, row_ref, vox_ref, gamma_ref, part_ref, weight_ref):
+def back_share(received_ref, tiles_ref, row_ref, vox_ref, part_ref, weight_ref):
     received = received_ref[...]
     weight_ref[...] = select_columns(jnp.transpose(received), one_hot(SENT, row_ref[...]))
     heads = jnp.sum(received.reshape(N_VOX, PAD, TILE), axis=0)
     share = back_tiles(tiles_ref, weight_ref)
     part_ref[0:TILE, :] = jnp.transpose(share)
-    write_tail(part_ref, vox_ref[...], heads[NORM : NORM + 1, :], gamma_ref[0:1, :], heads[NORM2 : NORM2 + 1, :])
+    write_tail(part_ref, vox_ref[...], *(heads[row : row + 1, :] for row in (NORM, LOCAL, OTHER)))
     return share
 
 
-def back_kernel(received_ref, tiles_ref, row_ref, vox_ref, gamma_ref, part_ref, share_ref, weight_ref):
-    share_ref[...] = back_share(received_ref, tiles_ref, row_ref, vox_ref, gamma_ref, part_ref, weight_ref)
-
-
-def back_last_kernel(received_ref, tiles_ref, row_ref, vox_ref, gamma_ref, part_ref, weight_ref):
-    back_share(received_ref, tiles_ref, row_ref, vox_ref, gamma_ref, part_ref, weight_ref)
+def back_kernel(received_ref, tiles_ref, row_ref, vox_ref, part_ref, share_ref, weight_ref):
+    share_ref[...] = back_share(received_ref, tiles_ref, row_ref, vox_ref, part_ref, weight_ref)
+
+
+def back_last_kernel(received_ref, tiles_ref, row_ref, vox_ref, part_ref, weight_ref):
+    back_share(received_ref, tiles_ref, row_ref, vox_ref, part_ref, weight_ref)
 
 
 def quad_sum(own_ref, one_ref, two_ref, three_ref):
@@ -207,7 +201,7 @@
     near_ref[VT_DEV:SUM, :] = tail
 
 
-def forward_tiles(values, share, tiles_ref, row_ref, extra_ref, payload_ref, sums_ref):
+def forward_tiles(values, share, tiles_ref, gamma_ref, sums_ref):
     def step(index, unused):
         for inner in range(8):
             ray = index * 8 + inner
@@ -216,18 +210,20 @@
         return unused
 
     lax.fori_loop(0, TILE // 8, step, 0)
+    gamma_ref[...] = jnp.broadcast_to(jnp.sum(values * share, axis=0, keepdims=True), (8, TILE))
     rays = sums_ref[pl.ds(0, TILE, stride=8), :]
     for inner in range(1, 8):
         rays = rays + sums_ref[pl.ds(inner, TILE, stride=8), :]
-    gamma = jnp.sum(values * share, axis=0, keepdims=True)
-    head = jnp.where((iota((SENT, TILE), 0) & (PAD - 1)) == NORM, gamma, extra_ref[...])
-    payload_ref[...] = select_rows(one_hot(SENT, row_ref[...]), jnp.transpose(rays)) + head
-
-
-def forward_first_kernel(mine_ref, far_ref, share_ref, tiles_ref, row_ref, extra_ref, payload_ref, values_ref, sums_ref):
+    return jnp.transpose(rays)
+
+
+def forward_first_kernel(
+    mine_ref, far_ref, share_ref, tiles_ref, row_ref, extra_ref, payload_ref, values_ref, gamma_ref, sums_ref
+):
     values = mine_ref[...] + far_ref[0:TILE, :]
     values_ref[...] = values
-    forward_tiles(values, share_ref[...], tiles_ref, row_ref, extra_ref, payload_ref, sums_ref)
+    rays = forward_tiles(values, share_ref[...], tiles_ref, gamma_ref, sums_ref)
+    payload_ref[...] = select_rows(one_hot(SENT, row_ref[...]), rays) + extra_ref[...]
 
 
 def lane_sum(tail, place):
@@ -235,8 +231,8 @@
 
 
 def forward_kernel(
-    mine_ref, send_ref, far_ref, share_ref, values0_ref, share0_ref, tiles_ref, row_ref, extra_ref,
-    payload_ref, scalars_ref, sums_ref,
+    mine_ref, send_ref, far_ref, share_ref, values0_ref, share0_ref, tiles_ref, slot_ref,
+    payload_ref, scalars_ref, gamma_ref, sums_ref,
 ):
     tail = send_ref[TILE:PART, :] + far_ref[TILE:PART, :]
     gamma, square = lane_sum(tail, GAMMA), lane_sum(tail, IMAGE)
@@ -245,10 +241,19 @@
     scalars_ref[...] = jnp.where(sub == 0, gamma, jnp.where(sub == 1, square, step))
     values = values0_ref[...] - step * (mine_ref[...] + far_ref[0:TILE, :])
     share = share0_ref[...] - step * share_ref[...]
-    forward_tiles(values, share, tiles_ref, row_ref, extra_ref, payload_ref, sums_ref)
-
-
-def owner_parts(received_ref):
+    rays = forward_tiles(values, share, tiles_ref, gamma_ref, sums_ref)
+    payload_ref[...] = select_rows(one_hot(TILE, slot_ref[...]), rays)
+
+
+def back_message(choice, image, rows):
+    place = iota((SENT, TILE), 0) & (PAD - 1)
+    head = jnp.zeros((SENT, TILE), F32)
+    for where, row in rows:
+        head = jnp.where(place == where, row, head)
+    return select_rows(choice, image) + head
+
+
+def owner_first_kernel(received_ref, gamma_ref, payload_ref, image_ref, choice_ref, compact_ref):
     received = received_ref[...]
     blocks = received.reshape(N_VOX, PAD, TILE)
     head = jnp.broadcast_to(blocks[:, MAP : MAP + 1, :], (N_VOX, PAD, TILE)).reshape(SENT, TILE)
@@ -257,30 +262,24 @@
     hit = (column.astype(jnp.int32) == lane) & (place < CAP)
     choice = jnp.where(hit, 1.0, 0.0)
     image = select_rows(jnp.transpose(choice).astype(BF16), received)
-    gamma = jnp.sum(blocks, axis=0)[NORM : NORM + 1, :]
-    return choice.astype(BF16), image, jnp.broadcast_to(gamma, (8, TILE))
-
-
-def owner_first_kernel(received_ref, payload_ref, image_ref, gamma_ref):
-    choice, image, gamma_ref[...] = owner_parts(received_ref)
     owned = image_ref.shape[0]
     lower = image[0:owned, :]
     image_ref[...] = lower
     square = jnp.sum(lower * lower, axis=0, keepdims=True)
-    place = iota((SENT, TILE), 0) & (PAD - 1)
-    payload_ref[...] = select_rows(choice, image) + jnp.where(place == NORM, square, 0.0)
-
-
-def owner_kernel(received_ref, image0_ref, payload_ref, image_ref, gamma_ref):
-    choice, image, gamma_ref[...] = owner_parts(received_ref)
+    payload_ref[...] = back_message(choice.astype(BF16), image, ((NORM, square), (LOCAL, gamma_ref[0:1, :])))
+    choice_ref[...] = choice
+    compact_ref[...] = jnp.transpose(choice.reshape(N_VOX, PAD, TILE)[:, 0:CAP, :].reshape(TILE, TILE))
+
+
+def owner_kernel(received_ref, gamma_ref, image0_ref, choice_ref, compact_ref, payload_ref, image_ref):
+    image = select_rows(compact_ref[...].astype(BF16), received_ref[...])
     owned = image_ref.shape[0]
     lower = image[0:owned, :]
     image_ref[...] = lower
     square = jnp.sum(lower * lower, axis=0, keepdims=True)
     cross = jnp.sum(lower * image0_ref[...], axis=0, keepdims=True)
-    place = iota((SENT, TILE), 0) & (PAD - 1)
-    head = jnp.where(place == NORM, square, jnp.where(place == NORM2, cross, 0.0))
-    payload_ref[...] = select_rows(choice, image) + head
+    rows = ((NORM, square), (LOCAL, gamma_ref[0:1, :]), (OTHER, cross))
+    payload_ref[...] = back_message(choice_ref[...].astype(BF16), image, rows)
 
 
 def last_kernel(
@@ -349,9 +348,9 @@
         [],
         (tile_slot.reshape(1, TILE), slot_block, tile_vox.reshape(1, TILE)),
     )
-    own, share0, natural, slot_row, vox_row, extra, ids = call(
+    own, share0, natural, slot_row, slot, vox_row, extra, ids = call(
         back_first_kernel,
-        [part, block, (TILE, TILE, TILE), indices, indices, sent, scalar],
+        [part, block, (TILE, TILE, TILE), indices, indices, indices, sent, scalar],
         [
             block,
             pltpu.VMEM((1, TILE), jnp.int32),
@@ -373,25 +372,27 @@
         (natural,),
         cost=pl.CostEstimate(flops=0, bytes_accessed=2**24, transcendentals=0),
     )
-    payload, values0 = call(
-        forward_first_kernel, [sent, block], [sums], (mine, far, share0, tiles, slot_row, extra)
-    )
-    payload, image0, gamma = call(owner_first_kernel, [sent, rays, scalar], [], (over_vox(payload),))
-    own, share = call(back_kernel, [part, block], [block], (over_vox(payload), tiles, slot_row, vox_row, gamma))
+    payload, values0, gamma = call(
+        forward_first_kernel, [sent, block, scalar], [sums], (mine, far, share0, tiles, slot_row, extra)
+    )
+    payload, image0, choice, compact = call(
+        owner_first_kernel, [sent, rays, sent, block], [], (over_vox(payload), gamma)
+    )
+    own, share = call(back_kernel, [part, block], [block], (over_vox(payload), tiles, slot_row, vox_row))
     near, mine, send = call(
         quad_kernel, [(2 * VT_DEV, TILE), block, part], [], (*quad(own), ids, near)
     )
     far, near = lax.optimization_barrier((across(send, 6), near))
     inner_far = across(near, 6)
-    payload, scalars = call(
+    payload, scalars, gamma = call(
         forward_kernel,
-        [sent, scalar],
+        [block, scalar, scalar],
         [sums],
-        (mine, send, far, share, values0, share0, tiles, slot_row, extra),
+        (mine, send, far, share, values0, share0, tiles, slot),
     )
     received, inner_far = lax.optimization_barrier((over_vox(payload), inner_far))
-    payload, image1, gamma = call(owner_kernel, [sent, rays, scalar], [], (received, image0))
-    (own,) = call(back_last_kernel, [part], [block], (over_vox(payload), tiles, slot_row, vox_row, gamma))
+    payload, image1 = call(owner_kernel, [sent, rays], [], (received, gamma, image0, choice, compact))
+    (own,) = call(back_last_kernel, [part], [block], (over_vox(payload), tiles, slot_row, vox_row))
     (last,) = call(quad_last_kernel, [(SUM, TILE)], [], quad(own))
     return tuple(
         call(

time: 136 us -> 135 us (level)
  no operation moved by 1% of the time
where the time goes in v4:
time: 135 us
  blocking collectives  63 us (47%)
  starting transfers between devices  31.3 us (23%)
  waiting for transfers between devices  20.9 us (15%)
  Pallas kernels  16 us (12%)
  local copies, waits for them, and re-layouts  2.72 us (2%)
    all_to_all x4, blocking collectives, over_vox(): return lax.all_to_all(array, 'vox', 0, 0, tiled=True)  44.7 us
    ppermute x14, starting transfers between devices, across(): lax.ppermute(array, 'row', [(index, index ^ distance) for index in range(...  31.3 us
    ppermute x14, waiting for transfers between devices, across(): lax.ppermute(array, 'row', [(index, index ^ distance) for index in range(...  20.9 us
    all_to_all x1, blocking collectives, local(): lax.all_to_all(copies, 'vox', 0, 0, tiled=True, axis_index_groups=chips)  18.3 us
    pallas_call x14, Pallas kernels, call(): pl.pallas_call(kernel, out_shape=outs, in_specs=specs + [vmem] * (len(arg...  16 us
    unnamed x10, local copies, waits for them, and re-layouts  2.72 us
  transfers between devices with their start and end apart: 15, of which 5 were waited for; matrix products, arithmetic and copies ran while one was open for 0% of the time, Pallas kernels for 4%

profile of v4, /device:TPU:32, one launch (start us, length us, event | category | flops | bytes accessed | tf_op | source)
XLA Modules:
  0.0 134.8 jit_solution(14131350746783339912)
XLA Ops:
  0.6 0.0 copy-start
  0.6 0.7 copy-done
  1.4 18.3 %all_to_all.57 = f32[16,64,128]{2,1,0:T(8,128)S(1)} all-to-all(f32[16,64,128]{2,1,0:T(8,128)S(1)} %bitcast.14), channel_id=1, replica_groups={{0,16,32,48,64,80,96,112,128,144,160,176,192,208,224,240},{8,24,40,56,7..., dimensions={0} | all-to-all | bytes 1048576 | tf_op jit(solution)/shard_map/all_to_all | solution.py:342
  19.8 0.0 collective-permute-start
  19.8 0.7 copy-done.2
  20.4 0.7 copy-done.3
  21.1 0.7 copy-done.4
  21.7 0.0 collective-permute-done.other_ref
  21.7 4.4 %shard_map.78 = (f32[136,128]{1,0:T(8,128)S(1)}, f32[128,128]{1,0:T(8,128)S(1)}, f32[128,128,128]{2,1,0:T(8,128)S(1)}, s32[1,128]{1,0:T(1,128)S(1)}, s32[1,128]{...) custom-call(f32[128,128,128]{2,1,0:T(8,128)} %tiles_hbm.1, ...), custom_call_target="tpu_custom_call" | custom-call | tf_op jit(solution)/shard_map/pallas_call | solution.py:309
  26.2 2.0 %collective-permute-start.3 = (f32[136,128]{1,0:T(8,128)S(1)}, f32[136,128]{1,0:T(8,128)S(1)}, u32[]{:S(2)}, u32[]{:S(2)}) collective-permute-start(f32[136,128]{1,0:T(8,128)S(1)} %get-tuple-element.45.own_ref), channel_id=1, source_target_pairs={{0,3},{1,2},{2,1},{3,0},{4,7},{5,6},{6,5},{7,4},{8,11},{9,10},{10,... | collective-permute-start | bytes 208904 | tf_op jit(solution)/shard_map/ppermute | solution.py:335
  28.2 1.5 %collective-permute-start.2 = (f32[136,128]{1,0:T(8,128)S(1)}, f32[136,128]{1,0:T(8,128)S(1)}, u32[]{:S(2)}, u32[]{:S(2)}) collective-permute-start(f32[136,128]{1,0:T(8,128)S(1)} %get-tuple-element.45.own_ref), channel_id=1, source_target_pairs={{0,2},{1,3},{2,0},{3,1},{4,6},{5,7},{6,4},{7,5},{8,10},{9,11},{10,... | collective-permute-start | bytes 208904 | tf_op jit(solution)/shard_map/ppermute | solution.py:335
  29.7 1.4 %collective-permute-start.1 = (f32[136,128]{1,0:T(8,128)S(1)}, f32[136,128]{1,0:T(8,128)S(1)}, u32[]{:S(2)}, u32[]{:S(2)}) collective-permute-start(f32[136,128]{1,0:T(8,128)S(1)} %get-tuple-element.45.own_ref), channel_id=1, source_target_pairs={{0,1},{1,0},{2,3},{3,2},{4,5},{5,4},{6,7},{7,6},{8,9},{9,8},{10,11... | collective-permute-start | bytes 208904 | tf_op jit(solution)/shard_map/ppermute | solution.py:335
  31.0 5.1 %collective-permute-start.4 = (f32[8,128]{1,0:T(8,128)S(1)}, f32[8,128]{1,0:T(8,128)S(1)}, u32[]{:S(2)}, u32[]{:S(2)}) collective-permute-start(f32[8,128]{1,0:T(8,128)S(1)} %get-tuple-element.46), channel_id=1, source_target_pairs={{0,6},{1,7},{2,4},{3,5},{4,2},{5,3},{6,0},{7,1},{8,14},{9,15},{10,... | collective-permute-start | bytes 12296 | tf_op jit(solution)/shard_map/ppermute | solution.py:335
  36.1 1.6 %collective-permute-done.4.ids_ref = f32[8,128]{1,0:T(8,128)S(1)} collective-permute-done((f32[8,128]{1,0:T(8,128)S(1)}, f32[8,128]{1,0:T(8,128)S(1)}, u32[]{:S(2)}, u32[]{:S(2)}) %collective-permute-start.4) | collective-permute-done | bytes 4128 | tf_op jit(solution)/shard_map/ppermute | solution.py:335
  37.7 0.0 collective-permute-done.2.two_ref
  37.7 0.0 collective-permute-done.1.one_ref
  37.7 0.6 shard_map.79
  38.2 4.2 %collective-permute-start.5 = (f32[136,128]{1,0:T(8,128)S(1)}, f32[136,128]{1,0:T(8,128)S(1)}, u32[]{:S(2)}, u32[]{:S(2)}) collective-permute-start(f32[136,128]{1,0:T(8,128)S(1)} %get-tuple-element.50), channel_id=1, source_target_pairs={{0,6},{1,7},{2,4},{3,5},{4,2},{5,3},{6,0},{7,1},{8,14},{9,15},{10,... | collective-permute-start | bytes 208904 | tf_op jit(solution)/shard_map/ppermute | solution.py:335
  42.5 4.2 %shard_map.80.tiles_ref = f32[128,128,128]{2,1,0:T(8,128)S(1)} custom-call(f32[128,128,128]{2,1,0:T(8,128)S(1)} %get-tuple-element.52.natural_ref), custom_call_target="tpu_custom_call" | custom-call | bytes 16777216 | tf_op jit(solution)/shard_map/pallas_call | solution.py:309
  46.7 1.0 shard_map.81
  47.7 11.4 %all_to_all.58 = f32[32,8,128]{2,1,0:T(8,128)S(1)} all-to-all(f32[32,8,128]{2,1,0:T(8,128)S(1)} %bitcast.19), channel_id=1, replica_groups=mesh['vox'=32,'row'=8] {'vox'}, dimensions={0} | all-to-all | bytes 262144 | tf_op jit(solution)/shard_map/all_to_all | solution.py:332
  59.2 0.5 shard_map.82
  59.7 11.3 %all_to_all.59 = f32[32,8,128]{2,1,0:T(8,128)S(1)} all-to-all(f32[32,8,128]{2,1,0:T(8,128)S(1)} %bitcast.20), channel_id=1, replica_groups=mesh['vox'=32,'row'=8] {'vox'}, dimensions={0} | all-to-all | bytes 262144 | tf_op jit(solution)/shard_map/all_to_all | solution.py:332
  71.0 1.0 shard_map.83
  72.0 1.1 collective-permute-start.8
  73.1 1.8 %collective-permute-start.7 = (f32[136,128]{1,0:T(8,128)S(1)}, f32[136,128]{1,0:T(8,128)S(1)}, u32[]{:S(2)}, u32[]{:S(2)}) collective-permute-start(f32[136,128]{1,0:T(8,128)S(1)} %get-tuple-element.59.own_ref), channel_id=1, source_target_pairs={{0,2},{1,3},{2,0},{3,1},{4,6},{5,7},{6,4},{7,5},{8,10},{9,11},{10,... | collective-permute-start | bytes 208904 | tf_op jit(solution)/shard_map/ppermute | solution.py:335
  74.9 0.7 collective-permute-start.6
  75.6 4.4 %collective-permute-done.8.three_ref = f32[136,128]{1,0:T(8,128)S(1)} collective-permute-done((f32[136,128]{1,0:T(8,128)S(1)}, f32[136,128]{1,0:T(8,128)S(1)}, u32[]{:S(2)}, u32[]{:S(2)}) %collective-permute-start.8) | collective-permute-done | bytes 69664 | tf_op jit(solution)/shard_map/ppermute | solution.py:335
  80.0 0.6 shard_map.84
  80.5 4.1 %collective-permute-start.9 = (f32[136,128]{1,0:T(8,128)S(1)}, f32[136,128]{1,0:T(8,128)S(1)}, u32[]{:S(2)}, u32[]{:S(2)}) collective-permute-start(f32[136,128]{1,0:T(8,128)S(1)} %get-tuple-element.62.send_ref), channel_id=1, source_target_pairs={{0,6},{1,7},{2,4},{3,5},{4,2},{5,3},{6,0},{7,1},{8,14},{9,15},{10,... | collective-permute-start | bytes 208904 | tf_op jit(solution)/shard_map/ppermute | solution.py:335
  84.6 3.2 %collective-permute-done.9.far_ref = f32[136,128]{1,0:T(8,128)S(1)} collective-permute-done((f32[136,128]{1,0:T(8,128)S(1)}, f32[136,128]{1,0:T(8,128)S(1)}, u32[]{:S(2)}, u32[]{:S(2)}) %collective-permute-start.9) | collective-permute-done | bytes 69664 | tf_op jit(solution)/shard_map/ppermute | solution.py:335
  87.8 3.2 %collective-permute-start.10 = (f32[512,128]{1,0:T(8,128)S(1)}, f32[512,128]{1,0:T(8,128)S(1)}, u32[]{:S(2)}, u32[]{:S(2)}) collective-permute-start(f32[512,128]{1,0:T(8,128)S(1)} %get-tuple-element.69.inner_near_ref), channel_id=1, source_target_pairs={{0,6},{1,7},{2,4},{3,5},{4,2},{5,3},{6,0},{7,1},{8,14},{9,15},{10,... | collective-permute-start | bytes 786440 | tf_op jit(solution)/shard_map/ppermute | solution.py:335
  91.0 1.1 shard_map.85
  92.2 10.8 %all_to_all.60 = f32[32,4,128]{2,1,0:T(4,128)S(1)} all-to-all(f32[32,4,128]{2,1,0:T(4,128)S(1)} %bitcast.22), channel_id=1, replica_groups=mesh['vox'=32,'row'=8] {'vox'}, dimensions={0} | all-to-all | bytes 131072 | tf_op jit(solution)/shard_map/all_to_all | solution.py:332
  103.0 0.0 collective-permute-done.10.inner_far_ref
  103.0 0.3 shard_map.86
  103.3 11.2 %all_to_all.61 = f32[32,8,128]{2,1,0:T(8,128)S(1)} all-to-all(f32[32,8,128]{2,1,0:T(8,128)S(1)} %bitcast.21), channel_id=1, replica_groups=mesh['vox'=32,'row'=8] {'vox'}, dimensions={0} | all-to-all | bytes 262144 | tf_op jit(solution)/shard_map/all_to_all | solution.py:332
  114.5 1.0 shard_map.87.own_ref
  115.5 1.1 collective-permute-start.13
  116.6 1.8 %collective-permute-start.12 = (f32[136,128]{1,0:T(8,128)S(1)}, f32[136,128]{1,0:T(8,128)S(1)}, u32[]{:S(2)}, u32[]{:S(2)}) collective-permute-start(f32[136,128]{1,0:T(8,128)S(1)} %shard_map.87.own_ref), channel_id=1, source_target_pairs={{0,2},{1,3},{2,0},{3,1},{4,6},{5,7},{6,4},{7,5},{8,10},{9,11},{10,... | collective-permute-start | bytes 208904 | tf_op jit(solution)/shard_map/ppermute | solution.py:335
  118.4 0.7 collective-permute-start.11
  119.1 4.4 %collective-permute-done.13.three_ref = f32[136,128]{1,0:T(8,128)S(1)} collective-permute-done((f32[136,128]{1,0:T(8,128)S(1)}, f32[136,128]{1,0:T(8,128)S(1)}, u32[]{:S(2)}, u32[]{:S(2)}) %collective-permute-start.13) | collective-permute-done | bytes 69664 | tf_op jit(solution)/shard_map/ppermute | solution.py:335
  123.5 0.0 collective-permute-done.12.two_ref
  123.5 0.0 collective-permute-done.11.one_ref
  123.5 0.3 shard_map.88.near_ref
  123.8 2.8 %collective-permute-start.14 = (f32[264,128]{1,0:T(8,128)S(1)}, f32[264,128]{1,0:T(8,128)S(1)}, u32[]{:S(2)}, u32[]{:S(2)}) collective-permute-start(f32[264,128]{1,0:T(8,128)S(1)} %shard_map.88.near_ref), channel_id=1, source_target_pairs={{0,6},{1,7},{2,4},{3,5},{4,2},{5,3},{6,0},{7,1},{8,14},{9,15},{10,... | collective-permute-start | bytes 405512 | tf_op jit(solution)/shard_map/ppermute | solution.py:335
  126.6 7.3 %collective-permute-done.14.far_ref = f32[264,128]{1,0:T(8,128)S(1)} collective-permute-done((f32[264,128]{1,0:T(8,128)S(1)}, f32[264,128]{1,0:T(8,128)S(1)}, u32[]{:S(2)}, u32[]{:S(2)}) %collective-permute-start.14) | collective-permute-done | bytes 135200 | tf_op jit(solution)/shard_map/ppermute | solution.py:335
  134.0 0.8 shard_map.89
  (11 shorter events, 0.1 us)
Async XLA Ops:
  0.6 0.8 copy-start
  19.8 2.0 %collective-permute-start = (f32[1024,128]{1,0:T(8,128)S(1)}, f32[1024,128]{1,0:T(8,128)S(1)}, u32[]{:S(2)}, u32[]{:S(2)}) collective-permute-start(f32[1024,128]{1,0:T(8,128)S(1)} %bitcast.12), channel_id=1, source_target_pairs={{0,8},{8,0},{16,24},{24,16},{32,40},{40,32},{48,56},{56,48},{64,72... | collective-permute-start | bytes 1572872 | tf_op jit(solution)/shard_map/ppermute | solution.py:344
  19.8 0.7 copy-start.2
  20.4 0.7 copy-start.3
  21.1 0.7 copy-start.4
  26.2 11.5 %collective-permute-start.3 = (f32[136,128]{1,0:T(8,128)S(1)}, f32[136,128]{1,0:T(8,128)S(1)}, u32[]{:S(2)}, u32[]{:S(2)}) collective-permute-start(f32[136,128]{1,0:T(8,128)S(1)} %get-tuple-element.45.own_ref), channel_id=1, source_target_pairs={{0,3},{1,2},{2,1},{3,0},{4,7},{5,6},{6,5},{7,4},{8,11},{9,10},{10,... | collective-permute-start | bytes 208904 | tf_op jit(solution)/shard_map/ppermute | solution.py:335
  28.2 9.5 %collective-permute-start.2 = (f32[136,128]{1,0:T(8,128)S(1)}, f32[136,128]{1,0:T(8,128)S(1)}, u32[]{:S(2)}, u32[]{:S(2)}) collective-permute-start(f32[136,128]{1,0:T(8,128)S(1)} %get-tuple-element.45.own_ref), channel_id=1, source_target_pairs={{0,2},{1,3},{2,0},{3,1},{4,6},{5,7},{6,4},{7,5},{8,10},{9,11},{10,... | collective-permute-start | bytes 208904 | tf_op jit(solution)/shard_map/ppermute | solution.py:335
  29.7 8.0 %collective-permute-start.1 = (f32[136,128]{1,0:T(8,128)S(1)}, f32[136,128]{1,0:T(8,128)S(1)}, u32[]{:S(2)}, u32[]{:S(2)}) collective-permute-start(f32[136,128]{1,0:T(8,128)S(1)} %get-tuple-element.45.own_ref), channel_id=1, source_target_pairs={{0,1},{1,0},{2,3},{3,2},{4,5},{5,4},{6,7},{7,6},{8,9},{9,8},{10,11... | collective-permute-start | bytes 208904 | tf_op jit(solution)/shard_map/ppermute | solution.py:335
  31.0 6.6 %collective-permute-start.4 = (f32[8,128]{1,0:T(8,128)S(1)}, f32[8,128]{1,0:T(8,128)S(1)}, u32[]{:S(2)}, u32[]{:S(2)}) collective-permute-start(f32[8,128]{1,0:T(8,128)S(1)} %get-tuple-element.46), channel_id=1, source_target_pairs={{0,6},{1,7},{2,4},{3,5},{4,2},{5,3},{6,0},{7,1},{8,14},{9,15},{10,... | collective-permute-start | bytes 12296 | tf_op jit(solution)/shard_map/ppermute | solution.py:335
  38.2 8.5 %collective-permute-start.5 = (f32[136,128]{1,0:T(8,128)S(1)}, f32[136,128]{1,0:T(8,128)S(1)}, u32[]{:S(2)}, u32[]{:S(2)}) collective-permute-start(f32[136,128]{1,0:T(8,128)S(1)} %get-tuple-element.50), channel_id=1, source_target_pairs={{0,6},{1,7},{2,4},{3,5},{4,2},{5,3},{6,0},{7,1},{8,14},{9,15},{10,... | collective-permute-start | bytes 208904 | tf_op jit(solution)/shard_map/ppermute | solution.py:335
  72.0 8.0 %collective-permute-start.8 = (f32[136,128]{1,0:T(8,128)S(1)}, f32[136,128]{1,0:T(8,128)S(1)}, u32[]{:S(2)}, u32[]{:S(2)}) collective-permute-start(f32[136,128]{1,0:T(8,128)S(1)} %get-tuple-element.59.own_ref), channel_id=1, source_target_pairs={{0,3},{1,2},{2,1},{3,0},{4,7},{5,6},{6,5},{7,4},{8,11},{9,10},{10,... | collective-permute-start | bytes 208904 | tf_op jit(solution)/shard_map/ppermute | solution.py:335
  73.1 6.9 %collective-permute-start.7 = (f32[136,128]{1,0:T(8,128)S(1)}, f32[136,128]{1,0:T(8,128)S(1)}, u32[]{:S(2)}, u32[]{:S(2)}) collective-permute-start(f32[136,128]{1,0:T(8,128)S(1)} %get-tuple-element.59.own_ref), channel_id=1, source_target_pairs={{0,2},{1,3},{2,0},{3,1},{4,6},{5,7},{6,4},{7,5},{8,10},{9,11},{10,... | collective-permute-start | bytes 208904 | tf_op jit(solution)/shard_map/ppermute | solution.py:335
  74.9 5.1 %collective-permute-start.6 = (f32[136,128]{1,0:T(8,128)S(1)}, f32[136,128]{1,0:T(8,128)S(1)}, u32[]{:S(2)}, u32[]{:S(2)}) collective-permute-start(f32[136,128]{1,0:T(8,128)S(1)} %get-tuple-element.59.own_ref), channel_id=1, source_target_pairs={{0,1},{1,0},{2,3},{3,2},{4,5},{5,4},{6,7},{7,6},{8,9},{9,8},{10,11... | collective-permute-start | bytes 208904 | tf_op jit(solution)/shard_map/ppermute | solution.py:335
  80.5 7.3 %collective-permute-start.9 = (f32[136,128]{1,0:T(8,128)S(1)}, f32[136,128]{1,0:T(8,128)S(1)}, u32[]{:S(2)}, u32[]{:S(2)}) collective-permute-start(f32[136,128]{1,0:T(8,128)S(1)} %get-tuple-element.62.send_ref), channel_id=1, source_target_pairs={{0,6},{1,7},{2,4},{3,5},{4,2},{5,3},{6,0},{7,1},{8,14},{9,15},{10,... | collective-permute-start | bytes 208904 | tf_op jit(solution)/shard_map/ppermute | solution.py:335
  87.8 15.2 %collective-permute-start.10 = (f32[512,128]{1,0:T(8,128)S(1)}, f32[512,128]{1,0:T(8,128)S(1)}, u32[]{:S(2)}, u32[]{:S(2)}) collective-permute-start(f32[512,128]{1,0:T(8,128)S(1)} %get-tuple-element.69.inner_near_ref), channel_id=1, source_target_pairs={{0,6},{1,7},{2,4},{3,5},{4,2},{5,3},{6,0},{7,1},{8,14},{9,15},{10,... | collective-permute-start | bytes 786440 | tf_op jit(solution)/shard_map/ppermute | solution.py:335
  91.0 42.9 %copy-start.1 = (f32[64,128]{1,0:T(8,128)S(1)}, f32[64,128]{1,0:T(8,128)}, u32[]{:S(2)}) copy-start(f32[64,128]{1,0:T(8,128)} %ray_ref.3) | copy-start | bytes 98308
  115.5 8.0 %collective-permute-start.13 = (f32[136,128]{1,0:T(8,128)S(1)}, f32[136,128]{1,0:T(8,128)S(1)}, u32[]{:S(2)}, u32[]{:S(2)}) collective-permute-start(f32[136,128]{1,0:T(8,128)S(1)} %shard_map.87.own_ref), channel_id=1, source_target_pairs={{0,3},{1,2},{2,1},{3,0},{4,7},{5,6},{6,5},{7,4},{8,11},{9,10},{10,... | collective-permute-start | bytes 208904 | tf_op jit(solution)/shard_map/ppermute | solution.py:335
  116.6 6.9 %collective-permute-start.12 = (f32[136,128]{1,0:T(8,128)S(1)}, f32[136,128]{1,0:T(8,128)S(1)}, u32[]{:S(2)}, u32[]{:S(2)}) collective-permute-start(f32[136,128]{1,0:T(8,128)S(1)} %shard_map.87.own_ref), channel_id=1, source_target_pairs={{0,2},{1,3},{2,0},{3,1},{4,6},{5,7},{6,4},{7,5},{8,10},{9,11},{10,... | collective-permute-start | bytes 208904 | tf_op jit(solution)/shard_map/ppermute | solution.py:335
  118.4 5.1 %collective-permute-start.11 = (f32[136,128]{1,0:T(8,128)S(1)}, f32[136,128]{1,0:T(8,128)S(1)}, u32[]{:S(2)}, u32[]{:S(2)}) collective-permute-start(f32[136,128]{1,0:T(8,128)S(1)} %shard_map.87.own_ref), channel_id=1, source_target_pairs={{0,1},{1,0},{2,3},{3,2},{4,5},{5,4},{6,7},{7,6},{8,9},{9,8},{10,11... | collective-permute-start | bytes 208904 | tf_op jit(solution)/shard_map/ppermute | solution.py:335
  123.8 10.1 %collective-permute-start.14 = (f32[264,128]{1,0:T(8,128)S(1)}, f32[264,128]{1,0:T(8,128)S(1)}, u32[]{:S(2)}, u32[]{:S(2)}) collective-permute-start(f32[264,128]{1,0:T(8,128)S(1)} %shard_map.88.near_ref), channel_id=1, source_target_pairs={{0,6},{1,7},{2,4},{3,5},{4,2},{5,3},{6,0},{7,1},{8,14},{9,15},{10,... | collective-permute-start | bytes 405512 | tf_op jit(solution)/shard_map/ppermute | solution.py:335

commit v5 on v4

--- a/solution.py
+++ b/solution.py
@@ -1,3 +1,5 @@
+import functools
+
 import jax
 import jax.numpy as jnp
 from jax import lax
@@ -11,6 +13,7 @@
 N_VOX = 32
 N_ROW = 8
 CORES = 2
+HALF = TILE // 2
 CHIPS = N_VOX // CORES
 CHUNKS = 8
 PAD = 8
@@ -29,18 +32,24 @@
     return lax.broadcasted_iota(jnp.int32, shape, dim)
 
 
+def three_terms(values):
+    high = values.astype(BF16)
+    rest = values - high.astype(F32)
+    middle = rest.astype(BF16)
+    return high, middle, (rest - middle.astype(F32)).astype(BF16)
+
+
 def select_rows(choice, values):
-    high = values.astype(BF16)
-    middle = (values - high.astype(F32)).astype(BF16)
-    total = jnp.dot(choice, middle, preferred_element_type=F32)
-    return total + jnp.dot(choice, high, preferred_element_type=F32)
+    high, middle, low = three_terms(values)
+    small = jnp.dot(choice, jnp.concatenate([middle, low], axis=1), preferred_element_type=F32)
+    small = small[:, TILE:] + small[:, 0:TILE]
+    return small + jnp.dot(choice, high, preferred_element_type=F32)
 
 
 def select_columns(values, choice):
-    high = values.astype(BF16)
-    middle = (values - high.astype(F32)).astype(BF16)
-    total = jnp.dot(middle, choice, preferred_element_type=F32)
-    return total + jnp.dot(high, choice, preferred_element_type=F32)
+    rows = values.shape[0]
+    terms = jnp.dot(jnp.concatenate(three_terms(values), axis=0), choice, preferred_element_type=F32)
+    return (terms[2 * rows :, :] + terms[rows : 2 * rows, :]) + terms[0:rows, :]
 
 
 def one_hot(rows, index):
@@ -61,25 +70,29 @@
     pack_ref[2:3, :] = vox_ref[...]
 
 
-def relay_kernel(natural_ref, tiles_ref):
+def relay_kernel(natural_ref, tiles_ref, *, first):
     def step(index, unused):
-        block = natural_ref[:, pl.ds(pl.multiple_of(index * 8, 8), 8), :]
+        block = natural_ref[:, pl.ds(pl.multiple_of(first + index * 8, 8), 8), :]
         block = jnp.swapaxes(block, 0, 1)
         for inner in range(8):
             tiles_ref[index * 8 + inner] = jnp.transpose(block[inner])
         return unused
 
-    lax.fori_loop(0, TILE // 8, step, 0)
-
-
-def back_tiles(tiles_ref, weight_ref):
-    def step(index, total):
-        for inner in range(8):
-            ray = index * 8 + inner
-            total = total + tiles_ref[ray] * weight_ref[pl.ds(ray, 1), :]
-        return total
-
-    return lax.fori_loop(0, TILE // 8, step, jnp.zeros((TILE, TILE), F32))
+    lax.fori_loop(0, HALF // 8, step, 0)
+
+
+def back_tiles(low_ref, high_ref, weight_ref):
+    total = jnp.zeros((TILE, TILE), F32)
+    for first, tiles_ref in ((0, low_ref), (HALF, high_ref)):
+
+        def step(index, total):
+            for inner in range(8):
+                ray = index * 8 + inner
+                total = total + tiles_ref[ray] * weight_ref[pl.ds(first + ray, 1), :]
+            return total
+
+        total = lax.fori_loop(0, HALF // 8, step, total)
+    return total
 
 
 def write_tail(part_ref, vox_row, image, gamma, cross):
@@ -132,7 +145,7 @@
     for tile in range(TILE):
         index = place_ref[0, tile]
         here = index < half
-        row = jnp.where(here, index, index - half)
+        row = index & (half - 1)
         picked_ref[tile : tile + 1, :] = jnp.where(here, same_ref[pl.ds(row, 1), :], other_ref[pl.ds(row, 1), :])
     weight = jnp.transpose(picked_ref[...])
     for group in range(TILE // 8):
@@ -145,22 +158,22 @@
     share_ref[...] = jnp.transpose(part_ref[0:TILE, :])
 
 
-def back_share(received_ref, tiles_ref, row_ref, vox_ref, part_ref, weight_ref):
+def back_share(received_ref, low_ref, high_ref, row_ref, vox_ref, part_ref, weight_ref):
     received = received_ref[...]
     weight_ref[...] = select_columns(jnp.transpose(received), one_hot(SENT, row_ref[...]))
     heads = jnp.sum(received.reshape(N_VOX, PAD, TILE), axis=0)
-    share = back_tiles(tiles_ref, weight_ref)
+    share = back_tiles(low_ref, high_ref, weight_ref)
     part_ref[0:TILE, :] = jnp.transpose(share)
     write_tail(part_ref, vox_ref[...], *(heads[row : row + 1, :] for row in (NORM, LOCAL, OTHER)))
     return share
 
 
-def back_kernel(received_ref, tiles_ref, row_ref, vox_ref, part_ref, share_ref, weight_ref):
-    share_ref[...] = back_share(received_ref, tiles_ref, row_ref, vox_ref, part_ref, weight_ref)
-
-
-def back_last_kernel(received_ref, tiles_ref, row_ref, vox_ref, part_ref, weight_ref):
-    back_share(received_ref, tiles_ref, row_ref, vox_ref, part_ref, weight_ref)
+def back_kernel(received_ref, low_ref, high_ref, row_ref, vox_ref, part_ref, share_ref, weight_ref):
+    share_ref[...] = back_share(received_ref, low_ref, high_ref, row_ref, vox_ref, part_ref, weight_ref)
+
+
+def back_last_kernel(received_ref, low_ref, high_ref, row_ref, vox_ref, part_ref, weight_ref):
+    back_share(received_ref, low_ref, high_ref, row_ref, vox_ref, part_ref, weight_ref)
 
 
 def quad_sum(own_ref, one_ref, two_ref, three_ref):
@@ -201,15 +214,18 @@
     near_ref[VT_DEV:SUM, :] = tail
 
 
-def forward_tiles(values, share, tiles_ref, gamma_ref, sums_ref):
-    def step(index, unused):
-        for inner in range(8):
-            ray = index * 8 + inner
-            product = tiles_ref[ray] * values
-            sums_ref[pl.ds(pl.multiple_of(ray * 8, 8), 8), :] = jnp.sum(product.reshape(TILE // 8, 8, TILE), axis=0)
-        return unused
-
-    lax.fori_loop(0, TILE // 8, step, 0)
+def forward_tiles(values, share, low_ref, high_ref, gamma_ref, sums_ref):
+    for first, tiles_ref in ((0, low_ref), (HALF, high_ref)):
+
+        def step(index, unused):
+            for inner in range(8):
+                ray = index * 8 + inner
+                product = tiles_ref[ray] * values
+                row = pl.multiple_of((first + ray) * 8, 8)
+                sums_ref[pl.ds(row, 8), :] = jnp.sum(product.reshape(TILE // 8, 8, TILE), axis=0)
+            return unused
+
+        lax.fori_loop(0, HALF // 8, step, 0)
     gamma_ref[...] = jnp.broadcast_to(jnp.sum(values * share, axis=0, keepdims=True), (8, TILE))
     rays = sums_ref[pl.ds(0, TILE, stride=8), :]
     for inner in range(1, 8):
@@ -218,11 +234,11 @@
 
 
 def forward_first_kernel(
-    mine_ref, far_ref, share_ref, tiles_ref, row_ref, extra_ref, payload_ref, values_ref, gamma_ref, sums_ref
+    mine_ref, far_ref, share_ref, low_ref, high_ref, row_ref, extra_ref, payload_ref, values_ref, gamma_ref, sums_ref
 ):
     values = mine_ref[...] + far_ref[0:TILE, :]
     values_ref[...] = values
-    rays = forward_tiles(values, share_ref[...], tiles_ref, gamma_ref, sums_ref)
+    rays = forward_tiles(values, share_ref[...], low_ref, high_ref, gamma_ref, sums_ref)
     payload_ref[...] = select_rows(one_hot(SENT, row_ref[...]), rays) + extra_ref[...]
 
 
@@ -231,7 +247,7 @@
 
 
 def forward_kernel(
-    mine_ref, send_ref, far_ref, share_ref, values0_ref, share0_ref, tiles_ref, slot_ref,
+    mine_ref, send_ref, far_ref, share_ref, values0_ref, share0_ref, low_ref, high_ref, slot_ref,
     payload_ref, scalars_ref, gamma_ref, sums_ref,
 ):
     tail = send_ref[TILE:PART, :] + far_ref[TILE:PART, :]
@@ -241,7 +257,7 @@
     scalars_ref[...] = jnp.where(sub == 0, gamma, jnp.where(sub == 1, square, step))
     values = values0_ref[...] - step * (mine_ref[...] + far_ref[0:TILE, :])
     share = share0_ref[...] - step * share_ref[...]
-    rays = forward_tiles(values, share, tiles_ref, gamma_ref, sums_ref)
+    rays = forward_tiles(values, share, low_ref, high_ref, gamma_ref, sums_ref)
     payload_ref[...] = select_rows(one_hot(TILE, slot_ref[...]), rays)
 
 
@@ -362,23 +378,29 @@
         limit=42,
     )
     ids = across(ids, 6)
-    near, mine, send = call(quad_first_kernel, [field, block, part], [], (*quad(own), ids))
+    def relay(natural, first):
+        return call(
+            functools.partial(relay_kernel, first=first),
+            [(HALF, TILE, TILE)],
+            [],
+            (natural,),
+            cost=pl.CostEstimate(flops=0, bytes_accessed=2**23, transcendentals=0),
+        )[0]
+
+    messages = quad(own)
+    low = relay(natural, 0)
+    messages, ids, low = lax.optimization_barrier((messages, ids, low))
+    near, mine, send = call(quad_first_kernel, [field, block, part], [], (*messages, ids))
     send, natural = lax.optimization_barrier((send, natural))
     far = across(send, 6)
-    (tiles,) = call(
-        relay_kernel,
-        [(TILE, TILE, TILE)],
-        [],
-        (natural,),
-        cost=pl.CostEstimate(flops=0, bytes_accessed=2**24, transcendentals=0),
-    )
+    high = relay(natural, HALF)
     payload, values0, gamma = call(
-        forward_first_kernel, [sent, block, scalar], [sums], (mine, far, share0, tiles, slot_row, extra)
+        forward_first_kernel, [sent, block, scalar], [sums], (mine, far, share0, low, high, slot_row, extra)
     )
     payload, image0, choice, compact = call(
         owner_first_kernel, [sent, rays, sent, block], [], (over_vox(payload), gamma)
     )
-    own, share = call(back_kernel, [part, block], [block], (over_vox(payload), tiles, slot_row, vox_row))
+    own, share = call(back_kernel, [part, block], [block], (over_vox(payload), low, high, slot_row, vox_row))
     near, mine, send = call(
         quad_kernel, [(2 * VT_DEV, TILE), block, part], [], (*quad(own), ids, near)
     )
@@ -388,11 +410,11 @@
         forward_kernel,
         [block, scalar, scalar],
         [sums],
-        (mine, send, far, share, values0, share0, tiles, slot),
+        (mine, send, far, share, values0, share0, low, high, slot),
     )
     received, inner_far = lax.optimization_barrier((over_vox(payload), inner_far))
     payload, image1 = call(owner_kernel, [sent, rays], [], (received, gamma, image0, choice, compact))
-    (own,) = call(back_last_kernel, [part], [block], (over_vox(payload), tiles, slot_row, vox_row))
+    (own,) = call(back_last_kernel, [part], [block], (over_vox(payload), low, high, slot_row, vox_row))
     (last,) = call(quad_last_kernel, [(SUM, TILE)], [], quad(own))
     return tuple(
         call(

time: 135 us -> 136 us (level)
    pallas_call x14 -> x15, Pallas kernels: 16 us -> 16.4 us  [call(): pl.pallas_call(kernel, out_shape=outs, in_specs=specs + [vmem] * (len(arg...]
where the time goes in v5:
time: 136 us; the launch traced here: 135 us
  blocking collectives  63 us (46%)
  starting transfers between devices  30.7 us (23%)
  waiting for transfers between devices  21.6 us (16%)
  Pallas kernels  16.4 us (12%)
  local copies, waits for them, and re-layouts  2.72 us (2%)
    all_to_all x4, blocking collectives, over_vox(): return lax.all_to_all(array, 'vox', 0, 0, tiled=True)  44.7 us
    ppermute x14, starting transfers between devices, across(): lax.ppermute(array, 'row', [(index, index ^ distance) for index in range(...  30.7 us
    ppermute x14, waiting for transfers between devices, across(): lax.ppermute(array, 'row', [(index, index ^ distance) for index in range(...  21.6 us
    all_to_all x1, blocking collectives, local(): lax.all_to_all(copies, 'vox', 0, 0, tiled=True, axis_index_groups=chips)  18.3 us
    pallas_call x15, Pallas kernels, call(): pl.pallas_call(kernel, out_shape=outs, in_specs=specs + [vmem] * (len(arg...  16.4 us
    unnamed x10, local copies, waits for them, and re-layouts  2.72 us
  transfers between devices with their start and end apart: 15, of which 5 were waited for; matrix products, arithmetic and copies ran while one was open for 0% of the time, Pallas kernels for 4%

profile of v5, /device:TPU:32, one launch (start us, length us, event | category | flops | bytes accessed | tf_op | source)
XLA Modules:
  0.0 135.2 jit_solution(2106015908740361524)
XLA Ops:
  0.6 0.0 copy-start
  0.6 0.7 copy-done
  1.4 18.3 %all_to_all.57 = f32[16,64,128]{2,1,0:T(8,128)S(1)} all-to-all(f32[16,64,128]{2,1,0:T(8,128)S(1)} %bitcast.14), channel_id=1, replica_groups={{0,16,32,48,64,80,96,112,128,144,160,176,192,208,224,240},{8,24,40,56,7..., dimensions={0} | all-to-all | bytes 1048576 | tf_op jit(solution)/shard_map/all_to_all | solution.py:358
  19.8 0.0 collective-permute-start
  19.8 0.7 copy-done.2
  20.4 0.7 copy-done.3
  21.1 0.7 copy-done.4
  21.7 0.0 collective-permute-done.other_ref
  21.7 4.4 %shard_map.78 = (f32[136,128]{1,0:T(8,128)S(1)}, f32[128,128]{1,0:T(8,128)S(1)}, f32[128,128,128]{2,1,0:T(8,128)S(1)}, s32[1,128]{1,0:T(1,128)S(1)}, s32[1,128]{...) custom-call(f32[128,128,128]{2,1,0:T(8,128)} %tiles_hbm.1, ...), custom_call_target="tpu_custom_call" | custom-call | tf_op jit(solution)/shard_map/pallas_call | solution.py:325
  26.2 2.0 %collective-permute-start.3 = (f32[136,128]{1,0:T(8,128)S(1)}, f32[136,128]{1,0:T(8,128)S(1)}, u32[]{:S(2)}, u32[]{:S(2)}) collective-permute-start(f32[136,128]{1,0:T(8,128)S(1)} %get-tuple-element.54.own_ref), channel_id=1, source_target_pairs={{0,3},{1,2},{2,1},{3,0},{4,7},{5,6},{6,5},{7,4},{8,11},{9,10},{10,... | collective-permute-start | bytes 208904 | tf_op jit(solution)/shard_map/ppermute | solution.py:351
  28.2 1.5 %collective-permute-start.2 = (f32[136,128]{1,0:T(8,128)S(1)}, f32[136,128]{1,0:T(8,128)S(1)}, u32[]{:S(2)}, u32[]{:S(2)}) collective-permute-start(f32[136,128]{1,0:T(8,128)S(1)} %get-tuple-element.54.own_ref), channel_id=1, source_target_pairs={{0,2},{1,3},{2,0},{3,1},{4,6},{5,7},{6,4},{7,5},{8,10},{9,11},{10,... | collective-permute-start | bytes 208904 | tf_op jit(solution)/shard_map/ppermute | solution.py:351
  29.7 1.4 %collective-permute-start.1 = (f32[136,128]{1,0:T(8,128)S(1)}, f32[136,128]{1,0:T(8,128)S(1)}, u32[]{:S(2)}, u32[]{:S(2)}) collective-permute-start(f32[136,128]{1,0:T(8,128)S(1)} %get-tuple-element.54.own_ref), channel_id=1, source_target_pairs={{0,1},{1,0},{2,3},{3,2},{4,5},{5,4},{6,7},{7,6},{8,9},{9,8},{10,11... | collective-permute-start | bytes 208904 | tf_op jit(solution)/shard_map/ppermute | solution.py:351
  31.0 5.1 %collective-permute-start.4 = (f32[8,128]{1,0:T(8,128)S(1)}, f32[8,128]{1,0:T(8,128)S(1)}, u32[]{:S(2)}, u32[]{:S(2)}) collective-permute-start(f32[8,128]{1,0:T(8,128)S(1)} %get-tuple-element.52), channel_id=1, source_target_pairs={{0,6},{1,7},{2,4},{3,5},{4,2},{5,3},{6,0},{7,1},{8,14},{9,15},{10,... | collective-permute-start | bytes 12296 | tf_op jit(solution)/shard_map/ppermute | solution.py:351
  36.1 2.1 %shard_map.79.low_ref = f32[64,128,128]{2,1,0:T(8,128)S(1)} custom-call(f32[128,128,128]{2,1,0:T(8,128)S(1)} %get-tuple-element.64.natural_ref), custom_call_target="tpu_custom_call" | custom-call | bytes 8388608 | tf_op jit(solution)/shard_map/pallas_call | solution.py:325
  38.2 0.0 collective-permute-done.4.ids_ref
  38.2 0.0 collective-permute-done.3.three_ref
  38.2 0.0 collective-permute-done.1.one_ref
  38.2 0.7 shard_map.80
  38.9 3.7 %collective-permute-start.5 = (f32[136,128]{1,0:T(8,128)S(1)}, f32[136,128]{1,0:T(8,128)S(1)}, u32[]{:S(2)}, u32[]{:S(2)}) collective-permute-start(f32[136,128]{1,0:T(8,128)S(1)} %get-tuple-element.61), channel_id=1, source_target_pairs={{0,6},{1,7},{2,4},{3,5},{4,2},{5,3},{6,0},{7,1},{8,14},{9,15},{10,... | collective-permute-start | bytes 208904 | tf_op jit(solution)/shard_map/ppermute | solution.py:351
  42.6 2.1 %shard_map.81.high_ref = f32[64,128,128]{2,1,0:T(8,128)S(1)} custom-call(f32[128,128,128]{2,1,0:T(8,128)S(1)} %get-tuple-element.64.natural_ref), custom_call_target="tpu_custom_call" | custom-call | bytes 8388608 | tf_op jit(solution)/shard_map/pallas_call | solution.py:325
  44.7 2.2 %collective-permute-done.5.far_ref = f32[136,128]{1,0:T(8,128)S(1)} collective-permute-done((f32[136,128]{1,0:T(8,128)S(1)}, f32[136,128]{1,0:T(8,128)S(1)}, u32[]{:S(2)}, u32[]{:S(2)}) %collective-permute-start.5) | collective-permute-done | bytes 69664 | tf_op jit(solution)/shard_map/ppermute | solution.py:351
  46.9 1.1 shard_map.82
  48.0 11.4 %all_to_all.58 = f32[32,8,128]{2,1,0:T(8,128)S(1)} all-to-all(f32[32,8,128]{2,1,0:T(8,128)S(1)} %bitcast.19), channel_id=1, replica_groups=mesh['vox'=32,'row'=8] {'vox'}, dimensions={0} | all-to-all | bytes 262144 | tf_op jit(solution)/shard_map/all_to_all | solution.py:348
  59.4 0.5 shard_map.83
  59.9 11.3 %all_to_all.59 = f32[32,8,128]{2,1,0:T(8,128)S(1)} all-to-all(f32[32,8,128]{2,1,0:T(8,128)S(1)} %bitcast.20), channel_id=1, replica_groups=mesh['vox'=32,'row'=8] {'vox'}, dimensions={0} | all-to-all | bytes 262144 | tf_op jit(solution)/shard_map/all_to_all | solution.py:348
  71.2 1.0 shard_map.84
  72.2 1.1 collective-permute-start.8
  73.3 1.7 %collective-permute-start.7 = (f32[136,128]{1,0:T(8,128)S(1)}, f32[136,128]{1,0:T(8,128)S(1)}, u32[]{:S(2)}, u32[]{:S(2)}) collective-permute-start(f32[136,128]{1,0:T(8,128)S(1)} %get-tuple-element.71.own_ref), channel_id=1, source_target_pairs={{0,2},{1,3},{2,0},{3,1},{4,6},{5,7},{6,4},{7,5},{8,10},{9,11},{10,... | collective-permute-start | bytes 208904 | tf_op jit(solution)/shard_map/ppermute | solution.py:351
  75.0 0.8 collective-permute-start.6
  75.8 4.4 %collective-permute-done.8.three_ref = f32[136,128]{1,0:T(8,128)S(1)} collective-permute-done((f32[136,128]{1,0:T(8,128)S(1)}, f32[136,128]{1,0:T(8,128)S(1)}, u32[]{:S(2)}, u32[]{:S(2)}) %collective-permute-start.8) | collective-permute-done | bytes 69664 | tf_op jit(solution)/shard_map/ppermute | solution.py:351
  80.2 0.0 collective-permute-done.7.two_ref
  80.2 0.7 shard_map.85
  80.9 4.0 %collective-permute-start.9 = (f32[136,128]{1,0:T(8,128)S(1)}, f32[136,128]{1,0:T(8,128)S(1)}, u32[]{:S(2)}, u32[]{:S(2)}) collective-permute-start(f32[136,128]{1,0:T(8,128)S(1)} %get-tuple-element.74.send_ref), channel_id=1, source_target_pairs={{0,6},{1,7},{2,4},{3,5},{4,2},{5,3},{6,0},{7,1},{8,14},{9,15},{10,... | collective-permute-start | bytes 208904 | tf_op jit(solution)/shard_map/ppermute | solution.py:351
  84.9 3.3 %collective-permute-done.9.far_ref = f32[136,128]{1,0:T(8,128)S(1)} collective-permute-done((f32[136,128]{1,0:T(8,128)S(1)}, f32[136,128]{1,0:T(8,128)S(1)}, u32[]{:S(2)}, u32[]{:S(2)}) %collective-permute-start.9) | collective-permute-done | bytes 69664 | tf_op jit(solution)/shard_map/ppermute | solution.py:351
  88.2 3.2 %collective-permute-start.10 = (f32[512,128]{1,0:T(8,128)S(1)}, f32[512,128]{1,0:T(8,128)S(1)}, u32[]{:S(2)}, u32[]{:S(2)}) collective-permute-start(f32[512,128]{1,0:T(8,128)S(1)} %get-tuple-element.81.inner_near_ref), channel_id=1, source_target_pairs={{0,6},{1,7},{2,4},{3,5},{4,2},{5,3},{6,0},{7,1},{8,14},{9,15},{10,... | collective-permute-start | bytes 786440 | tf_op jit(solution)/shard_map/ppermute | solution.py:351
  91.3 1.2 shard_map.86
  92.5 10.8 %all_to_all.60 = f32[32,4,128]{2,1,0:T(4,128)S(1)} all-to-all(f32[32,4,128]{2,1,0:T(4,128)S(1)} %bitcast.22), channel_id=1, replica_groups=mesh['vox'=32,'row'=8] {'vox'}, dimensions={0} | all-to-all | bytes 131072 | tf_op jit(solution)/shard_map/all_to_all | solution.py:348
  103.3 0.4 shard_map.87
  103.7 11.2 %all_to_all.61 = f32[32,8,128]{2,1,0:T(8,128)S(1)} all-to-all(f32[32,8,128]{2,1,0:T(8,128)S(1)} %bitcast.21), channel_id=1, replica_groups=mesh['vox'=32,'row'=8] {'vox'}, dimensions={0} | all-to-all | bytes 262144 | tf_op jit(solution)/shard_map/all_to_all | solution.py:348
  114.9 1.0 shard_map.88.own_ref
  115.9 1.1 collective-permute-start.13
  117.0 1.8 %collective-permute-start.12 = (f32[136,128]{1,0:T(8,128)S(1)}, f32[136,128]{1,0:T(8,128)S(1)}, u32[]{:S(2)}, u32[]{:S(2)}) collective-permute-start(f32[136,128]{1,0:T(8,128)S(1)} %shard_map.88.own_ref), channel_id=1, source_target_pairs={{0,2},{1,3},{2,0},{3,1},{4,6},{5,7},{6,4},{7,5},{8,10},{9,11},{10,... | collective-permute-start | bytes 208904 | tf_op jit(solution)/shard_map/ppermute | solution.py:351
  118.8 0.7 collective-permute-start.11
  119.5 4.4 %collective-permute-done.13.three_ref = f32[136,128]{1,0:T(8,128)S(1)} collective-permute-done((f32[136,128]{1,0:T(8,128)S(1)}, f32[136,128]{1,0:T(8,128)S(1)}, u32[]{:S(2)}, u32[]{:S(2)}) %collective-permute-start.13) | collective-permute-done | bytes 69664 | tf_op jit(solution)/shard_map/ppermute | solution.py:351
  123.9 0.4 shard_map.89.near_ref
  124.3 2.9 %collective-permute-start.14 = (f32[264,128]{1,0:T(8,128)S(1)}, f32[264,128]{1,0:T(8,128)S(1)}, u32[]{:S(2)}, u32[]{:S(2)}) collective-permute-start(f32[264,128]{1,0:T(8,128)S(1)} %shard_map.89.near_ref), channel_id=1, source_target_pairs={{0,6},{1,7},{2,4},{3,5},{4,2},{5,3},{6,0},{7,1},{8,14},{9,15},{10,... | collective-permute-start | bytes 405512 | tf_op jit(solution)/shard_map/ppermute | solution.py:351
  127.1 7.2 %collective-permute-done.14.far_ref = f32[264,128]{1,0:T(8,128)S(1)} collective-permute-done((f32[264,128]{1,0:T(8,128)S(1)}, f32[264,128]{1,0:T(8,128)S(1)}, u32[]{:S(2)}, u32[]{:S(2)}) %collective-permute-start.14) | collective-permute-done | bytes 135200 | tf_op jit(solution)/shard_map/ppermute | solution.py:351
  134.4 0.8 shard_map.90
  (12 shorter events, 0.1 us)
Async XLA Ops:
  0.6 0.8 copy-start
  19.8 2.0 %collective-permute-start = (f32[1024,128]{1,0:T(8,128)S(1)}, f32[1024,128]{1,0:T(8,128)S(1)}, u32[]{:S(2)}, u32[]{:S(2)}) collective-permute-start(f32[1024,128]{1,0:T(8,128)S(1)} %bitcast.12), channel_id=1, source_target_pairs={{0,8},{8,0},{16,24},{24,16},{32,40},{40,32},{48,56},{56,48},{64,72... | collective-permute-start | bytes 1572872 | tf_op jit(solution)/shard_map/ppermute | solution.py:360
  19.8 0.7 copy-start.2
  20.4 0.7 copy-start.3
  21.1 0.7 copy-start.4
  26.2 12.0 %collective-permute-start.3 = (f32[136,128]{1,0:T(8,128)S(1)}, f32[136,128]{1,0:T(8,128)S(1)}, u32[]{:S(2)}, u32[]{:S(2)}) collective-permute-start(f32[136,128]{1,0:T(8,128)S(1)} %get-tuple-element.54.own_ref), channel_id=1, source_target_pairs={{0,3},{1,2},{2,1},{3,0},{4,7},{5,6},{6,5},{7,4},{8,11},{9,10},{10,... | collective-permute-start | bytes 208904 | tf_op jit(solution)/shard_map/ppermute | solution.py:351
  28.2 10.0 %collective-permute-start.2 = (f32[136,128]{1,0:T(8,128)S(1)}, f32[136,128]{1,0:T(8,128)S(1)}, u32[]{:S(2)}, u32[]{:S(2)}) collective-permute-start(f32[136,128]{1,0:T(8,128)S(1)} %get-tuple-element.54.own_ref), channel_id=1, source_target_pairs={{0,2},{1,3},{2,0},{3,1},{4,6},{5,7},{6,4},{7,5},{8,10},{9,11},{10,... | collective-permute-start | bytes 208904 | tf_op jit(solution)/shard_map/ppermute | solution.py:351
  29.7 8.6 %collective-permute-start.1 = (f32[136,128]{1,0:T(8,128)S(1)}, f32[136,128]{1,0:T(8,128)S(1)}, u32[]{:S(2)}, u32[]{:S(2)}) collective-permute-start(f32[136,128]{1,0:T(8,128)S(1)} %get-tuple-element.54.own_ref), channel_id=1, source_target_pairs={{0,1},{1,0},{2,3},{3,2},{4,5},{5,4},{6,7},{7,6},{8,9},{9,8},{10,11... | collective-permute-start | bytes 208904 | tf_op jit(solution)/shard_map/ppermute | solution.py:351
  31.0 7.2 %collective-permute-start.4 = (f32[8,128]{1,0:T(8,128)S(1)}, f32[8,128]{1,0:T(8,128)S(1)}, u32[]{:S(2)}, u32[]{:S(2)}) collective-permute-start(f32[8,128]{1,0:T(8,128)S(1)} %get-tuple-element.52), channel_id=1, source_target_pairs={{0,6},{1,7},{2,4},{3,5},{4,2},{5,3},{6,0},{7,1},{8,14},{9,15},{10,... | collective-permute-start | bytes 12296 | tf_op jit(solution)/shard_map/ppermute | solution.py:351
  38.9 8.0 %collective-permute-start.5 = (f32[136,128]{1,0:T(8,128)S(1)}, f32[136,128]{1,0:T(8,128)S(1)}, u32[]{:S(2)}, u32[]{:S(2)}) collective-permute-start(f32[136,128]{1,0:T(8,128)S(1)} %get-tuple-element.61), channel_id=1, source_target_pairs={{0,6},{1,7},{2,4},{3,5},{4,2},{5,3},{6,0},{7,1},{8,14},{9,15},{10,... | collective-permute-start | bytes 208904 | tf_op jit(solution)/shard_map/ppermute | solution.py:351
  72.2 8.0 %collective-permute-start.8 = (f32[136,128]{1,0:T(8,128)S(1)}, f32[136,128]{1,0:T(8,128)S(1)}, u32[]{:S(2)}, u32[]{:S(2)}) collective-permute-start(f32[136,128]{1,0:T(8,128)S(1)} %get-tuple-element.71.own_ref), channel_id=1, source_target_pairs={{0,3},{1,2},{2,1},{3,0},{4,7},{5,6},{6,5},{7,4},{8,11},{9,10},{10,... | collective-permute-start | bytes 208904 | tf_op jit(solution)/shard_map/ppermute | solution.py:351
  73.3 6.9 %collective-permute-start.7 = (f32[136,128]{1,0:T(8,128)S(1)}, f32[136,128]{1,0:T(8,128)S(1)}, u32[]{:S(2)}, u32[]{:S(2)}) collective-permute-start(f32[136,128]{1,0:T(8,128)S(1)} %get-tuple-element.71.own_ref), channel_id=1, source_target_pairs={{0,2},{1,3},{2,0},{3,1},{4,6},{5,7},{6,4},{7,5},{8,10},{9,11},{10,... | collective-permute-start | bytes 208904 | tf_op jit(solution)/shard_map/ppermute | solution.py:351
  75.0 5.2 %collective-permute-start.6 = (f32[136,128]{1,0:T(8,128)S(1)}, f32[136,128]{1,0:T(8,128)S(1)}, u32[]{:S(2)}, u32[]{:S(2)}) collective-permute-start(f32[136,128]{1,0:T(8,128)S(1)} %get-tuple-element.71.own_ref), channel_id=1, source_target_pairs={{0,1},{1,0},{2,3},{3,2},{4,5},{5,4},{6,7},{7,6},{8,9},{9,8},{10,11... | collective-permute-start | bytes 208904 | tf_op jit(solution)/shard_map/ppermute | solution.py:351
  80.9 7.3 %collective-permute-start.9 = (f32[136,128]{1,0:T(8,128)S(1)}, f32[136,128]{1,0:T(8,128)S(1)}, u32[]{:S(2)}, u32[]{:S(2)}) collective-permute-start(f32[136,128]{1,0:T(8,128)S(1)} %get-tuple-element.74.send_ref), channel_id=1, source_target_pairs={{0,6},{1,7},{2,4},{3,5},{4,2},{5,3},{6,0},{7,1},{8,14},{9,15},{10,... | collective-permute-start | bytes 208904 | tf_op jit(solution)/shard_map/ppermute | solution.py:351
  88.2 15.1 %collective-permute-start.10 = (f32[512,128]{1,0:T(8,128)S(1)}, f32[512,128]{1,0:T(8,128)S(1)}, u32[]{:S(2)}, u32[]{:S(2)}) collective-permute-start(f32[512,128]{1,0:T(8,128)S(1)} %get-tuple-element.81.inner_near_ref), channel_id=1, source_target_pairs={{0,6},{1,7},{2,4},{3,5},{4,2},{5,3},{6,0},{7,1},{8,14},{9,15},{10,... | collective-permute-start | bytes 786440 | tf_op jit(solution)/shard_map/ppermute | solution.py:351
  91.3 43.0 %copy-start.1 = (f32[64,128]{1,0:T(8,128)S(1)}, f32[64,128]{1,0:T(8,128)}, u32[]{:S(2)}) copy-start(f32[64,128]{1,0:T(8,128)} %ray_ref.3) | copy-start | bytes 98308
  115.9 8.0 %collective-permute-start.13 = (f32[136,128]{1,0:T(8,128)S(1)}, f32[136,128]{1,0:T(8,128)S(1)}, u32[]{:S(2)}, u32[]{:S(2)}) collective-permute-start(f32[136,128]{1,0:T(8,128)S(1)} %shard_map.88.own_ref), channel_id=1, source_target_pairs={{0,3},{1,2},{2,1},{3,0},{4,7},{5,6},{6,5},{7,4},{8,11},{9,10},{10,... | collective-permute-start | bytes 208904 | tf_op jit(solution)/shard_map/ppermute | solution.py:351
  117.0 6.9 %collective-permute-start.12 = (f32[136,128]{1,0:T(8,128)S(1)}, f32[136,128]{1,0:T(8,128)S(1)}, u32[]{:S(2)}, u32[]{:S(2)}) collective-permute-start(f32[136,128]{1,0:T(8,128)S(1)} %shard_map.88.own_ref), channel_id=1, source_target_pairs={{0,2},{1,3},{2,0},{3,1},{4,6},{5,7},{6,4},{7,5},{8,10},{9,11},{10,... | collective-permute-start | bytes 208904 | tf_op jit(solution)/shard_map/ppermute | solution.py:351
  118.8 5.1 %collective-permute-start.11 = (f32[136,128]{1,0:T(8,128)S(1)}, f32[136,128]{1,0:T(8,128)S(1)}, u32[]{:S(2)}, u32[]{:S(2)}) collective-permute-start(f32[136,128]{1,0:T(8,128)S(1)} %shard_map.88.own_ref), channel_id=1, source_target_pairs={{0,1},{1,0},{2,3},{3,2},{4,5},{5,4},{6,7},{7,6},{8,9},{9,8},{10,11... | collective-permute-start | bytes 208904 | tf_op jit(solution)/shard_map/ppermute | solution.py:351
  124.3 10.1 %collective-permute-start.14 = (f32[264,128]{1,0:T(8,128)S(1)}, f32[264,128]{1,0:T(8,128)S(1)}, u32[]{:S(2)}, u32[]{:S(2)}) collective-permute-start(f32[264,128]{1,0:T(8,128)S(1)} %shard_map.89.near_ref), channel_id=1, source_target_pairs={{0,6},{1,7},{2,4},{3,5},{4,2},{5,3},{6,0},{7,1},{8,14},{9,15},{10,... | collective-permute-start | bytes 405512 | tf_op jit(solution)/shard_map/ppermute | solution.py:351

commit v6 on v5

--- a/solution.py
+++ b/solution.py
@@ -107,7 +107,7 @@
 def back_first_kernel(
     tiles_hbm, same_ref, other_ref, pack_ref,
     part_ref, share_ref, natural_ref, row_ref, slot_ref, vox_ref, extra_ref, ids_ref,
-    picked_ref, index_ref, place_ref, sems,
+    picked_ref, sums_ref, index_ref, place_ref, sems,
 ):
     size = TILE // CHUNKS
     moves = []
@@ -151,11 +151,14 @@
     for group in range(TILE // 8):
         if group * 8 % size == 0:
             moves[group * 8 // size].wait()
-        rows = []
         for tile in range(group * 8, group * 8 + 8):
-            rows.append(jnp.sum(natural_ref[tile] * weight[:, tile : tile + 1], axis=0, keepdims=True))
-        part_ref[group * 8 : group * 8 + 8, :] = jnp.concatenate(rows, axis=0)
-    share_ref[...] = jnp.transpose(part_ref[0:TILE, :])
+            product = natural_ref[tile] * weight[:, tile : tile + 1]
+            sums_ref[tile * 8 : tile * 8 + 8, :] = jnp.sum(product.reshape(TILE // 8, 8, TILE), axis=0)
+    share = sums_ref[pl.ds(0, TILE, stride=8), :]
+    for inner in range(1, 8):
+        share = share + sums_ref[pl.ds(inner, TILE, stride=8), :]
+    part_ref[0:TILE, :] = share
+    share_ref[...] = jnp.transpose(share)
 
 
 def back_share(received_ref, low_ref, high_ref, row_ref, vox_ref, part_ref, weight_ref):
@@ -176,12 +179,17 @@
     back_share(received_ref, low_ref, high_ref, row_ref, vox_ref, part_ref, weight_ref)
 
 
-def quad_sum(own_ref, one_ref, two_ref, three_ref):
-    def spread(ref):
-        where = ref[TILE + IDS : TILE + IDS + 1, :].astype(jnp.int32)
-        return select_rows(one_hot(VT_DEV, where), ref[0:TILE, :])
-
-    field = (spread(own_ref) + spread(one_ref)) + (spread(two_ref) + spread(three_ref))
+def spread(ref):
+    where = ref[TILE + IDS : TILE + IDS + 1, :].astype(jnp.int32)
+    return select_rows(one_hot(VT_DEV, where), ref[0:TILE, :])
+
+
+def spread_kernel(own_ref, spread_ref):
+    spread_ref[...] = spread(own_ref)
+
+
+def quad_sum(own_ref, spread_ref, one_ref, two_ref, three_ref):
+    field = (spread_ref[...] + spread(one_ref)) + (spread(two_ref) + spread(three_ref))
     tail = slice(TILE, PART)
     return field, (own_ref[tail, :] + one_ref[tail, :]) + (two_ref[tail, :] + three_ref[tail, :])
 
@@ -195,21 +203,21 @@
     send_ref[TILE:PART, :] = tail
 
 
-def quad_first_kernel(own_ref, one_ref, two_ref, three_ref, ids_ref, near_ref, mine_ref, send_ref):
-    field, tail = quad_sum(own_ref, one_ref, two_ref, three_ref)
+def quad_first_kernel(own_ref, spread_ref, one_ref, two_ref, three_ref, ids_ref, near_ref, mine_ref, send_ref):
+    field, tail = quad_sum(own_ref, spread_ref, one_ref, two_ref, three_ref)
     read_tiles(field, tail, own_ref, ids_ref, mine_ref, send_ref)
     near_ref[...] = field
 
 
-def quad_kernel(own_ref, one_ref, two_ref, three_ref, ids_ref, before_ref, near_ref, mine_ref, send_ref):
-    field, tail = quad_sum(own_ref, one_ref, two_ref, three_ref)
+def quad_kernel(own_ref, spread_ref, one_ref, two_ref, three_ref, ids_ref, before_ref, near_ref, mine_ref, send_ref):
+    field, tail = quad_sum(own_ref, spread_ref, one_ref, two_ref, three_ref)
     read_tiles(field, tail, own_ref, ids_ref, mine_ref, send_ref)
     near_ref[0:VT_DEV, :] = before_ref[...]
     near_ref[VT_DEV:, :] = field
 
 
-def quad_last_kernel(own_ref, one_ref, two_ref, three_ref, near_ref):
-    field, tail = quad_sum(own_ref, one_ref, two_ref, three_ref)
+def quad_last_kernel(own_ref, spread_ref, one_ref, two_ref, three_ref, near_ref):
+    field, tail = quad_sum(own_ref, spread_ref, one_ref, two_ref, three_ref)
     near_ref[0:VT_DEV, :] = field
     near_ref[VT_DEV:SUM, :] = tail
 
@@ -351,7 +359,10 @@
         return lax.ppermute(array, "row", [(index, index ^ distance) for index in range(N_ROW)])
 
     def quad(own):
-        return (own, *(across(own, distance) for distance in (1, 2, 3)))
+        others = [across(own, distance) for distance in (1, 2, 3)]
+        cost = pl.CostEstimate(flops=0, bytes_accessed=2**22, transcendentals=0)
+        (own_field,) = call(spread_kernel, [field], [], (own,), cost=cost)
+        return (own, own_field, *others)
 
     (copies,) = call(copies_kernel, [(CHIPS * owned, TILE)], [], (ray_data,))
     chips = [[chip * CORES + core for chip in range(CHIPS)] for core in range(CORES)]
@@ -369,6 +380,7 @@
         [part, block, (TILE, TILE, TILE), indices, indices, indices, sent, scalar],
         [
             block,
+            sums,
             pltpu.VMEM((1, TILE), jnp.int32),
             pltpu.SMEM((1, TILE), jnp.int32),
             pltpu.SemaphoreType.DMA((CHUNKS + 1,)),

time: 136 us -> 135 us (level)
    pallas_call x15 -> x18, Pallas kernels: 16.4 us -> 16.7 us  [call(): pl.pallas_call(kernel, out_shape=outs, in_specs=specs + [vmem] * (len(arg...]
where the time goes in v6:
time: 135 us
  blocking collectives  63 us (47%)
  starting transfers between devices  30.5 us (23%)
  waiting for transfers between devices  21.1 us (16%)
  Pallas kernels  16.7 us (12%)
  local copies, waits for them, and re-layouts  2.72 us (2%)
    all_to_all x4, blocking collectives, over_vox(): return lax.all_to_all(array, 'vox', 0, 0, tiled=True)  44.7 us
    ppermute x14, starting transfers between devices, across(): lax.ppermute(array, 'row', [(index, index ^ distance) for index in range(...  30.5 us
    ppermute x14, waiting for transfers between devices, across(): lax.ppermute(array, 'row', [(index, index ^ distance) for index in range(...  21.1 us
    all_to_all x1, blocking collectives, local(): lax.all_to_all(copies, 'vox', 0, 0, tiled=True, axis_index_groups=chips)  18.3 us
    pallas_call x18, Pallas kernels, call(): pl.pallas_call(kernel, out_shape=outs, in_specs=specs + [vmem] * (len(arg...  16.7 us
    unnamed x10, local copies, waits for them, and re-layouts  2.72 us
  transfers between devices with their start and end apart: 15, of which 5 were waited for; matrix products, arithmetic and copies ran while one was open for 0% of the time, Pallas kernels for 4%

profile of v6, /device:TPU:32, one launch (start us, length us, event | category | flops | bytes accessed | tf_op | source)
XLA Modules:
  0.0 134.9 jit_solution(4526230533776089894)
XLA Ops:
  0.6 0.0 copy-start
  0.6 0.7 copy-done
  1.4 18.3 %all_to_all.57 = f32[16,64,128]{2,1,0:T(8,128)S(1)} all-to-all(f32[16,64,128]{2,1,0:T(8,128)S(1)} %bitcast.14), channel_id=1, replica_groups={{0,16,32,48,64,80,96,112,128,144,160,176,192,208,224,240},{8,24,40,56,7..., dimensions={0} | all-to-all | bytes 1048576 | tf_op jit(solution)/shard_map/all_to_all | solution.py:369
  19.8 0.7 copy-done.2
  20.4 0.7 copy-done.3
  21.1 0.7 copy-done.4
  21.7 0.0 collective-permute-done.other_ref
  21.7 4.3 %shard_map.78 = (f32[136,128]{1,0:T(8,128)S(1)}, f32[128,128]{1,0:T(8,128)S(1)}, f32[128,128,128]{2,1,0:T(8,128)S(1)}, s32[1,128]{1,0:T(1,128)S(1)}, s32[1,128]{...) custom-call(f32[128,128,128]{2,1,0:T(8,128)} %tiles_hbm.1, ...), custom_call_target="tpu_custom_call" | custom-call | tf_op jit(solution)/shard_map/pallas_call | solution.py:333
  26.1 2.0 %collective-permute-start.3 = (f32[136,128]{1,0:T(8,128)S(1)}, f32[136,128]{1,0:T(8,128)S(1)}, u32[]{:S(2)}, u32[]{:S(2)}) collective-permute-start(f32[136,128]{1,0:T(8,128)S(1)} %get-tuple-element.55.own_ref), channel_id=1, source_target_pairs={{0,3},{1,2},{2,1},{3,0},{4,7},{5,6},{6,5},{7,4},{8,11},{9,10},{10,... | collective-permute-start | bytes 208904 | tf_op jit(solution)/shard_map/ppermute | solution.py:359
  28.1 1.5 %collective-permute-start.2 = (f32[136,128]{1,0:T(8,128)S(1)}, f32[136,128]{1,0:T(8,128)S(1)}, u32[]{:S(2)}, u32[]{:S(2)}) collective-permute-start(f32[136,128]{1,0:T(8,128)S(1)} %get-tuple-element.55.own_ref), channel_id=1, source_target_pairs={{0,2},{1,3},{2,0},{3,1},{4,6},{5,7},{6,4},{7,5},{8,10},{9,11},{10,... | collective-permute-start | bytes 208904 | tf_op jit(solution)/shard_map/ppermute | solution.py:359
  29.5 1.4 %collective-permute-start.1 = (f32[136,128]{1,0:T(8,128)S(1)}, f32[136,128]{1,0:T(8,128)S(1)}, u32[]{:S(2)}, u32[]{:S(2)}) collective-permute-start(f32[136,128]{1,0:T(8,128)S(1)} %get-tuple-element.55.own_ref), channel_id=1, source_target_pairs={{0,1},{1,0},{2,3},{3,2},{4,5},{5,4},{6,7},{7,6},{8,9},{9,8},{10,11... | collective-permute-start | bytes 208904 | tf_op jit(solution)/shard_map/ppermute | solution.py:359
  30.9 5.1 %collective-permute-start.4 = (f32[8,128]{1,0:T(8,128)S(1)}, f32[8,128]{1,0:T(8,128)S(1)}, u32[]{:S(2)}, u32[]{:S(2)}) collective-permute-start(f32[8,128]{1,0:T(8,128)S(1)} %get-tuple-element.53), channel_id=1, source_target_pairs={{0,6},{1,7},{2,4},{3,5},{4,2},{5,3},{6,0},{7,1},{8,14},{9,15},{10,... | collective-permute-start | bytes 12296 | tf_op jit(solution)/shard_map/ppermute | solution.py:359
  35.9 0.2 shard_map.79.spread_ref
  36.1 2.1 %shard_map.80.low_ref = f32[64,128,128]{2,1,0:T(8,128)S(1)} custom-call(f32[128,128,128]{2,1,0:T(8,128)S(1)} %get-tuple-element.66.natural_ref), custom_call_target="tpu_custom_call" | custom-call | bytes 8388608 | tf_op jit(solution)/shard_map/pallas_call | solution.py:333
  38.3 0.0 collective-permute-done.4.ids_ref
  38.3 0.0 collective-permute-done.2.two_ref
  38.3 0.6 shard_map.81
  38.9 3.5 %collective-permute-start.5 = (f32[136,128]{1,0:T(8,128)S(1)}, f32[136,128]{1,0:T(8,128)S(1)}, u32[]{:S(2)}, u32[]{:S(2)}) collective-permute-start(f32[136,128]{1,0:T(8,128)S(1)} %get-tuple-element.63), channel_id=1, source_target_pairs={{0,6},{1,7},{2,4},{3,5},{4,2},{5,3},{6,0},{7,1},{8,14},{9,15},{10,... | collective-permute-start | bytes 208904 | tf_op jit(solution)/shard_map/ppermute | solution.py:359
  42.4 2.1 %shard_map.82.high_ref = f32[64,128,128]{2,1,0:T(8,128)S(1)} custom-call(f32[128,128,128]{2,1,0:T(8,128)S(1)} %get-tuple-element.66.natural_ref), custom_call_target="tpu_custom_call" | custom-call | bytes 8388608 | tf_op jit(solution)/shard_map/pallas_call | solution.py:333
  44.5 2.2 %collective-permute-done.5.far_ref = f32[136,128]{1,0:T(8,128)S(1)} collective-permute-done((f32[136,128]{1,0:T(8,128)S(1)}, f32[136,128]{1,0:T(8,128)S(1)}, u32[]{:S(2)}, u32[]{:S(2)}) %collective-permute-start.5) | collective-permute-done | bytes 69664 | tf_op jit(solution)/shard_map/ppermute | solution.py:359
  46.7 1.0 shard_map.83
  47.8 11.4 %all_to_all.58 = f32[32,8,128]{2,1,0:T(8,128)S(1)} all-to-all(f32[32,8,128]{2,1,0:T(8,128)S(1)} %bitcast.19), channel_id=1, replica_groups=mesh['vox'=32,'row'=8] {'vox'}, dimensions={0} | all-to-all | bytes 262144 | tf_op jit(solution)/shard_map/all_to_all | solution.py:356
  59.2 0.5 shard_map.84
  59.8 11.3 %all_to_all.59 = f32[32,8,128]{2,1,0:T(8,128)S(1)} all-to-all(f32[32,8,128]{2,1,0:T(8,128)S(1)} %bitcast.20), channel_id=1, replica_groups=mesh['vox'=32,'row'=8] {'vox'}, dimensions={0} | all-to-all | bytes 262144 | tf_op jit(solution)/shard_map/all_to_all | solution.py:356
  71.0 1.0 shard_map.85
  72.0 1.1 collective-permute-start.8
  73.1 1.7 %collective-permute-start.7 = (f32[136,128]{1,0:T(8,128)S(1)}, f32[136,128]{1,0:T(8,128)S(1)}, u32[]{:S(2)}, u32[]{:S(2)}) collective-permute-start(f32[136,128]{1,0:T(8,128)S(1)} %get-tuple-element.73.own_ref), channel_id=1, source_target_pairs={{0,2},{1,3},{2,0},{3,1},{4,6},{5,7},{6,4},{7,5},{8,10},{9,11},{10,... | collective-permute-start | bytes 208904 | tf_op jit(solution)/shard_map/ppermute | solution.py:359
  74.8 0.8 collective-permute-start.6
  75.6 0.2 shard_map.86.spread_ref
  75.8 4.2 %collective-permute-done.8.three_ref = f32[136,128]{1,0:T(8,128)S(1)} collective-permute-done((f32[136,128]{1,0:T(8,128)S(1)}, f32[136,128]{1,0:T(8,128)S(1)}, u32[]{:S(2)}, u32[]{:S(2)}) %collective-permute-start.8) | collective-permute-done | bytes 69664 | tf_op jit(solution)/shard_map/ppermute | solution.py:359
  80.0 0.6 shard_map.87
  80.7 4.0 %collective-permute-start.9 = (f32[136,128]{1,0:T(8,128)S(1)}, f32[136,128]{1,0:T(8,128)S(1)}, u32[]{:S(2)}, u32[]{:S(2)}) collective-permute-start(f32[136,128]{1,0:T(8,128)S(1)} %get-tuple-element.76.send_ref), channel_id=1, source_target_pairs={{0,6},{1,7},{2,4},{3,5},{4,2},{5,3},{6,0},{7,1},{8,14},{9,15},{10,... | collective-permute-start | bytes 208904 | tf_op jit(solution)/shard_map/ppermute | solution.py:359
  84.7 3.3 %collective-permute-done.9.far_ref = f32[136,128]{1,0:T(8,128)S(1)} collective-permute-done((f32[136,128]{1,0:T(8,128)S(1)}, f32[136,128]{1,0:T(8,128)S(1)}, u32[]{:S(2)}, u32[]{:S(2)}) %collective-permute-start.9) | collective-permute-done | bytes 69664 | tf_op jit(solution)/shard_map/ppermute | solution.py:359
  87.9 3.2 %collective-permute-start.10 = (f32[512,128]{1,0:T(8,128)S(1)}, f32[512,128]{1,0:T(8,128)S(1)}, u32[]{:S(2)}, u32[]{:S(2)}) collective-permute-start(f32[512,128]{1,0:T(8,128)S(1)} %get-tuple-element.83.inner_near_ref), channel_id=1, source_target_pairs={{0,6},{1,7},{2,4},{3,5},{4,2},{5,3},{6,0},{7,1},{8,14},{9,15},{10,... | collective-permute-start | bytes 786440 | tf_op jit(solution)/shard_map/ppermute | solution.py:359
  91.1 1.1 shard_map.88
  92.2 10.8 %all_to_all.60 = f32[32,4,128]{2,1,0:T(4,128)S(1)} all-to-all(f32[32,4,128]{2,1,0:T(4,128)S(1)} %bitcast.22), channel_id=1, replica_groups=mesh['vox'=32,'row'=8] {'vox'}, dimensions={0} | all-to-all | bytes 131072 | tf_op jit(solution)/shard_map/all_to_all | solution.py:356
  103.0 0.4 shard_map.89
  103.4 11.2 %all_to_all.61 = f32[32,8,128]{2,1,0:T(8,128)S(1)} all-to-all(f32[32,8,128]{2,1,0:T(8,128)S(1)} %bitcast.21), channel_id=1, replica_groups=mesh['vox'=32,'row'=8] {'vox'}, dimensions={0} | all-to-all | bytes 262144 | tf_op jit(solution)/shard_map/all_to_all | solution.py:356
  114.6 1.0 shard_map.90.own_ref
  115.6 1.1 collective-permute-start.13
  116.7 1.8 %collective-permute-start.12 = (f32[136,128]{1,0:T(8,128)S(1)}, f32[136,128]{1,0:T(8,128)S(1)}, u32[]{:S(2)}, u32[]{:S(2)}) collective-permute-start(f32[136,128]{1,0:T(8,128)S(1)} %shard_map.90.own_ref), channel_id=1, source_target_pairs={{0,2},{1,3},{2,0},{3,1},{4,6},{5,7},{6,4},{7,5},{8,10},{9,11},{10,... | collective-permute-start | bytes 208904 | tf_op jit(solution)/shard_map/ppermute | solution.py:359
  118.5 0.7 collective-permute-start.11
  119.2 0.2 shard_map.91.spread_ref
  119.4 4.2 %collective-permute-done.13.three_ref = f32[136,128]{1,0:T(8,128)S(1)} collective-permute-done((f32[136,128]{1,0:T(8,128)S(1)}, f32[136,128]{1,0:T(8,128)S(1)}, u32[]{:S(2)}, u32[]{:S(2)}) %collective-permute-start.13) | collective-permute-done | bytes 69664 | tf_op jit(solution)/shard_map/ppermute | solution.py:359
  123.6 0.3 shard_map.92.near_ref
  124.0 2.9 %collective-permute-start.14 = (f32[264,128]{1,0:T(8,128)S(1)}, f32[264,128]{1,0:T(8,128)S(1)}, u32[]{:S(2)}, u32[]{:S(2)}) collective-permute-start(f32[264,128]{1,0:T(8,128)S(1)} %shard_map.92.near_ref), channel_id=1, source_target_pairs={{0,6},{1,7},{2,4},{3,5},{4,2},{5,3},{6,0},{7,1},{8,14},{9,15},{10,... | collective-permute-start | bytes 405512 | tf_op jit(solution)/shard_map/ppermute | solution.py:359
  126.8 7.2 %collective-permute-done.14.far_ref = f32[264,128]{1,0:T(8,128)S(1)} collective-permute-done((f32[264,128]{1,0:T(8,128)S(1)}, f32[264,128]{1,0:T(8,128)S(1)}, u32[]{:S(2)}, u32[]{:S(2)}) %collective-permute-start.14) | collective-permute-done | bytes 135200 | tf_op jit(solution)/shard_map/ppermute | solution.py:359
  134.1 0.8 shard_map.93
  (15 shorter events, 0.1 us)
Async XLA Ops:
  0.6 0.8 copy-start
  19.8 2.0 %collective-permute-start = (f32[1024,128]{1,0:T(8,128)S(1)}, f32[1024,128]{1,0:T(8,128)S(1)}, u32[]{:S(2)}, u32[]{:S(2)}) collective-permute-start(f32[1024,128]{1,0:T(8,128)S(1)} %bitcast.12), channel_id=1, source_target_pairs={{0,8},{8,0},{16,24},{24,16},{32,40},{40,32},{48,56},{56,48},{64,72... | collective-permute-start | bytes 1572872 | tf_op jit(solution)/shard_map/ppermute | solution.py:371
  19.8 0.7 copy-start.2
  20.4 0.7 copy-start.3
  21.1 0.7 copy-start.4
  26.1 12.2 %collective-permute-start.3 = (f32[136,128]{1,0:T(8,128)S(1)}, f32[136,128]{1,0:T(8,128)S(1)}, u32[]{:S(2)}, u32[]{:S(2)}) collective-permute-start(f32[136,128]{1,0:T(8,128)S(1)} %get-tuple-element.55.own_ref), channel_id=1, source_target_pairs={{0,3},{1,2},{2,1},{3,0},{4,7},{5,6},{6,5},{7,4},{8,11},{9,10},{10,... | collective-permute-start | bytes 208904 | tf_op jit(solution)/shard_map/ppermute | solution.py:359
  28.1 10.2 %collective-permute-start.2 = (f32[136,128]{1,0:T(8,128)S(1)}, f32[136,128]{1,0:T(8,128)S(1)}, u32[]{:S(2)}, u32[]{:S(2)}) collective-permute-start(f32[136,128]{1,0:T(8,128)S(1)} %get-tuple-element.55.own_ref), channel_id=1, source_target_pairs={{0,2},{1,3},{2,0},{3,1},{4,6},{5,7},{6,4},{7,5},{8,10},{9,11},{10,... | collective-permute-start | bytes 208904 | tf_op jit(solution)/shard_map/ppermute | solution.py:359
  29.5 8.8 %collective-permute-start.1 = (f32[136,128]{1,0:T(8,128)S(1)}, f32[136,128]{1,0:T(8,128)S(1)}, u32[]{:S(2)}, u32[]{:S(2)}) collective-permute-start(f32[136,128]{1,0:T(8,128)S(1)} %get-tuple-element.55.own_ref), channel_id=1, source_target_pairs={{0,1},{1,0},{2,3},{3,2},{4,5},{5,4},{6,7},{7,6},{8,9},{9,8},{10,11... | collective-permute-start | bytes 208904 | tf_op jit(solution)/shard_map/ppermute | solution.py:359
  30.9 7.4 %collective-permute-start.4 = (f32[8,128]{1,0:T(8,128)S(1)}, f32[8,128]{1,0:T(8,128)S(1)}, u32[]{:S(2)}, u32[]{:S(2)}) collective-permute-start(f32[8,128]{1,0:T(8,128)S(1)} %get-tuple-element.53), channel_id=1, source_target_pairs={{0,6},{1,7},{2,4},{3,5},{4,2},{5,3},{6,0},{7,1},{8,14},{9,15},{10,... | collective-permute-start | bytes 12296 | tf_op jit(solution)/shard_map/ppermute | solution.py:359
  38.9 7.8 %collective-permute-start.5 = (f32[136,128]{1,0:T(8,128)S(1)}, f32[136,128]{1,0:T(8,128)S(1)}, u32[]{:S(2)}, u32[]{:S(2)}) collective-permute-start(f32[136,128]{1,0:T(8,128)S(1)} %get-tuple-element.63), channel_id=1, source_target_pairs={{0,6},{1,7},{2,4},{3,5},{4,2},{5,3},{6,0},{7,1},{8,14},{9,15},{10,... | collective-permute-start | bytes 208904 | tf_op jit(solution)/shard_map/ppermute | solution.py:359
  72.0 8.0 %collective-permute-start.8 = (f32[136,128]{1,0:T(8,128)S(1)}, f32[136,128]{1,0:T(8,128)S(1)}, u32[]{:S(2)}, u32[]{:S(2)}) collective-permute-start(f32[136,128]{1,0:T(8,128)S(1)} %get-tuple-element.73.own_ref), channel_id=1, source_target_pairs={{0,3},{1,2},{2,1},{3,0},{4,7},{5,6},{6,5},{7,4},{8,11},{9,10},{10,... | collective-permute-start | bytes 208904 | tf_op jit(solution)/shard_map/ppermute | solution.py:359
  73.1 6.9 %collective-permute-start.7 = (f32[136,128]{1,0:T(8,128)S(1)}, f32[136,128]{1,0:T(8,128)S(1)}, u32[]{:S(2)}, u32[]{:S(2)}) collective-permute-start(f32[136,128]{1,0:T(8,128)S(1)} %get-tuple-element.73.own_ref), channel_id=1, source_target_pairs={{0,2},{1,3},{2,0},{3,1},{4,6},{5,7},{6,4},{7,5},{8,10},{9,11},{10,... | collective-permute-start | bytes 208904 | tf_op jit(solution)/shard_map/ppermute | solution.py:359
  74.8 5.2 %collective-permute-start.6 = (f32[136,128]{1,0:T(8,128)S(1)}, f32[136,128]{1,0:T(8,128)S(1)}, u32[]{:S(2)}, u32[]{:S(2)}) collective-permute-start(f32[136,128]{1,0:T(8,128)S(1)} %get-tuple-element.73.own_ref), channel_id=1, source_target_pairs={{0,1},{1,0},{2,3},{3,2},{4,5},{5,4},{6,7},{7,6},{8,9},{9,8},{10,11... | collective-permute-start | bytes 208904 | tf_op jit(solution)/shard_map/ppermute | solution.py:359
  80.7 7.3 %collective-permute-start.9 = (f32[136,128]{1,0:T(8,128)S(1)}, f32[136,128]{1,0:T(8,128)S(1)}, u32[]{:S(2)}, u32[]{:S(2)}) collective-permute-start(f32[136,128]{1,0:T(8,128)S(1)} %get-tuple-element.76.send_ref), channel_id=1, source_target_pairs={{0,6},{1,7},{2,4},{3,5},{4,2},{5,3},{6,0},{7,1},{8,14},{9,15},{10,... | collective-permute-start | bytes 208904 | tf_op jit(solution)/shard_map/ppermute | solution.py:359
  87.9 15.1 %collective-permute-start.10 = (f32[512,128]{1,0:T(8,128)S(1)}, f32[512,128]{1,0:T(8,128)S(1)}, u32[]{:S(2)}, u32[]{:S(2)}) collective-permute-start(f32[512,128]{1,0:T(8,128)S(1)} %get-tuple-element.83.inner_near_ref), channel_id=1, source_target_pairs={{0,6},{1,7},{2,4},{3,5},{4,2},{5,3},{6,0},{7,1},{8,14},{9,15},{10,... | collective-permute-start | bytes 786440 | tf_op jit(solution)/shard_map/ppermute | solution.py:359
  91.1 43.0 %copy-start.1 = (f32[64,128]{1,0:T(8,128)S(1)}, f32[64,128]{1,0:T(8,128)}, u32[]{:S(2)}) copy-start(f32[64,128]{1,0:T(8,128)} %ray_ref.3) | copy-start | bytes 98308
  115.6 8.0 %collective-permute-start.13 = (f32[136,128]{1,0:T(8,128)S(1)}, f32[136,128]{1,0:T(8,128)S(1)}, u32[]{:S(2)}, u32[]{:S(2)}) collective-permute-start(f32[136,128]{1,0:T(8,128)S(1)} %shard_map.90.own_ref), channel_id=1, source_target_pairs={{0,3},{1,2},{2,1},{3,0},{4,7},{5,6},{6,5},{7,4},{8,11},{9,10},{10,... | collective-permute-start | bytes 208904 | tf_op jit(solution)/shard_map/ppermute | solution.py:359
  116.7 6.9 %collective-permute-start.12 = (f32[136,128]{1,0:T(8,128)S(1)}, f32[136,128]{1,0:T(8,128)S(1)}, u32[]{:S(2)}, u32[]{:S(2)}) collective-permute-start(f32[136,128]{1,0:T(8,128)S(1)} %shard_map.90.own_ref), channel_id=1, source_target_pairs={{0,2},{1,3},{2,0},{3,1},{4,6},{5,7},{6,4},{7,5},{8,10},{9,11},{10,... | collective-permute-start | bytes 208904 | tf_op jit(solution)/shard_map/ppermute | solution.py:359
  118.5 5.1 %collective-permute-start.11 = (f32[136,128]{1,0:T(8,128)S(1)}, f32[136,128]{1,0:T(8,128)S(1)}, u32[]{:S(2)}, u32[]{:S(2)}) collective-permute-start(f32[136,128]{1,0:T(8,128)S(1)} %shard_map.90.own_ref), channel_id=1, source_target_pairs={{0,1},{1,0},{2,3},{3,2},{4,5},{5,4},{6,7},{7,6},{8,9},{9,8},{10,11... | collective-permute-start | bytes 208904 | tf_op jit(solution)/shard_map/ppermute | solution.py:359
  124.0 10.1 %collective-permute-start.14 = (f32[264,128]{1,0:T(8,128)S(1)}, f32[264,128]{1,0:T(8,128)S(1)}, u32[]{:S(2)}, u32[]{:S(2)}) collective-permute-start(f32[264,128]{1,0:T(8,128)S(1)} %shard_map.92.near_ref), channel_id=1, source_target_pairs={{0,6},{1,7},{2,4},{3,5},{4,2},{5,3},{6,0},{7,1},{8,14},{9,15},{10,... | collective-permute-start | bytes 405512 | tf_op jit(solution)/shard_map/ppermute | solution.py:359

commit v7 on v6

--- a/solution.py
+++ b/solution.py
@@ -15,7 +15,7 @@
 CORES = 2
 HALF = TILE // 2
 CHIPS = N_VOX // CORES
-CHUNKS = 8
+CHUNKS = 16
 PAD = 8
 MAP = CAP
 NORM, LOCAL, OTHER = CAP, CAP + 1, CAP + 2

time: 135 us -> 136 us (level)
  no operation moved by 1% of the time
where the time goes in v7:
time: 136 us; the launch traced here: 135 us
  blocking collectives  63 us (46%)
  starting transfers between devices  30.5 us (22%)
  waiting for transfers between devices  21.1 us (16%)
  Pallas kernels  17.1 us (13%)
  local copies, waits for them, and re-layouts  2.72 us (2%)
    all_to_all x4, blocking collectives, over_vox(): return lax.all_to_all(array, 'vox', 0, 0, tiled=True)  44.7 us
    ppermute x14, starting transfers between devices, across(): lax.ppermute(array, 'row', [(index, index ^ distance) for index in range(...  30.5 us
    ppermute x14, waiting for transfers between devices, across(): lax.ppermute(array, 'row', [(index, index ^ distance) for index in range(...  21.1 us
    all_to_all x1, blocking collectives, local(): lax.all_to_all(copies, 'vox', 0, 0, tiled=True, axis_index_groups=chips)  18.3 us
    pallas_call x18, Pallas kernels, call(): pl.pallas_call(kernel, out_shape=outs, in_specs=specs + [vmem] * (len(arg...  17.1 us
    unnamed x10, local copies, waits for them, and re-layouts  2.72 us
  transfers between devices with their start and end apart: 15, of which 5 were waited for; matrix products, arithmetic and copies ran while one was open for 0% of the time, Pallas kernels for 4%

profile of v7, /device:TPU:32, one launch (start us, length us, event | category | flops | bytes accessed | tf_op | source)
XLA Modules:
  0.0 135.3 jit_solution(8363705197498633977)
XLA Ops:
  0.6 0.0 copy-start
  0.6 0.7 copy-done
  1.4 18.3 %all_to_all.57 = f32[16,64,128]{2,1,0:T(8,128)S(1)} all-to-all(f32[16,64,128]{2,1,0:T(8,128)S(1)} %bitcast.14), channel_id=1, replica_groups={{0,16,32,48,64,80,96,112,128,144,160,176,192,208,224,240},{8,24,40,56,7..., dimensions={0} | all-to-all | bytes 1048576 | tf_op jit(solution)/shard_map/all_to_all | solution.py:369
  19.8 0.0 collective-permute-start
  19.8 0.7 copy-done.2
  20.4 0.7 copy-done.3
  21.1 0.7 copy-done.4
  21.7 0.0 collective-permute-done.other_ref
  21.7 4.7 %shard_map.78 = (f32[136,128]{1,0:T(8,128)S(1)}, f32[128,128]{1,0:T(8,128)S(1)}, f32[128,128,128]{2,1,0:T(8,128)S(1)}, s32[1,128]{1,0:T(1,128)S(1)}, s32[1,128]{...) custom-call(f32[128,128,128]{2,1,0:T(8,128)} %tiles_hbm.1, ...), custom_call_target="tpu_custom_call" | custom-call | tf_op jit(solution)/shard_map/pallas_call | solution.py:333
  26.5 2.0 %collective-permute-start.3 = (f32[136,128]{1,0:T(8,128)S(1)}, f32[136,128]{1,0:T(8,128)S(1)}, u32[]{:S(2)}, u32[]{:S(2)}) collective-permute-start(f32[136,128]{1,0:T(8,128)S(1)} %get-tuple-element.55.own_ref), channel_id=1, source_target_pairs={{0,3},{1,2},{2,1},{3,0},{4,7},{5,6},{6,5},{7,4},{8,11},{9,10},{10,... | collective-permute-start | bytes 208904 | tf_op jit(solution)/shard_map/ppermute | solution.py:359
  28.5 1.5 %collective-permute-start.2 = (f32[136,128]{1,0:T(8,128)S(1)}, f32[136,128]{1,0:T(8,128)S(1)}, u32[]{:S(2)}, u32[]{:S(2)}) collective-permute-start(f32[136,128]{1,0:T(8,128)S(1)} %get-tuple-element.55.own_ref), channel_id=1, source_target_pairs={{0,2},{1,3},{2,0},{3,1},{4,6},{5,7},{6,4},{7,5},{8,10},{9,11},{10,... | collective-permute-start | bytes 208904 | tf_op jit(solution)/shard_map/ppermute | solution.py:359
  29.9 1.4 %collective-permute-start.1 = (f32[136,128]{1,0:T(8,128)S(1)}, f32[136,128]{1,0:T(8,128)S(1)}, u32[]{:S(2)}, u32[]{:S(2)}) collective-permute-start(f32[136,128]{1,0:T(8,128)S(1)} %get-tuple-element.55.own_ref), channel_id=1, source_target_pairs={{0,1},{1,0},{2,3},{3,2},{4,5},{5,4},{6,7},{7,6},{8,9},{9,8},{10,11... | collective-permute-start | bytes 208904 | tf_op jit(solution)/shard_map/ppermute | solution.py:359
  31.3 5.1 %collective-permute-start.4 = (f32[8,128]{1,0:T(8,128)S(1)}, f32[8,128]{1,0:T(8,128)S(1)}, u32[]{:S(2)}, u32[]{:S(2)}) collective-permute-start(f32[8,128]{1,0:T(8,128)S(1)} %get-tuple-element.53), channel_id=1, source_target_pairs={{0,6},{1,7},{2,4},{3,5},{4,2},{5,3},{6,0},{7,1},{8,14},{9,15},{10,... | collective-permute-start | bytes 12296 | tf_op jit(solution)/shard_map/ppermute | solution.py:359
  36.4 0.2 shard_map.79.spread_ref
  36.6 2.1 %shard_map.80.low_ref = f32[64,128,128]{2,1,0:T(8,128)S(1)} custom-call(f32[128,128,128]{2,1,0:T(8,128)S(1)} %get-tuple-element.66.natural_ref), custom_call_target="tpu_custom_call" | custom-call | bytes 8388608 | tf_op jit(solution)/shard_map/pallas_call | solution.py:333
  38.7 0.0 collective-permute-done.2.two_ref
  38.7 0.6 shard_map.81
  39.4 3.5 %collective-permute-start.5 = (f32[136,128]{1,0:T(8,128)S(1)}, f32[136,128]{1,0:T(8,128)S(1)}, u32[]{:S(2)}, u32[]{:S(2)}) collective-permute-start(f32[136,128]{1,0:T(8,128)S(1)} %get-tuple-element.63), channel_id=1, source_target_pairs={{0,6},{1,7},{2,4},{3,5},{4,2},{5,3},{6,0},{7,1},{8,14},{9,15},{10,... | collective-permute-start | bytes 208904 | tf_op jit(solution)/shard_map/ppermute | solution.py:359
  42.8 2.1 %shard_map.82.high_ref = f32[64,128,128]{2,1,0:T(8,128)S(1)} custom-call(f32[128,128,128]{2,1,0:T(8,128)S(1)} %get-tuple-element.66.natural_ref), custom_call_target="tpu_custom_call" | custom-call | bytes 8388608 | tf_op jit(solution)/shard_map/pallas_call | solution.py:333
  44.9 2.2 %collective-permute-done.5.far_ref = f32[136,128]{1,0:T(8,128)S(1)} collective-permute-done((f32[136,128]{1,0:T(8,128)S(1)}, f32[136,128]{1,0:T(8,128)S(1)}, u32[]{:S(2)}, u32[]{:S(2)}) %collective-permute-start.5) | collective-permute-done | bytes 69664 | tf_op jit(solution)/shard_map/ppermute | solution.py:359
  47.2 1.0 shard_map.83
  48.2 11.4 %all_to_all.58 = f32[32,8,128]{2,1,0:T(8,128)S(1)} all-to-all(f32[32,8,128]{2,1,0:T(8,128)S(1)} %bitcast.19), channel_id=1, replica_groups=mesh['vox'=32,'row'=8] {'vox'}, dimensions={0} | all-to-all | bytes 262144 | tf_op jit(solution)/shard_map/all_to_all | solution.py:356
  59.7 0.5 shard_map.84
  60.2 11.3 %all_to_all.59 = f32[32,8,128]{2,1,0:T(8,128)S(1)} all-to-all(f32[32,8,128]{2,1,0:T(8,128)S(1)} %bitcast.20), channel_id=1, replica_groups=mesh['vox'=32,'row'=8] {'vox'}, dimensions={0} | all-to-all | bytes 262144 | tf_op jit(solution)/shard_map/all_to_all | solution.py:356
  71.5 1.0 shard_map.85
  72.5 1.1 collective-permute-start.8
  73.5 1.7 %collective-permute-start.7 = (f32[136,128]{1,0:T(8,128)S(1)}, f32[136,128]{1,0:T(8,128)S(1)}, u32[]{:S(2)}, u32[]{:S(2)}) collective-permute-start(f32[136,128]{1,0:T(8,128)S(1)} %get-tuple-element.73.own_ref), channel_id=1, source_target_pairs={{0,2},{1,3},{2,0},{3,1},{4,6},{5,7},{6,4},{7,5},{8,10},{9,11},{10,... | collective-permute-start | bytes 208904 | tf_op jit(solution)/shard_map/ppermute | solution.py:359
  75.3 0.8 collective-permute-start.6
  76.0 0.2 shard_map.86.spread_ref
  76.3 4.2 %collective-permute-done.8.three_ref = f32[136,128]{1,0:T(8,128)S(1)} collective-permute-done((f32[136,128]{1,0:T(8,128)S(1)}, f32[136,128]{1,0:T(8,128)S(1)}, u32[]{:S(2)}, u32[]{:S(2)}) %collective-permute-start.8) | collective-permute-done | bytes 69664 | tf_op jit(solution)/shard_map/ppermute | solution.py:359
  80.4 0.6 shard_map.87
  81.1 4.0 %collective-permute-start.9 = (f32[136,128]{1,0:T(8,128)S(1)}, f32[136,128]{1,0:T(8,128)S(1)}, u32[]{:S(2)}, u32[]{:S(2)}) collective-permute-start(f32[136,128]{1,0:T(8,128)S(1)} %get-tuple-element.76.send_ref), channel_id=1, source_target_pairs={{0,6},{1,7},{2,4},{3,5},{4,2},{5,3},{6,0},{7,1},{8,14},{9,15},{10,... | collective-permute-start | bytes 208904 | tf_op jit(solution)/shard_map/ppermute | solution.py:359
  85.1 3.3 %collective-permute-done.9.far_ref = f32[136,128]{1,0:T(8,128)S(1)} collective-permute-done((f32[136,128]{1,0:T(8,128)S(1)}, f32[136,128]{1,0:T(8,128)S(1)}, u32[]{:S(2)}, u32[]{:S(2)}) %collective-permute-start.9) | collective-permute-done | bytes 69664 | tf_op jit(solution)/shard_map/ppermute | solution.py:359
  88.3 3.2 %collective-permute-start.10 = (f32[512,128]{1,0:T(8,128)S(1)}, f32[512,128]{1,0:T(8,128)S(1)}, u32[]{:S(2)}, u32[]{:S(2)}) collective-permute-start(f32[512,128]{1,0:T(8,128)S(1)} %get-tuple-element.83.inner_near_ref), channel_id=1, source_target_pairs={{0,6},{1,7},{2,4},{3,5},{4,2},{5,3},{6,0},{7,1},{8,14},{9,15},{10,... | collective-permute-start | bytes 786440 | tf_op jit(solution)/shard_map/ppermute | solution.py:359
  91.5 1.1 shard_map.88
  92.7 10.8 %all_to_all.60 = f32[32,4,128]{2,1,0:T(4,128)S(1)} all-to-all(f32[32,4,128]{2,1,0:T(4,128)S(1)} %bitcast.22), channel_id=1, replica_groups=mesh['vox'=32,'row'=8] {'vox'}, dimensions={0} | all-to-all | bytes 131072 | tf_op jit(solution)/shard_map/all_to_all | solution.py:356
  103.5 0.4 shard_map.89
  103.8 11.2 %all_to_all.61 = f32[32,8,128]{2,1,0:T(8,128)S(1)} all-to-all(f32[32,8,128]{2,1,0:T(8,128)S(1)} %bitcast.21), channel_id=1, replica_groups=mesh['vox'=32,'row'=8] {'vox'}, dimensions={0} | all-to-all | bytes 262144 | tf_op jit(solution)/shard_map/all_to_all | solution.py:356
  115.1 1.0 shard_map.90.own_ref
  116.1 1.1 collective-permute-start.13
  117.2 1.8 %collective-permute-start.12 = (f32[136,128]{1,0:T(8,128)S(1)}, f32[136,128]{1,0:T(8,128)S(1)}, u32[]{:S(2)}, u32[]{:S(2)}) collective-permute-start(f32[136,128]{1,0:T(8,128)S(1)} %shard_map.90.own_ref), channel_id=1, source_target_pairs={{0,2},{1,3},{2,0},{3,1},{4,6},{5,7},{6,4},{7,5},{8,10},{9,11},{10,... | collective-permute-start | bytes 208904 | tf_op jit(solution)/shard_map/ppermute | solution.py:359
  119.0 0.7 collective-permute-start.11
  119.6 0.2 shard_map.91.spread_ref
  119.8 4.2 %collective-permute-done.13.three_ref = f32[136,128]{1,0:T(8,128)S(1)} collective-permute-done((f32[136,128]{1,0:T(8,128)S(1)}, f32[136,128]{1,0:T(8,128)S(1)}, u32[]{:S(2)}, u32[]{:S(2)}) %collective-permute-start.13) | collective-permute-done | bytes 69664 | tf_op jit(solution)/shard_map/ppermute | solution.py:359
  124.1 0.3 shard_map.92.near_ref
  124.4 2.9 %collective-permute-start.14 = (f32[264,128]{1,0:T(8,128)S(1)}, f32[264,128]{1,0:T(8,128)S(1)}, u32[]{:S(2)}, u32[]{:S(2)}) collective-permute-start(f32[264,128]{1,0:T(8,128)S(1)} %shard_map.92.near_ref), channel_id=1, source_target_pairs={{0,6},{1,7},{2,4},{3,5},{4,2},{5,3},{6,0},{7,1},{8,14},{9,15},{10,... | collective-permute-start | bytes 405512 | tf_op jit(solution)/shard_map/ppermute | solution.py:359
  127.3 7.2 %collective-permute-done.14.far_ref = f32[264,128]{1,0:T(8,128)S(1)} collective-permute-done((f32[264,128]{1,0:T(8,128)S(1)}, f32[264,128]{1,0:T(8,128)S(1)}, u32[]{:S(2)}, u32[]{:S(2)}) %collective-permute-start.14) | collective-permute-done | bytes 135200 | tf_op jit(solution)/shard_map/ppermute | solution.py:359
  134.5 0.8 shard_map.93
  (15 shorter events, 0.1 us)
Async XLA Ops:
  0.6 0.8 copy-start
  19.8 2.0 %collective-permute-start = (f32[1024,128]{1,0:T(8,128)S(1)}, f32[1024,128]{1,0:T(8,128)S(1)}, u32[]{:S(2)}, u32[]{:S(2)}) collective-permute-start(f32[1024,128]{1,0:T(8,128)S(1)} %bitcast.12), channel_id=1, source_target_pairs={{0,8},{8,0},{16,24},{24,16},{32,40},{40,32},{48,56},{56,48},{64,72... | collective-permute-start | bytes 1572872 | tf_op jit(solution)/shard_map/ppermute | solution.py:371
  19.8 0.7 copy-start.2
  20.4 0.7 copy-start.3
  21.1 0.7 copy-start.4
  26.5 12.2 %collective-permute-start.3 = (f32[136,128]{1,0:T(8,128)S(1)}, f32[136,128]{1,0:T(8,128)S(1)}, u32[]{:S(2)}, u32[]{:S(2)}) collective-permute-start(f32[136,128]{1,0:T(8,128)S(1)} %get-tuple-element.55.own_ref), channel_id=1, source_target_pairs={{0,3},{1,2},{2,1},{3,0},{4,7},{5,6},{6,5},{7,4},{8,11},{9,10},{10,... | collective-permute-start | bytes 208904 | tf_op jit(solution)/shard_map/ppermute | solution.py:359
  28.5 10.2 %collective-permute-start.2 = (f32[136,128]{1,0:T(8,128)S(1)}, f32[136,128]{1,0:T(8,128)S(1)}, u32[]{:S(2)}, u32[]{:S(2)}) collective-permute-start(f32[136,128]{1,0:T(8,128)S(1)} %get-tuple-element.55.own_ref), channel_id=1, source_target_pairs={{0,2},{1,3},{2,0},{3,1},{4,6},{5,7},{6,4},{7,5},{8,10},{9,11},{10,... | collective-permute-start | bytes 208904 | tf_op jit(solution)/shard_map/ppermute | solution.py:359
  29.9 8.8 %collective-permute-start.1 = (f32[136,128]{1,0:T(8,128)S(1)}, f32[136,128]{1,0:T(8,128)S(1)}, u32[]{:S(2)}, u32[]{:S(2)}) collective-permute-start(f32[136,128]{1,0:T(8,128)S(1)} %get-tuple-element.55.own_ref), channel_id=1, source_target_pairs={{0,1},{1,0},{2,3},{3,2},{4,5},{5,4},{6,7},{7,6},{8,9},{9,8},{10,11... | collective-permute-start | bytes 208904 | tf_op jit(solution)/shard_map/ppermute | solution.py:359
  31.3 7.4 %collective-permute-start.4 = (f32[8,128]{1,0:T(8,128)S(1)}, f32[8,128]{1,0:T(8,128)S(1)}, u32[]{:S(2)}, u32[]{:S(2)}) collective-permute-start(f32[8,128]{1,0:T(8,128)S(1)} %get-tuple-element.53), channel_id=1, source_target_pairs={{0,6},{1,7},{2,4},{3,5},{4,2},{5,3},{6,0},{7,1},{8,14},{9,15},{10,... | collective-permute-start | bytes 12296 | tf_op jit(solution)/shard_map/ppermute | solution.py:359
  39.4 7.8 %collective-permute-start.5 = (f32[136,128]{1,0:T(8,128)S(1)}, f32[136,128]{1,0:T(8,128)S(1)}, u32[]{:S(2)}, u32[]{:S(2)}) collective-permute-start(f32[136,128]{1,0:T(8,128)S(1)} %get-tuple-element.63), channel_id=1, source_target_pairs={{0,6},{1,7},{2,4},{3,5},{4,2},{5,3},{6,0},{7,1},{8,14},{9,15},{10,... | collective-permute-start | bytes 208904 | tf_op jit(solution)/shard_map/ppermute | solution.py:359
  72.5 8.0 %collective-permute-start.8 = (f32[136,128]{1,0:T(8,128)S(1)}, f32[136,128]{1,0:T(8,128)S(1)}, u32[]{:S(2)}, u32[]{:S(2)}) collective-permute-start(f32[136,128]{1,0:T(8,128)S(1)} %get-tuple-element.73.own_ref), channel_id=1, source_target_pairs={{0,3},{1,2},{2,1},{3,0},{4,7},{5,6},{6,5},{7,4},{8,11},{9,10},{10,... | collective-permute-start | bytes 208904 | tf_op jit(solution)/shard_map/ppermute | solution.py:359
  73.5 6.9 %collective-permute-start.7 = (f32[136,128]{1,0:T(8,128)S(1)}, f32[136,128]{1,0:T(8,128)S(1)}, u32[]{:S(2)}, u32[]{:S(2)}) collective-permute-start(f32[136,128]{1,0:T(8,128)S(1)} %get-tuple-element.73.own_ref), channel_id=1, source_target_pairs={{0,2},{1,3},{2,0},{3,1},{4,6},{5,7},{6,4},{7,5},{8,10},{9,11},{10,... | collective-permute-start | bytes 208904 | tf_op jit(solution)/shard_map/ppermute | solution.py:359
  75.3 5.2 %collective-permute-start.6 = (f32[136,128]{1,0:T(8,128)S(1)}, f32[136,128]{1,0:T(8,128)S(1)}, u32[]{:S(2)}, u32[]{:S(2)}) collective-permute-start(f32[136,128]{1,0:T(8,128)S(1)} %get-tuple-element.73.own_ref), channel_id=1, source_target_pairs={{0,1},{1,0},{2,3},{3,2},{4,5},{5,4},{6,7},{7,6},{8,9},{9,8},{10,11... | collective-permute-start | bytes 208904 | tf_op jit(solution)/shard_map/ppermute | solution.py:359
  81.1 7.3 %collective-permute-start.9 = (f32[136,128]{1,0:T(8,128)S(1)}, f32[136,128]{1,0:T(8,128)S(1)}, u32[]{:S(2)}, u32[]{:S(2)}) collective-permute-start(f32[136,128]{1,0:T(8,128)S(1)} %get-tuple-element.76.send_ref), channel_id=1, source_target_pairs={{0,6},{1,7},{2,4},{3,5},{4,2},{5,3},{6,0},{7,1},{8,14},{9,15},{10,... | collective-permute-start | bytes 208904 | tf_op jit(solution)/shard_map/ppermute | solution.py:359
  88.3 15.1 %collective-permute-start.10 = (f32[512,128]{1,0:T(8,128)S(1)}, f32[512,128]{1,0:T(8,128)S(1)}, u32[]{:S(2)}, u32[]{:S(2)}) collective-permute-start(f32[512,128]{1,0:T(8,128)S(1)} %get-tuple-element.83.inner_near_ref), channel_id=1, source_target_pairs={{0,6},{1,7},{2,4},{3,5},{4,2},{5,3},{6,0},{7,1},{8,14},{9,15},{10,... | collective-permute-start | bytes 786440 | tf_op jit(solution)/shard_map/ppermute | solution.py:359
  91.5 43.0 %copy-start.1 = (f32[64,128]{1,0:T(8,128)S(1)}, f32[64,128]{1,0:T(8,128)}, u32[]{:S(2)}) copy-start(f32[64,128]{1,0:T(8,128)} %ray_ref.3) | copy-start | bytes 98308
  116.1 8.0 %collective-permute-start.13 = (f32[136,128]{1,0:T(8,128)S(1)}, f32[136,128]{1,0:T(8,128)S(1)}, u32[]{:S(2)}, u32[]{:S(2)}) collective-permute-start(f32[136,128]{1,0:T(8,128)S(1)} %shard_map.90.own_ref), channel_id=1, source_target_pairs={{0,3},{1,2},{2,1},{3,0},{4,7},{5,6},{6,5},{7,4},{8,11},{9,10},{10,... | collective-permute-start | bytes 208904 | tf_op jit(solution)/shard_map/ppermute | solution.py:359
  117.2 6.9 %collective-permute-start.12 = (f32[136,128]{1,0:T(8,128)S(1)}, f32[136,128]{1,0:T(8,128)S(1)}, u32[]{:S(2)}, u32[]{:S(2)}) collective-permute-start(f32[136,128]{1,0:T(8,128)S(1)} %shard_map.90.own_ref), channel_id=1, source_target_pairs={{0,2},{1,3},{2,0},{3,1},{4,6},{5,7},{6,4},{7,5},{8,10},{9,11},{10,... | collective-permute-start | bytes 208904 | tf_op jit(solution)/shard_map/ppermute | solution.py:359
  119.0 5.1 %collective-permute-start.11 = (f32[136,128]{1,0:T(8,128)S(1)}, f32[136,128]{1,0:T(8,128)S(1)}, u32[]{:S(2)}, u32[]{:S(2)}) collective-permute-start(f32[136,128]{1,0:T(8,128)S(1)} %shard_map.90.own_ref), channel_id=1, source_target_pairs={{0,1},{1,0},{2,3},{3,2},{4,5},{5,4},{6,7},{7,6},{8,9},{9,8},{10,11... | collective-permute-start | bytes 208904 | tf_op jit(solution)/shard_map/ppermute | solution.py:359
  124.4 10.1 %collective-permute-start.14 = (f32[264,128]{1,0:T(8,128)S(1)}, f32[264,128]{1,0:T(8,128)S(1)}, u32[]{:S(2)}, u32[]{:S(2)}) collective-permute-start(f32[264,128]{1,0:T(8,128)S(1)} %shard_map.92.near_ref), channel_id=1, source_target_pairs={{0,6},{1,7},{2,4},{3,5},{4,2},{5,3},{6,0},{7,1},{8,14},{9,15},{10,... | collective-permute-start | bytes 405512 | tf_op jit(solution)/shard_map/ppermute | solution.py:359
